TPU v7x, 32 devices: a whole 2x2x4 slice. The times are simulated.
32 devices in a mesh: ctx: 8 (over z, x), head: 4 (over y, core).
Axes of the slice: x: 2, y: 2, z: 4, core: 2. Of those that a mesh axis runs over, the one named last changes fastest.
Arguments:
- hidden: bfloat16 [1024, 8192], P('ctx', 'head'), may hold values from -6 to 6
- frozen_query_rows: bfloat16 [1024, 3072], P('ctx', 'head'), may hold values from -101 to 101
- frozen_key_rows: bfloat16 [1024, 256], P('ctx'), may hold values from -5 to 5
- frozen_value_rows: bfloat16 [1024, 256], P('ctx'), may hold values from -6 to 6
- adapter_down_factors: bfloat16 [8192, 64], P('head'), may hold values from -0.0625 to 0.0625
- query_up_factor: bfloat16 [32, 3072], P(None, 'head'), may hold values from -1 to 1
- value_up_factor: bfloat16 [32, 256], replicated, may hold values from -1 to 1
- slot_span_order: int32 [16], replicated, may hold values from 0 to 15, each once
Outputs:
- attended: bfloat16 [1024, 3072], P('ctx', 'head')
- log_normalizer: float32 [24, 1024], P('head', 'ctx')
Inputs may be any that keep to these rules, and one draw needn't show every extreme that they name: `slot_span_order`: every span number appears once.
All inputs are finite; a program needn't handle non-finite values.
Results may differ from a plain program's by a relative error of at most 0.018.
Values may be sent and summed in bfloat16 or wider, within the bound.
No kernel may reach another device: no remote copies, remote signals or barrier semaphores. Data moves between devices by JAX's collectives and lax.ppermute only.
A program may use at most 64 MiB of HBM per device.

v0:
```python
import math

import jax
import jax.numpy as jnp
from jax import lax
from jax.sharding import PartitionSpec as P

HEAD_SIZE = 128
KEY_VALUE_HEADS = 2
ADAPTER_RANK = 32


adapter_scale = 0.5
start_max = -1e30


def from_partner(value, axis, stride):
    return lax.ppermute(value, axis, [(i, i ^ 1 << stride) for i in range(lax.axis_size(axis))])


def spread_positions(span_ids, span_len):
    return (span_ids[:, None] * span_len + jnp.arange(span_len, dtype=jnp.int32)[None, :]).reshape(
        -1
    )


def stack_heads(matrix, width):
    return matrix.reshape(matrix.shape[0], -1, width).transpose(1, 0, 2).reshape(-1, width)


def empty_state(row_count, width):
    return (
        jnp.full((row_count,), start_max, jnp.float32),
        jnp.zeros((row_count,), jnp.float32),
        jnp.zeros((row_count, width), jnp.float32),
    )


def update_state(carry_state, query_matrix, query_pos, key_block, value_block, key_pos):
    running_max, denominator, numerator = carry_state
    scores = lax.dot_general(
        query_matrix, key_block, (((1,), (1,)), ((), ())), preferred_element_type=jnp.float32
    ) * (1.0 / math.sqrt(key_block.shape[1]))
    visible = key_pos[None, :] <= query_pos[:, None]
    block_max = jnp.max(jnp.where(visible, scores, -jnp.inf), axis=1)
    new_max = jnp.maximum(running_max, block_max)
    rescale = jnp.exp(running_max - new_max)
    weights = jnp.where(visible, jnp.exp(scores - new_max[:, None]), 0.0)
    denominator = denominator * rescale + jnp.sum(weights, axis=1)
    numerator = numerator * rescale[:, None] + jnp.dot(
        weights.astype(jnp.bfloat16), value_block, preferred_element_type=jnp.float32
    )
    return (new_max, denominator, numerator)


def sweep_keys(carry_state, query_matrix, query_pos, key_rows, value_rows, key_pos):
    key_count = key_rows.shape[0]
    block_len = math.gcd(key_count, 1024)

    def one_block(block_index, inner_state):
        offset = block_index * block_len
        key_block = lax.dynamic_slice_in_dim(key_rows, offset, block_len, 0)
        value_block = lax.dynamic_slice_in_dim(value_rows, offset, block_len, 0)
        pos_block = lax.dynamic_slice_in_dim(key_pos, offset, block_len, 0)
        return update_state(inner_state, query_matrix, query_pos, key_block, value_block, pos_block)

    return lax.fori_loop(0, key_count // block_len, one_block, carry_state)


def merge_states(first_state, second_state):
    first_max, first_total, first_sum = first_state
    second_max, second_total, second_sum = second_state
    new_max = jnp.maximum(first_max, second_max)
    first_scale = jnp.exp(first_max - new_max)
    second_scale = jnp.exp(second_max - new_max)
    return (
        new_max,
        first_total * first_scale + second_total * second_scale,
        first_sum * first_scale[:, None] + second_sum * second_scale[:, None],
    )


def local(
    hidden,
    frozen_query_rows,
    frozen_key_rows,
    frozen_value_rows,
    adapter_down_factors,
    query_up_factor,
    value_up_factor,
    slot_span_order,
):
    tok_dev = hidden.shape[0]
    span_len = tok_dev // 2
    partial_bottleneck = jnp.dot(hidden, adapter_down_factors, preferred_element_type=jnp.float32)
    adapter_bottleneck = lax.psum(partial_bottleneck.astype(jnp.bfloat16), "head")
    query_rows = (
        frozen_query_rows.astype(jnp.float32)
        + adapter_scale
        * jnp.dot(
            adapter_bottleneck[:, :ADAPTER_RANK],
            query_up_factor,
            preferred_element_type=jnp.float32,
        )
    ).astype(jnp.bfloat16)
    head_index = lax.axis_index("head")
    key_value_index = head_index // (lax.axis_size("head") // KEY_VALUE_HEADS)
    key_rows = lax.dynamic_slice_in_dim(frozen_key_rows, key_value_index * HEAD_SIZE, HEAD_SIZE, 1)
    value_base = lax.dynamic_slice_in_dim(
        frozen_value_rows, key_value_index * HEAD_SIZE, HEAD_SIZE, 1
    )
    value_up_update = lax.dynamic_slice_in_dim(
        value_up_factor, key_value_index * HEAD_SIZE, HEAD_SIZE, 1
    )
    value_rows = (
        value_base.astype(jnp.float32)
        + adapter_scale
        * jnp.dot(
            adapter_bottleneck[:, ADAPTER_RANK:],
            value_up_update,
            preferred_element_type=jnp.float32,
        )
    ).astype(jnp.bfloat16)
    span_pairs = slot_span_order.reshape(-1, 2)
    own_spans = lax.dynamic_slice_in_dim(span_pairs, lax.axis_index("ctx"), 1, 0).reshape(2)
    own_positions = spread_positions(own_spans, span_len)
    heads_dev = query_rows.shape[1] // HEAD_SIZE
    query_matrix = stack_heads(query_rows, HEAD_SIZE)
    query_pos = jnp.tile(own_positions, heads_dev)
    own_count = query_matrix.shape[0]
    half_side = head_index % 2
    partner = from_partner(query_matrix, "head", 0)
    stacked = jnp.concatenate([query_matrix, partner], axis=0)
    stacked_pos = jnp.concatenate([query_pos, query_pos])
    key_half = lax.dynamic_slice_in_dim(key_rows, half_side * span_len, span_len, 0)
    value_half = lax.dynamic_slice_in_dim(value_rows, half_side * span_len, span_len, 0)
    span_ids = jnp.where(half_side == 0, span_pairs[:, 0], span_pairs[:, 1])
    running_max, denominator, numerator = sweep_keys(
        empty_state(2 * own_count, HEAD_SIZE),
        stacked,
        stacked_pos,
        lax.all_gather(key_half, "ctx", axis=0, tiled=True),
        lax.all_gather(value_half, "ctx", axis=0, tiled=True),
        spread_positions(span_ids, span_len),
    )
    returned = (
        from_partner(running_max[own_count:].astype(jnp.bfloat16), "head", 0).astype(jnp.float32),
        from_partner(denominator[own_count:].astype(jnp.bfloat16), "head", 0).astype(jnp.float32),
        from_partner(numerator[own_count:].astype(jnp.bfloat16), "head", 0).astype(jnp.float32),
    )
    running_max, denominator, numerator = merge_states(
        (running_max[:own_count], denominator[:own_count], numerator[:own_count]), returned
    )
    result = (numerator / denominator[:, None]).astype(jnp.bfloat16)
    attended = (
        result.reshape(heads_dev, tok_dev, HEAD_SIZE)
        .transpose(1, 0, 2)
        .reshape(tok_dev, heads_dev * HEAD_SIZE)
    )
    log_normalizer = (running_max + jnp.log(denominator)).reshape(heads_dev, tok_dev)
    return (attended, log_normalizer)


def solution(mesh):
    placed = (
        P("ctx", "head"),
        P("ctx", "head"),
        P("ctx", None),
        P("ctx", None),
        P("head", None),
        P(None, "head"),
        P(),
        P(),
    )
    return jax.shard_map(
        local,
        mesh=mesh,
        in_specs=placed,
        out_specs=(P("ctx", "head"), P("head", "ctx")),
        check_vma=False,
    )
```

profile of v0, /device:TPU:0, one launch (start us, length us, event | category | flops | bytes accessed | tf_op | source)
XLA Modules:
  0.0 88.2 jit_solution(8973720072184126666)
XLA Ops:
  0.6 0.0 copy-start
  0.6 1.0 %copy-done = bf16[128,2048]{1,0:T(8,128)(2,1)S(1)} copy-done((bf16[128,2048]{1,0:T(8,128)(2,1)S(1)}, bf16[128,2048]{1,0:T(8,128)(2,1)}, u32[]{:S(2)}) %copy-start) | copy-done | bytes 524312
  1.7 1.2 %convolution_convert_fusion = bf16[128,64]{0,1:T(8,128)(2,1)S(1)} fusion(bf16[128,2048]{1,0:T(8,128)(2,1)S(1)} %copy-done, bf16[2048,64]{0,1:T(8,128)(2,1)} %param.12), kind=kOutput, calls=%fused_computation.14 | convolution fusion | flops 33562624 | bytes 802816 | tf_op jit(solution)/shard_map/dot_general | solution.py:95
  2.9 12.7 %psum.7 = bf16[128,64]{0,1:T(8,128)(2,1)S(1)} all-reduce(bf16[128,64]{0,1:T(8,128)(2,1)S(1)} %convolution_convert_fusion), channel_id=1, replica_groups=mesh['ctx'=8,'head'=4] {'head'}, use_global_device_ids=true, to_apply=%region_0.0 | all-reduce | flops 8192 | bytes 32768 | tf_op jit(solution)/shard_map/psum | solution.py:96
  15.6 1.2 %fusion.9 = bf16[128,768]{1,0:T(8,128)(2,1)S(1)} fusion(bf16[32,768]{1,0:T(8,128)(2,1)} %param.13, bf16[128,768]{1,0:T(8,128)(2,1)} %param.9, bf16[128,64]{0,1:T(8,128)(2,1)S(1)} %psum.7), kind=kOutput, calls=%fused_computation.13 | convolution fusion | flops 6684672 | bytes 450560 | tf_op jit(solution)/shard_map/dot_general | solution.py:100
  16.8 0.2 copy.11
  17.0 0.2 copy.12
  17.2 0.1 collective-permute-start
  17.3 0.7 reshape.73
  18.0 0.1 iota_add_fusion.1
  18.1 0.1 add.104
  18.2 0.2 multiply_reduce_fusion
  18.4 0.1 iota_add_fusion
  18.4 0.9 %fusion.18 = f32[128,128]{1,0:T(8,128)S(1)} fusion(bf16[128,64]{0,1:T(8,128)(2,1)S(1)} %psum.7, bf16[32,256]{1,0:T(8,128)(2,1)} %param.14, s32[]{:T(128)S(6)} %select_n.56), kind=kOutput, calls=%fused_computation.26 | convolution fusion | flops 1048576 | bytes 81924 | tf_op jit(solution)/shard_map/dot_general | solution.py:118
  19.3 0.7 fusion.17
  20.1 31.0 %all_gather.7 = bf16[512,128]{1,0:T(8,128)(2,1)S(1)} all-gather(bf16[64,128]{1,0:T(8,128)(2,1)S(1)} %fusion.17), channel_id=1, replica_groups=mesh['ctx'=8,'head'=4] {'ctx'}, dimensions={0}, use_global_device_ids=true | all-gather | bytes 147456 | tf_op jit(solution)/shard_map/all_gather | solution.py:143
  51.0 0.1 add.99
  51.1 0.9 dynamic_slice.23
  51.9 30.5 %all_gather.6 = bf16[512,128]{1,0:T(8,128)(2,1)S(1)} all-gather(bf16[64,128]{1,0:T(8,128)(2,1)S(1)} %dynamic_slice.23), channel_id=1, replica_groups=mesh['ctx'=8,'head'=4] {'ctx'}, dimensions={0}, use_global_device_ids=true | all-gather | bytes 147456 | tf_op jit(solution)/shard_map/all_gather | solution.py:142
  82.5 0.0 collective-permute-done
  82.5 0.6 fusion
  83.1 0.6 fusion.1
  83.8 0.1 collective-permute-start.1
  83.9 0.5 collective-permute-start.3
  84.3 0.9 %convolution_add_fusion = f32[1536,128]{1,0:T(8,128)S(1)} fusion(bf16[512,128]{1,0:T(8,128)(2,1)S(1)} %all_gather.7, f32[1536,512]{0,1:T(8,128)S(1)} %get-tuple-element.41, f32[1536]{0:T(1024)S(1)} %broadcast_maximum_fusion, s32[1536]{0:T(1024)S(1)} %pad_add_fusion, s32[512]{0:T(512)S(1)} %add.99, f32[1536]{0:T(1024)S(1)} %get-tuple-element.29), kind=kOutput, calls=%fused_computation.4 | convolution fusion | flops 204668928 | bytes 4083712 | tf_op jit(solution)/shard_map/while/body/eval_jaxpr/dot_general | solution.py:50
  85.3 0.1 collective-permute-start.2
  85.5 0.0 collective-permute-done.1
  85.5 0.0 collective-permute-done.3
  85.5 0.6 fusion.25
  86.1 0.7 collective-permute-done.2
  86.8 0.4 fusion.15
  87.2 0.2 copy.13
  87.4 0.8 copy.14
  (8 shorter events, 0.1 us)
Async XLA Ops:
  0.6 1.0 %copy-start = (bf16[128,2048]{1,0:T(8,128)(2,1)S(1)}, bf16[128,2048]{1,0:T(8,128)(2,1)}, u32[]{:S(2)}) copy-start(bf16[128,2048]{1,0:T(8,128)(2,1)} %param.8) | copy-start | bytes 1572868
  17.2 65.3 %collective-permute-start = (bf16[768,128]{1,0:T(8,128)(2,1)S(1)}, bf16[768,128]{1,0:T(8,128)(2,1)S(1)}, u32[]{:S(2)}, u32[]{:S(2)}) collective-permute-start(bf16[768,128]{1,0:T(8,128)(2,1)S(1)} %bitcast.22), channel_id=1, source_target_pairs={{0,1},{1,0},{2,3},{3,2},{4,5},{5,4},{6,7},{7,6},{8,9},{9,8},{10,11... | collective-permute-start | bytes 589832 | tf_op jit(solution)/shard_map/ppermute | solution.py:18
  83.8 1.7 %collective-permute-start.1 = (bf16[768]{0:T(1024)(128)(2,1)S(1)}, bf16[768]{0:T(1024)(128)(2,1)S(1)}, u32[]{:S(2)}, u32[]{:S(2)}) collective-permute-start(bf16[768]{0:T(1024)(128)(2,1)S(1)} %slice.75), channel_id=1, source_target_pairs={{0,1},{1,0},{2,3},{3,2},{4,5},{5,4},{6,7},{7,6},{8,9},{9,8},{10,11... | collective-permute-start | bytes 4616 | tf_op jit(solution)/shard_map/ppermute | solution.py:18
  83.9 1.6 %collective-permute-start.3 = (bf16[768]{0:T(1024)(128)(2,1)S(1)}, bf16[768]{0:T(1024)(128)(2,1)S(1)}, u32[]{:S(2)}, u32[]{:S(2)}) collective-permute-start(bf16[768]{0:T(1024)(128)(2,1)S(1)} %slice.74), channel_id=1, source_target_pairs={{0,1},{1,0},{2,3},{3,2},{4,5},{5,4},{6,7},{7,6},{8,9},{9,8},{10,11... | collective-permute-start | bytes 4616 | tf_op jit(solution)/shard_map/ppermute | solution.py:18
  85.3 1.5 %collective-permute-start.2 = (bf16[768,128]{1,0:T(8,128)(2,1)S(1)}, bf16[768,128]{1,0:T(8,128)(2,1)S(1)}, u32[]{:S(2)}, u32[]{:S(2)}) collective-permute-start(bf16[768,128]{1,0:T(8,128)(2,1)S(1)} %slice.73), channel_id=1, source_target_pairs={{0,1},{1,0},{2,3},{3,2},{4,5},{5,4},{6,7},{7,6},{8,9},{9,8},{10,11... | collective-permute-start | bytes 589832 | tf_op jit(solution)/shard_map/ppermute | solution.py:18
where the time goes:
time: 88.6 us; the launch traced here: 88.2 us
  blocking collectives  74.2 us (84%)
  matrix products  4.86 us (5%)
  local copies, waits for them, and re-layouts  4.16 us (5%)
  other arithmetic  2.73 us (3%)
    all_gather x1, blocking collectives, local(): lax.all_gather(value_half, 'ctx', axis=0, tiled=True)  31 us
    all_gather x1, blocking collectives, local(): lax.all_gather(key_half, 'ctx', axis=0, tiled=True)  30.5 us
    psum x1, blocking collectives, local(): lax.psum(partial_bottleneck.astype(jnp.bfloat16), 'head')  12.7 us
    unnamed x3, local copies, waits for them, and re-layouts  1.87 us
  transfers between devices with their start and end apart: 4, of which 1 were waited for; matrix products, arithmetic and copies ran while one was open for 6% of the time, Pallas kernels for 0%

commit v1 on v0

v1 whole, which is shorter than its diff:
```python
import functools
import math

import jax
import jax.numpy as jnp
from jax import lax
from jax.experimental import pallas as pl
from jax.experimental.pallas import tpu as pltpu
from jax.sharding import PartitionSpec as P

HEAD_SIZE = 128
KEY_VALUE_HEADS = 2
ADAPTER_RANK = 32
ADAPTER_SCALE = 0.5
MASKED = -1e30
AXES = ("ctx", "head")


def exchange(value, ctx_bit, head_bits):
    ctx_count, head_count = lax.axis_size("ctx"), lax.axis_size("head")
    pairs = [
        (i * head_count + h, (i ^ ctx_bit) * head_count + (h ^ head_bits))
        for i in range(ctx_count)
        for h in range(head_count)
    ]
    return lax.ppermute(value, AXES, pairs)


def gather_patterns(bits):
    patterns = [0]
    for bit in bits:
        patterns += [p ^ bit for p in patterns]
    return patterns


def attention_kernel(
    patterns,
    place_ref,
    order_ref,
    frozen_query_ref,
    low_ref,
    query_up_ref,
    kv_ref,
    low_value_ref,
    value_up_ref,
    attended_ref,
    normalizer_ref,
    bias_ref,
    value_ref,
):
    tok_dev, width = frozen_query_ref.shape
    span = tok_dev // 2
    heads = width // HEAD_SIZE
    ctx, side = place_ref[0], place_ref[1]
    blocks = len(patterns)
    key_count = kv_ref.shape[0]

    queries = (
        frozen_query_ref[...].astype(jnp.float32)
        + ADAPTER_SCALE
        * jnp.dot(
            low_ref[:, :ADAPTER_RANK], query_up_ref[...], preferred_element_type=jnp.float32
        )
    ).astype(jnp.bfloat16)

    row = lax.broadcasted_iota(jnp.int32, (tok_dev, HEAD_SIZE), 0)
    lane = lax.broadcasted_iota(jnp.int32, (tok_dev, HEAD_SIZE), 1)
    query_pos = (
        jnp.where(row < span, order_ref[2 * ctx], order_ref[2 * ctx + 1]) * span + row % span
    )
    halves = []
    for entry in range(2 * blocks):
        pattern = patterns[entry % blocks]
        half = (side + pattern.bit_count() + entry // blocks) % 2
        halves.append((entry % blocks, half, order_ref[2 * (ctx ^ pattern) + half]))
    for tile in range(blocks):
        first, second = halves[2 * tile], halves[2 * tile + 1]
        key_pos = jnp.where(lane < span, first[2], second[2]) * span + lane % span
        bias_ref[:, tile * HEAD_SIZE : (tile + 1) * HEAD_SIZE] = jnp.where(
            key_pos <= query_pos, 0.0, MASKED
        )
    for entry in range(2 * blocks):
        index, half, _ = halves[entry]
        rows = pl.ds(pl.multiple_of(index * tok_dev + half * span, span), span)
        here = slice(entry * span, (entry + 1) * span)
        value_ref[here, :HEAD_SIZE] = (
            kv_ref[here, HEAD_SIZE:].astype(jnp.float32)
            + ADAPTER_SCALE
            * jnp.dot(
                low_value_ref[rows, :], value_up_ref[...], preferred_element_type=jnp.float32
            )
        ).astype(jnp.bfloat16)
    value_ref[:, HEAD_SIZE:] = jnp.ones((key_count, HEAD_SIZE), jnp.bfloat16)

    keys = kv_ref[:, :HEAD_SIZE]
    diagonal = row == lane
    factor = 1.0 / math.sqrt(HEAD_SIZE)
    for head in range(heads):
        columns = slice(head * HEAD_SIZE, (head + 1) * HEAD_SIZE)
        scores = (
            lax.dot_general(
                queries[:, columns], keys, (((1,), (1,)), ((), ())), preferred_element_type=jnp.float32
            )
            * factor
            + bias_ref[...]
        )
        row_max = jnp.max(scores, axis=1, keepdims=True)
        weights = jnp.exp(scores - row_max).astype(jnp.bfloat16)
        sums = jnp.dot(weights, value_ref[...], preferred_element_type=jnp.float32)
        total = sums[:, HEAD_SIZE:]
        attended_ref[:, columns] = (sums[:, :HEAD_SIZE] / total).astype(jnp.bfloat16)
        normal = row_max + jnp.log(total)
        normalizer_ref[head : head + 1, :] = jnp.sum(
            jnp.where(diagonal, normal, 0.0), axis=0, keepdims=True
        )


def attend(patterns, place, order, frozen_query, low, query_up, kv, low_value, value_up):
    tok_dev, width = frozen_query.shape
    heads = width // HEAD_SIZE
    key_count = kv.shape[0]
    smem = pl.BlockSpec(memory_space=pltpu.SMEM)
    vmem = pl.BlockSpec(memory_space=pltpu.VMEM)
    return pl.pallas_call(
        functools.partial(attention_kernel, patterns),
        out_shape=(
            jax.ShapeDtypeStruct((tok_dev, width), jnp.bfloat16),
            jax.ShapeDtypeStruct((heads, tok_dev), jnp.float32),
        ),
        in_specs=[smem, smem] + [vmem] * 6,
        out_specs=(vmem, vmem),
        scratch_shapes=[
            pltpu.VMEM((tok_dev, key_count), jnp.float32),
            pltpu.VMEM((key_count, 2 * HEAD_SIZE), jnp.bfloat16),
        ],
        compiler_params=pltpu.CompilerParams(vmem_limit_bytes=32 * 1024 * 1024),
        cost_estimate=pl.CostEstimate(
            flops=4 * tok_dev * width * key_count,
            bytes_accessed=2 * (tok_dev * width * 2 + key_count * 2 * HEAD_SIZE),
            transcendentals=heads * tok_dev * key_count,
        ),
    )(place, order, frozen_query, low, query_up, kv, low_value, value_up)


def attend_long(patterns, place, order, frozen_query, low, query_up, kv, low_value, value_up):
    tok_dev, width = frozen_query.shape
    span = tok_dev // 2
    heads = width // HEAD_SIZE
    blocks = len(patterns)
    ctx, side = place[0], place[1]
    queries = (
        frozen_query.astype(jnp.float32)
        + ADAPTER_SCALE
        * jnp.dot(low[:, :ADAPTER_RANK], query_up, preferred_element_type=jnp.float32)
    ).astype(jnp.bfloat16)
    queries = queries.reshape(tok_dev, heads, HEAD_SIZE).transpose(1, 0, 2).reshape(-1, HEAD_SIZE)
    pattern = jnp.tile(jnp.array(patterns, jnp.int32), 2)
    parity = jnp.array([p.bit_count() for p in patterns] + [p.bit_count() + 1 for p in patterns])
    half = (side + parity.astype(jnp.int32)) % 2
    key_spans = order[2 * (ctx ^ pattern) + half]
    inner = jnp.arange(span, dtype=jnp.int32)
    key_pos = (key_spans[:, None] * span + inner).reshape(-1)
    query_spans = lax.dynamic_slice_in_dim(order, 2 * ctx, 2)
    query_pos = jnp.tile((query_spans[:, None] * span + inner).reshape(-1), heads)
    index = jnp.tile(jnp.arange(blocks, dtype=jnp.int32), 2)
    low_rows = low_value.reshape(2 * blocks, span, ADAPTER_RANK)[2 * index + half]
    values = (
        kv[:, HEAD_SIZE:].astype(jnp.float32)
        + ADAPTER_SCALE
        * jnp.dot(
            low_rows.reshape(-1, ADAPTER_RANK), value_up, preferred_element_type=jnp.float32
        )
    ).astype(jnp.bfloat16)
    chunk = math.gcd(kv.shape[0], 1024)

    def step(number, state):
        top, total, summed = state
        at = number * chunk
        keys = lax.dynamic_slice_in_dim(kv, at, chunk, 0)[:, :HEAD_SIZE]
        scores = lax.dot_general(
            queries, keys, (((1,), (1,)), ((), ())), preferred_element_type=jnp.float32
        ) * (1.0 / math.sqrt(HEAD_SIZE))
        visible = lax.dynamic_slice_in_dim(key_pos, at, chunk)[None, :] <= query_pos[:, None]
        new_top = jnp.maximum(top, jnp.max(jnp.where(visible, scores, MASKED), axis=1))
        scale = jnp.exp(top - new_top)
        weights = jnp.where(visible, jnp.exp(scores - new_top[:, None]), 0.0)
        summed = summed * scale[:, None] + jnp.dot(
            weights.astype(jnp.bfloat16),
            lax.dynamic_slice_in_dim(values, at, chunk, 0),
            preferred_element_type=jnp.float32,
        )
        return (new_top, total * scale + jnp.sum(weights, axis=1), summed)

    rows = heads * tok_dev
    top, total, summed = lax.fori_loop(
        0,
        kv.shape[0] // chunk,
        step,
        (
            jnp.full((rows,), MASKED, jnp.float32),
            jnp.zeros((rows,), jnp.float32),
            jnp.zeros((rows, HEAD_SIZE), jnp.float32),
        ),
    )
    attended = (summed / total[:, None]).astype(jnp.bfloat16)
    attended = attended.reshape(heads, tok_dev, HEAD_SIZE).transpose(1, 0, 2)
    return attended.reshape(tok_dev, width), (top + jnp.log(total)).reshape(heads, tok_dev)


def local(
    hidden,
    frozen_query_rows,
    frozen_key_rows,
    frozen_value_rows,
    adapter_down_factors,
    query_up_factor,
    value_up_factor,
    slot_span_order,
):
    ctx_count, head_count = lax.axis_size("ctx"), lax.axis_size("head")
    ctx, head = lax.axis_index("ctx"), lax.axis_index("head")
    side = head % 2
    group = head // (head_count // KEY_VALUE_HEADS)
    bits = [ctx_count >> k for k in range(1, ctx_count.bit_length())]
    if len(bits) == 3:
        bits = [bits[0], bits[2], bits[1]]
    patterns = gather_patterns(bits)
    half = hidden.shape[0] // 2

    partial = jnp.dot(hidden, adapter_down_factors, preferred_element_type=jnp.float32)
    low = partial.astype(jnp.bfloat16)
    head_bit = 1
    while head_bit < head_count:
        other = exchange(low, 0, head_bit | 1)
        low = (low.astype(jnp.float32) + other.astype(jnp.float32)).astype(jnp.bfloat16)
        head_bit *= 2

    def own_half(rows):
        return lax.dynamic_slice(
            rows, (side * half, group * HEAD_SIZE), (half, HEAD_SIZE)
        )

    kv = jnp.concatenate([own_half(frozen_key_rows), own_half(frozen_value_rows)], axis=1)
    low_value = low[:, ADAPTER_RANK:]
    for bit in bits:
        low_value = jnp.concatenate([low_value, exchange(low_value, bit, 1)], axis=0)
        kv = jnp.concatenate([kv, exchange(kv, bit, 1)], axis=0)
    kv = jnp.concatenate([kv, exchange(kv, 0, 1)], axis=0)
    value_up = lax.dynamic_slice_in_dim(value_up_factor, group * HEAD_SIZE, HEAD_SIZE, 1)
    place = jnp.stack([ctx, side]).astype(jnp.int32)
    run = attend if kv.shape[0] <= 1024 else attend_long
    return run(
        patterns, place, slot_span_order, frozen_query_rows, low, query_up_factor, kv, low_value, value_up
    )


def solution(mesh):
    placed = (
        P("ctx", "head"),
        P("ctx", "head"),
        P("ctx", None),
        P("ctx", None),
        P("head", None),
        P(None, "head"),
        P(),
        P(),
    )
    return jax.shard_map(
        local,
        mesh=mesh,
        in_specs=placed,
        out_specs=(P("ctx", "head"), P("head", "ctx")),
        check_vma=False,
    )
```

time: 88.6 us -> 30.4 us (0.34)
  blocking collectives: 74.2 us -> 0 us
  starting transfers between devices: 0.78 us -> 12.2 us
  waiting for transfers between devices: 0.74 us -> 9.21 us
  matrix products: 4.86 us -> 1.24 us
  Pallas kernels: 0 us -> 2.89 us
  other arithmetic: 2.73 us -> 0.25 us
    all_gather x2 -> x0, blocking collectives: 61.5 us -> none  [the longest x1 31 us: local(): lax.all_gather(value_half, 'ctx', axis=0, tiled=True)]
    psum x1 -> x0, blocking collectives: 12.7 us -> none  [local(): lax.psum(partial_bottleneck.astype(jnp.bfloat16), 'head')]
    ppermute x4 -> x9, starting transfers between devices: 0.78 us -> 12.2 us  [exchange(): return lax.ppermute(value, AXES, pairs)]
    ppermute x4 -> x9, waiting for transfers between devices: 0.74 us -> 9.21 us  [exchange(): return lax.ppermute(value, AXES, pairs)]
    dot_general x4 -> x0, matrix products: 3.61 us -> none  [the longest x1 1.19 us: local(): jnp.dot(adapter_bottleneck[:, :ADAPTER_RANK], query_up_factor, preferred_...]
    pallas_call x0 -> x1, Pallas kernels: none -> 2.89 us  [attend(): pl.pallas_call(functools.partial(attention_kernel, patterns), out_shape=(...]
    convert_element_type x2, other arithmetic: 1.11 us -> 0.03 us  [local(): (low.astype(jnp.float32) + other.astype(jnp.float32)).astype(jnp.bfloat16)]
    reshape x2 -> x0, local copies, waits for them, and re-layouts: 0.91 us -> none  [the longest x1 0.73 us: local(): span_pairs = slot_span_order.reshape(-1, 2)]
  transfers between devices with their start and end apart: 4 -> 9, of which waited for: 1 -> 5; matrix products, arithmetic and copies ran while one was open for 6% -> 6% of each run, Pallas kernels for 0% -> 0%
where the time goes in v1:
time: 30.4 us; the launch traced here: 30 us
  starting transfers between devices  12.2 us (40%)
  waiting for transfers between devices  9.21 us (30%)
  local copies, waits for them, and re-layouts  3.47 us (11%)
  Pallas kernels  2.89 us (10%)
  matrix products  1.24 us (4%)
  between operations  0.75 us (2%)
    ppermute x9, starting transfers between devices, exchange(): return lax.ppermute(value, AXES, pairs)  12.2 us
    ppermute x9, waiting for transfers between devices, exchange(): return lax.ppermute(value, AXES, pairs)  9.21 us
    pallas_call x1, Pallas kernels, attend(): pl.pallas_call(functools.partial(attention_kernel, patterns), out_shape=(...  2.89 us
    unnamed x13, local copies, waits for them, and re-layouts  1.94 us
    dynamic_slice x2, local copies, waits for them, and re-layouts, own_half(): lax.dynamic_slice(rows, (side * half, group * HEAD_SIZE), (half, HEAD_SIZE))  1.44 us
    dot_general x1, matrix products, local(): jnp.dot(hidden, adapter_down_factors, preferred_element_type=jnp.float32)  1.24 us
  transfers between devices with their start and end apart: 9, of which 5 were waited for; matrix products, arithmetic and copies ran while one was open for 6% of the time, Pallas kernels for 0%

profile of v1, /device:TPU:0, one launch (start us, length us, event | category | flops | bytes accessed | tf_op | source)
XLA Modules:
  0.0 30.0 jit_solution(5088826600095200577)
XLA Ops:
  0.6 0.0 copy-start
  0.6 1.0 %copy-done = bf16[128,2048]{1,0:T(8,128)(2,1)S(1)} copy-done((bf16[128,2048]{1,0:T(8,128)(2,1)S(1)}, bf16[128,2048]{1,0:T(8,128)(2,1)}, u32[]{:S(2)}) %copy-start) | copy-done | bytes 524312
  1.7 1.2 %convolution_convert_fusion = bf16[128,64]{1,0:T(8,128)(2,1)S(1)} fusion(bf16[128,2048]{1,0:T(8,128)(2,1)S(1)} %copy-done, bf16[2048,64]{0,1:T(8,128)(2,1)} %param.12), kind=kOutput, calls=%fused_computation | convolution fusion | flops 33562624 | bytes 802816 | tf_op jit(solution)/shard_map/dot_general | solution.py:230
  2.9 0.5 %collective-permute-start = (bf16[128,64]{1,0:T(8,128)(2,1)S(1)}, bf16[128,64]{1,0:T(8,128)(2,1)S(1)}, u32[]{:S(2)}, u32[]{:S(2)}) collective-permute-start(bf16[128,64]{1,0:T(8,128)(2,1)S(1)} %convolution_convert_fusion), channel_id=1, source_target_pairs={{0,1},{1,0},{2,3},{3,2},{4,5},{5,4},{6,7},{7,6},{8,9},{9,8},{10,11... | collective-permute-start | bytes 49160 | tf_op jit(solution)/shard_map/ppermute | solution.py:26
  3.4 0.7 %dynamic_slice.10 = bf16[64,128]{1,0:T(8,128)(2,1)S(1)} dynamic-slice(bf16[128,256]{1,0:T(8,128)(2,1)} %param.11, s32[]{:T(128)S(6)} %select_n.21, s32[]{:T(128)S(6)} %select_n.23), dynamic_slice_sizes={64,128} | dynamic-slice | bytes 32772 | tf_op jit(solution)/shard_map/dynamic_slice | solution.py:239
  4.2 0.7 %dynamic_slice.9 = bf16[64,128]{1,0:T(8,128)(2,1)S(1)} dynamic-slice(bf16[128,256]{1,0:T(8,128)(2,1)} %param.10, s32[]{:T(128)S(6)} %select_n.21, s32[]{:T(128)S(6)} %select_n.23), dynamic_slice_sizes={64,128} | dynamic-slice | bytes 32772 | tf_op jit(solution)/shard_map/dynamic_slice | solution.py:239
  4.9 0.0 copy-start.4
  4.9 3.8 %collective-permute-start.2 = (bf16[64,256]{1,0:T(8,128)(2,1)S(1)}, bf16[64,256]{1,0:T(8,128)(2,1)S(1)}, u32[]{:S(2)}, u32[]{:S(2)}) collective-permute-start(bf16[64,256]{1,0:T(8,128)(2,1)S(1)} %get-tuple-element.2), channel_id=1, source_target_pairs={{0,17},{1,16},{2,19},{3,18},{4,21},{5,20},{6,23},{7,22},{8,25},{9,... | collective-permute-start | bytes 98312 | tf_op jit(solution)/shard_map/ppermute | solution.py:26
  8.6 0.0 copy-done.4
  8.7 0.0 collective-permute-done
  8.7 1.2 %collective-permute-start.1 = (bf16[128,64]{1,0:T(8,128)(2,1)S(1)}, bf16[128,64]{1,0:T(8,128)(2,1)S(1)}, u32[]{:S(2)}, u32[]{:S(2)}) collective-permute-start(bf16[128,64]{1,0:T(8,128)(2,1)S(1)} %add_convert_fusion.1), channel_id=1, source_target_pairs={{0,3},{1,2},{2,1},{3,0},{4,7},{5,6},{6,5},{7,4},{8,11},{9,10},{10,... | collective-permute-start | bytes 49160 | tf_op jit(solution)/shard_map/ppermute | solution.py:26
  9.9 0.1 pad_add_fusion.place_ref
  10.0 2.2 %collective-permute-done.1 = bf16[128,64]{1,0:T(8,128)(2,1)S(1)} collective-permute-done((bf16[128,64]{1,0:T(8,128)(2,1)S(1)}, bf16[128,64]{1,0:T(8,128)(2,1)S(1)}, u32[]{:S(2)}, u32[]{:S(2)}) %collective-permute-start.1) | collective-permute-done | bytes 16416 | tf_op jit(solution)/shard_map/ppermute | solution.py:26
  12.2 0.1 slice.4
  12.3 0.5 %collective-permute-start.6 = (bf16[128,32]{1,0:T(8,128)(2,1)S(1)}, bf16[128,32]{1,0:T(8,128)(2,1)S(1)}, u32[]{:S(2)}, u32[]{:S(2)}) collective-permute-start(bf16[128,32]{1,0:T(8,128)(2,1)S(1)} %slice.4), channel_id=1, source_target_pairs={{0,17},{1,16},{2,19},{3,18},{4,21},{5,20},{6,23},{7,22},{8,25},{9,... | collective-permute-start | bytes 24584 | tf_op jit(solution)/shard_map/ppermute | solution.py:26
  12.8 0.0 collective-permute-done.2
  12.8 1.2 %collective-permute-start.3 = (bf16[128,256]{1,0:T(8,128)(2,1)S(1)}, bf16[128,256]{1,0:T(8,128)(2,1)S(1)}, u32[]{:S(2)}, u32[]{:S(2)}) collective-permute-start(bf16[128,256]{1,0:T(8,128)(2,1)S(1)} %pad_maximum_fusion.4), channel_id=1, source_target_pairs={{0,5},{1,4},{2,7},{3,6},{4,1},{5,0},{6,3},{7,2},{8,13},{9,12},{10,... | collective-permute-start | bytes 196616 | tf_op jit(solution)/shard_map/ppermute | solution.py:26
  14.1 2.5 %collective-permute-done.6 = bf16[128,32]{1,0:T(8,128)(2,1)S(1)} collective-permute-done((bf16[128,32]{1,0:T(8,128)(2,1)S(1)}, bf16[128,32]{1,0:T(8,128)(2,1)S(1)}, u32[]{:S(2)}, u32[]{:S(2)}) %collective-permute-start.6) | collective-permute-done | bytes 8224 | tf_op jit(solution)/shard_map/ppermute | solution.py:26
  16.6 1.3 %collective-permute-start.7 = (bf16[256,32]{1,0:T(8,128)(2,1)S(1)}, bf16[256,32]{1,0:T(8,128)(2,1)S(1)}, u32[]{:S(2)}, u32[]{:S(2)}) collective-permute-start(bf16[256,32]{1,0:T(8,128)(2,1)S(1)} %pad_maximum_fusion.5), channel_id=1, source_target_pairs={{0,5},{1,4},{2,7},{3,6},{4,1},{5,0},{6,3},{7,2},{8,13},{9,12},{10,... | collective-permute-start | bytes 49160 | tf_op jit(solution)/shard_map/ppermute | solution.py:26
  17.9 0.0 collective-permute-done.3
  17.9 1.6 %collective-permute-start.4 = (bf16[256,256]{1,0:T(8,128)(2,1)S(1)}, bf16[256,256]{1,0:T(8,128)(2,1)S(1)}, u32[]{:S(2)}, u32[]{:S(2)}) collective-permute-start(bf16[256,256]{1,0:T(8,128)(2,1)S(1)} %pad_maximum_fusion.2), channel_id=1, source_target_pairs={{0,9},{1,8},{2,11},{3,10},{4,13},{5,12},{6,15},{7,14},{8,1},{9,0},... | collective-permute-start | bytes 393224 | tf_op jit(solution)/shard_map/ppermute | solution.py:26
  19.6 1.2 %collective-permute-done.7 = bf16[256,32]{1,0:T(8,128)(2,1)S(1)} collective-permute-done((bf16[256,32]{1,0:T(8,128)(2,1)S(1)}, bf16[256,32]{1,0:T(8,128)(2,1)S(1)}, u32[]{:S(2)}, u32[]{:S(2)}) %collective-permute-start.7) | collective-permute-done | bytes 16416 | tf_op jit(solution)/shard_map/ppermute | solution.py:26
  20.8 1.7 %collective-permute-start.8 = (bf16[512,32]{1,0:T(8,128)(2,1)S(1)}, bf16[512,32]{1,0:T(8,128)(2,1)S(1)}, u32[]{:S(2)}, u32[]{:S(2)}) collective-permute-start(bf16[512,32]{1,0:T(8,128)(2,1)S(1)} %pad_maximum_fusion.3), channel_id=1, source_target_pairs={{0,9},{1,8},{2,11},{3,10},{4,13},{5,12},{6,15},{7,14},{8,1},{9,0},... | collective-permute-start | bytes 98312 | tf_op jit(solution)/shard_map/ppermute | solution.py:26
  22.5 0.8 %collective-permute-done.4 = bf16[256,256]{1,0:T(8,128)(2,1)S(1)} collective-permute-done((bf16[256,256]{1,0:T(8,128)(2,1)S(1)}, bf16[256,256]{1,0:T(8,128)(2,1)S(1)}, u32[]{:S(2)}, u32[]{:S(2)}) %collective-permute-start.4) | collective-permute-done | bytes 131104 | tf_op jit(solution)/shard_map/ppermute | solution.py:26
  23.4 0.4 %collective-permute-start.5 = (bf16[512,256]{1,0:T(8,128)(2,1)S(1)}, bf16[512,256]{1,0:T(8,128)(2,1)S(1)}, u32[]{:S(2)}, u32[]{:S(2)}) collective-permute-start(bf16[512,256]{1,0:T(8,128)(2,1)S(1)} %pad_maximum_fusion), channel_id=1, source_target_pairs={{0,1},{1,0},{2,3},{3,2},{4,5},{5,4},{6,7},{7,6},{8,9},{9,8},{10,11... | collective-permute-start | bytes 786440 | tf_op jit(solution)/shard_map/ppermute | solution.py:26
  23.7 2.4 %collective-permute-done.8 = bf16[512,32]{1,0:T(8,128)(2,1)S(1)} collective-permute-done((bf16[512,32]{1,0:T(8,128)(2,1)S(1)}, bf16[512,32]{1,0:T(8,128)(2,1)S(1)}, u32[]{:S(2)}, u32[]{:S(2)}) %collective-permute-start.8) | collective-permute-done | bytes 32800 | tf_op jit(solution)/shard_map/ppermute | solution.py:26
  26.1 0.1 pad_maximum_fusion.1.low_value_ref
  26.2 0.0 copy-start.1
  26.2 0.0 copy-start.2
  26.2 0.0 copy-start.3
  26.2 0.0 collective-permute-done.5
  26.3 0.9 %copy-done.1 = bf16[128,768]{1,0:T(8,128)(2,1)S(1)} copy-done((bf16[128,768]{1,0:T(8,128)(2,1)S(1)}, bf16[128,768]{1,0:T(8,128)(2,1)}, u32[]{:S(2)}) %copy-start.1) | copy-done | bytes 196632
  27.1 0.0 copy-done.2
  27.1 0.0 copy-done.3
  27.1 2.9 %shard_map.95 = (bf16[128,768]{1,0:T(8,128)(2,1)}, f32[6,128]{1,0:T(8,128)}) custom-call(s32[2]{0:T(128)S(1)} %pad_add_fusion.place_ref, s32[16]{0:T(128)S(1)} %copy-done.3, bf16[128,768]{1,0:T(8,128)(2,1)S(1)} %copy-done.1, bf16[128,64]{1,0:T(8,128)(2,1)S(1)} %add_convert_fusion.low_ref, bf16[32,768]{1,0:T(8,128)(2,1)S(1)} %copy-done.2, ...), custom_call_target="tpu_custom_call" | custom-call | flops 402653184 | bytes 917504 | tf_op jit(solution)/shard_map/pallas_call | solution.py:124
  (13 shorter events, 0.2 us)
Async XLA Ops:
  0.6 1.0 %copy-start = (bf16[128,2048]{1,0:T(8,128)(2,1)S(1)}, bf16[128,2048]{1,0:T(8,128)(2,1)}, u32[]{:S(2)}) copy-start(bf16[128,2048]{1,0:T(8,128)(2,1)} %param.8) | copy-start | bytes 1572868
  2.9 5.7 %collective-permute-start = (bf16[128,64]{1,0:T(8,128)(2,1)S(1)}, bf16[128,64]{1,0:T(8,128)(2,1)S(1)}, u32[]{:S(2)}, u32[]{:S(2)}) collective-permute-start(bf16[128,64]{1,0:T(8,128)(2,1)S(1)} %convolution_convert_fusion), channel_id=1, source_target_pairs={{0,1},{1,0},{2,3},{3,2},{4,5},{5,4},{6,7},{7,6},{8,9},{9,8},{10,11... | collective-permute-start | bytes 49160 | tf_op jit(solution)/shard_map/ppermute | solution.py:26
  4.9 3.8 %copy-start.4 = (bf16[32,256]{1,0:T(8,128)(2,1)S(1)}, bf16[32,256]{1,0:T(8,128)(2,1)}, u32[]{:S(2)}) copy-start(bf16[32,256]{1,0:T(8,128)(2,1)} %param.14) | copy-start | bytes 49156
  4.9 7.9 %collective-permute-start.2 = (bf16[64,256]{1,0:T(8,128)(2,1)S(1)}, bf16[64,256]{1,0:T(8,128)(2,1)S(1)}, u32[]{:S(2)}, u32[]{:S(2)}) collective-permute-start(bf16[64,256]{1,0:T(8,128)(2,1)S(1)} %get-tuple-element.2), channel_id=1, source_target_pairs={{0,17},{1,16},{2,19},{3,18},{4,21},{5,20},{6,23},{7,22},{8,25},{9,... | collective-permute-start | bytes 98312 | tf_op jit(solution)/shard_map/ppermute | solution.py:26
  8.7 3.5 %collective-permute-start.1 = (bf16[128,64]{1,0:T(8,128)(2,1)S(1)}, bf16[128,64]{1,0:T(8,128)(2,1)S(1)}, u32[]{:S(2)}, u32[]{:S(2)}) collective-permute-start(bf16[128,64]{1,0:T(8,128)(2,1)S(1)} %add_convert_fusion.1), channel_id=1, source_target_pairs={{0,3},{1,2},{2,1},{3,0},{4,7},{5,6},{6,5},{7,4},{8,11},{9,10},{10,... | collective-permute-start | bytes 49160 | tf_op jit(solution)/shard_map/ppermute | solution.py:26
  12.3 4.3 %collective-permute-start.6 = (bf16[128,32]{1,0:T(8,128)(2,1)S(1)}, bf16[128,32]{1,0:T(8,128)(2,1)S(1)}, u32[]{:S(2)}, u32[]{:S(2)}) collective-permute-start(bf16[128,32]{1,0:T(8,128)(2,1)S(1)} %slice.4), channel_id=1, source_target_pairs={{0,17},{1,16},{2,19},{3,18},{4,21},{5,20},{6,23},{7,22},{8,25},{9,... | collective-permute-start | bytes 24584 | tf_op jit(solution)/shard_map/ppermute | solution.py:26
  12.8 5.1 %collective-permute-start.3 = (bf16[128,256]{1,0:T(8,128)(2,1)S(1)}, bf16[128,256]{1,0:T(8,128)(2,1)S(1)}, u32[]{:S(2)}, u32[]{:S(2)}) collective-permute-start(bf16[128,256]{1,0:T(8,128)(2,1)S(1)} %pad_maximum_fusion.4), channel_id=1, source_target_pairs={{0,5},{1,4},{2,7},{3,6},{4,1},{5,0},{6,3},{7,2},{8,13},{9,12},{10,... | collective-permute-start | bytes 196616 | tf_op jit(solution)/shard_map/ppermute | solution.py:26
  16.6 4.2 %collective-permute-start.7 = (bf16[256,32]{1,0:T(8,128)(2,1)S(1)}, bf16[256,32]{1,0:T(8,128)(2,1)S(1)}, u32[]{:S(2)}, u32[]{:S(2)}) collective-permute-start(bf16[256,32]{1,0:T(8,128)(2,1)S(1)} %pad_maximum_fusion.5), channel_id=1, source_target_pairs={{0,5},{1,4},{2,7},{3,6},{4,1},{5,0},{6,3},{7,2},{8,13},{9,12},{10,... | collective-permute-start | bytes 49160 | tf_op jit(solution)/shard_map/ppermute | solution.py:26
  17.9 5.4 %collective-permute-start.4 = (bf16[256,256]{1,0:T(8,128)(2,1)S(1)}, bf16[256,256]{1,0:T(8,128)(2,1)S(1)}, u32[]{:S(2)}, u32[]{:S(2)}) collective-permute-start(bf16[256,256]{1,0:T(8,128)(2,1)S(1)} %pad_maximum_fusion.2), channel_id=1, source_target_pairs={{0,9},{1,8},{2,11},{3,10},{4,13},{5,12},{6,15},{7,14},{8,1},{9,0},... | collective-permute-start | bytes 393224 | tf_op jit(solution)/shard_map/ppermute | solution.py:26
  20.8 5.3 %collective-permute-start.8 = (bf16[512,32]{1,0:T(8,128)(2,1)S(1)}, bf16[512,32]{1,0:T(8,128)(2,1)S(1)}, u32[]{:S(2)}, u32[]{:S(2)}) collective-permute-start(bf16[512,32]{1,0:T(8,128)(2,1)S(1)} %pad_maximum_fusion.3), channel_id=1, source_target_pairs={{0,9},{1,8},{2,11},{3,10},{4,13},{5,12},{6,15},{7,14},{8,1},{9,0},... | collective-permute-start | bytes 98312 | tf_op jit(solution)/shard_map/ppermute | solution.py:26
  23.4 2.9 %collective-permute-start.5 = (bf16[512,256]{1,0:T(8,128)(2,1)S(1)}, bf16[512,256]{1,0:T(8,128)(2,1)S(1)}, u32[]{:S(2)}, u32[]{:S(2)}) collective-permute-start(bf16[512,256]{1,0:T(8,128)(2,1)S(1)} %pad_maximum_fusion), channel_id=1, source_target_pairs={{0,1},{1,0},{2,3},{3,2},{4,5},{5,4},{6,7},{7,6},{8,9},{9,8},{10,11... | collective-permute-start | bytes 786440 | tf_op jit(solution)/shard_map/ppermute | solution.py:26
  26.2 0.9 %copy-start.1 = (bf16[128,768]{1,0:T(8,128)(2,1)S(1)}, bf16[128,768]{1,0:T(8,128)(2,1)}, u32[]{:S(2)}) copy-start(bf16[128,768]{1,0:T(8,128)(2,1)} %frozen_query_ref.1) | copy-start | bytes 589828
  26.2 0.9 %copy-start.2 = (bf16[32,768]{1,0:T(8,128)(2,1)S(1)}, bf16[32,768]{1,0:T(8,128)(2,1)}, u32[]{:S(2)}) copy-start(bf16[32,768]{1,0:T(8,128)(2,1)} %query_up_ref.1) | copy-start | bytes 147460
  26.2 0.9 %copy-start.3 = (s32[16]{0:T(128)S(1)}, s32[16]{0:T(128)}, u32[]{:S(2)}) copy-start(s32[16]{0:T(128)} %order_ref.1) | copy-start | bytes 196

commit v2 on v1

v2 whole, which is shorter than its diff:
```python
import functools
import math

import jax
import jax.numpy as jnp
from jax import lax
from jax.experimental import pallas as pl
from jax.experimental.pallas import tpu as pltpu
from jax.sharding import PartitionSpec as P

HEAD_SIZE = 128
KEY_VALUE_HEADS = 2
ADAPTER_RANK = 32
ADAPTER_SCALE = 0.5
MASKED = -1e30
AXES = ("ctx", "head")
SCORE_FACTOR = math.log2(math.e) / math.sqrt(HEAD_SIZE)
VMEM_LIMIT = 24 * 1024 * 1024


def exchange(value, ctx_bit, head_bits):
    ctx_count, head_count = lax.axis_size("ctx"), lax.axis_size("head")
    pairs = [
        (i * head_count + h, (i ^ ctx_bit) * head_count + (h ^ head_bits))
        for i in range(ctx_count)
        for h in range(head_count)
    ]
    return lax.ppermute(value, AXES, pairs)


def gather_patterns(bits):
    patterns = [0]
    for bit in bits:
        patterns += [p ^ bit for p in patterns]
    return patterns


def half_blocks(patterns, ctx, side):
    blocks = len(patterns)
    found = []
    for entry in range(2 * blocks):
        pattern = patterns[entry % blocks]
        half = (side + pattern.bit_count() + entry // blocks) % 2
        found.append((entry % blocks, half, 2 * (ctx ^ pattern) + half))
    return found


def diagonal_row(matrix):
    row = lax.broadcasted_iota(jnp.int32, matrix.shape, 0)
    lane = lax.broadcasted_iota(jnp.int32, matrix.shape, 1)
    return jnp.sum(jnp.where(row == lane, matrix, 0.0), axis=0, keepdims=True)


def prologue_kernel(
    hidden_ref, down_ref, key_ref, value_ref, low_ref, kv_ref, hidden_buf, down_buf, sems, kv_sems
):
    head = lax.axis_index("head")
    side = head % 2
    group = head // (lax.axis_size("head") // KEY_VALUE_HEADS)
    half = kv_ref.shape[0]
    rows = pl.ds(pl.multiple_of(side * half, half), half)
    columns = pl.ds(pl.multiple_of(group * HEAD_SIZE, HEAD_SIZE), HEAD_SIZE)
    chunks = sems.shape[0]
    depth = down_ref.shape[0] // chunks
    copies = []
    for chunk in range(chunks):
        part = pl.ds(chunk * depth, depth)
        pair = (
            pltpu.make_async_copy(hidden_ref.at[:, part], hidden_buf.at[:, part], sems.at[chunk, 0]),
            pltpu.make_async_copy(down_ref.at[part, :], down_buf.at[part, :], sems.at[chunk, 1]),
        )
        for copy in pair:
            copy.start()
        copies.append(pair)
    kv_copies = [
        pltpu.make_async_copy(
            ref.at[rows, columns], kv_ref.at[:, pl.ds(n * HEAD_SIZE, HEAD_SIZE)], kv_sems.at[n]
        )
        for n, ref in enumerate((key_ref, value_ref))
    ]
    for copy in kv_copies:
        copy.start()
    total = jnp.zeros((hidden_ref.shape[0], down_ref.shape[1]), jnp.float32)
    for chunk in range(chunks):
        for copy in copies[chunk]:
            copy.wait()
        part = slice(chunk * depth, (chunk + 1) * depth)
        total += jnp.dot(
            hidden_buf[:, part], down_buf[part, :], preferred_element_type=jnp.float32
        )
    low_ref[...] = total.T.astype(jnp.bfloat16)
    for copy in kv_copies:
        copy.wait()


def prologue(hidden, down, keys, values):
    tok_dev, depth = hidden.shape
    rank = down.shape[1]
    chunks = 4
    any_space = pl.BlockSpec(memory_space=pl.ANY)
    vmem = pl.BlockSpec(memory_space=pltpu.VMEM)
    return pl.pallas_call(
        prologue_kernel,
        out_shape=(
            jax.ShapeDtypeStruct((rank, tok_dev), jnp.bfloat16),
            jax.ShapeDtypeStruct((tok_dev // 2, 2 * HEAD_SIZE), jnp.bfloat16),
        ),
        in_specs=[any_space] * 4,
        out_specs=(vmem, vmem),
        scratch_shapes=[
            pltpu.VMEM(hidden.shape, jnp.bfloat16),
            pltpu.VMEM(down.shape, jnp.bfloat16),
            pltpu.SemaphoreType.DMA((chunks, 2)),
            pltpu.SemaphoreType.DMA((2,)),
        ],
        compiler_params=pltpu.CompilerParams(vmem_limit_bytes=VMEM_LIMIT),
        cost_estimate=pl.CostEstimate(
            flops=2 * tok_dev * depth * rank, bytes_accessed=tok_dev * depth * 4, transcendentals=0
        ),
    )(hidden, down, keys, values)


def weights_kernel(
    patterns, order_ref, frozen_query_ref, low_ref, query_up_ref, kv_ref, weights_ref, top_ref, bias_ref
):
    tok_dev, width = frozen_query_ref.shape
    span = tok_dev // 2
    heads = width // HEAD_SIZE
    ctx, side = lax.axis_index("ctx"), lax.axis_index("head") % 2

    queries = (
        frozen_query_ref[...].astype(jnp.float32)
        + ADAPTER_SCALE
        * lax.dot_general(
            low_ref[:ADAPTER_RANK, :],
            query_up_ref[...],
            (((0,), (0,)), ((), ())),
            preferred_element_type=jnp.float32,
        )
    ).astype(jnp.bfloat16)

    row = lax.broadcasted_iota(jnp.int32, (tok_dev, HEAD_SIZE), 0)
    lane = lax.broadcasted_iota(jnp.int32, (tok_dev, HEAD_SIZE), 1)
    query_pos = (
        jnp.where(row < span, order_ref[2 * ctx], order_ref[2 * ctx + 1]) * span + row % span
    )
    halves = half_blocks(patterns, ctx, side)
    for tile in range(len(patterns)):
        first, second = order_ref[halves[2 * tile][2]], order_ref[halves[2 * tile + 1][2]]
        key_pos = jnp.where(lane < span, first, second) * span + lane % span
        bias_ref[:, tile * HEAD_SIZE : (tile + 1) * HEAD_SIZE] = jnp.where(
            key_pos <= query_pos, 0.0, MASKED
        )
    keys = kv_ref[:, :HEAD_SIZE]
    for head in range(heads):
        scores = (
            lax.dot_general(
                queries[:, head * HEAD_SIZE : (head + 1) * HEAD_SIZE],
                keys,
                (((1,), (1,)), ((), ())),
                preferred_element_type=jnp.float32,
            )
            * SCORE_FACTOR
            + bias_ref[...]
        )
        top = jnp.max(scores, axis=1, keepdims=True)
        weights_ref[head * tok_dev : (head + 1) * tok_dev, :] = jnp.exp2(scores - top).astype(
            jnp.bfloat16
        )
        top_ref[head : head + 1, :] = diagonal_row(jnp.broadcast_to(top, (tok_dev, tok_dev)))


def make_weights(patterns, order, frozen_query, low, query_up, kv):
    tok_dev, width = frozen_query.shape
    heads = width // HEAD_SIZE
    key_count = kv.shape[0]
    vmem = pl.BlockSpec(memory_space=pltpu.VMEM)
    return pl.pallas_call(
        functools.partial(weights_kernel, patterns),
        out_shape=(
            jax.ShapeDtypeStruct((heads * tok_dev, key_count), jnp.bfloat16),
            jax.ShapeDtypeStruct((heads, tok_dev), jnp.float32),
        ),
        in_specs=[pl.BlockSpec(memory_space=pltpu.SMEM)] + [vmem] * 4,
        out_specs=(vmem, vmem),
        scratch_shapes=[pltpu.VMEM((tok_dev, key_count), jnp.float32)],
        compiler_params=pltpu.CompilerParams(vmem_limit_bytes=VMEM_LIMIT),
        cost_estimate=pl.CostEstimate(
            flops=2 * tok_dev * width * key_count,
            bytes_accessed=2 * tok_dev * heads * key_count,
            transcendentals=heads * tok_dev * key_count,
        ),
    )(order, frozen_query, low, query_up, kv)


def values_kernel(
    patterns, weights_ref, top_ref, kv_ref, low_value_ref, value_up_ref, attended_ref, normalizer_ref, value_ref
):
    heads, tok_dev = top_ref.shape
    span = tok_dev // 2
    head_index = lax.axis_index("head")
    ctx, side = lax.axis_index("ctx"), head_index % 2
    group = head_index // (lax.axis_size("head") // KEY_VALUE_HEADS)
    value_up = value_up_ref[:, pl.ds(pl.multiple_of(group * HEAD_SIZE, HEAD_SIZE), HEAD_SIZE)]
    updates = [
        ADAPTER_SCALE
        * lax.dot_general(
            low_value_ref[n * ADAPTER_RANK : (n + 1) * ADAPTER_RANK, :],
            value_up,
            (((0,), (0,)), ((), ())),
            preferred_element_type=jnp.float32,
        )
        for n in range(len(patterns))
    ]
    for entry, (block, half, _) in enumerate(half_blocks(patterns, ctx, side)):
        here = slice(entry * span, (entry + 1) * span)
        update = jnp.where(half == 0, updates[block][:span], updates[block][span:])
        value_ref[here, :HEAD_SIZE] = (
            kv_ref[here, HEAD_SIZE:].astype(jnp.float32) + update
        ).astype(jnp.bfloat16)
    value_ref[:, HEAD_SIZE:] = jnp.ones((value_ref.shape[0], HEAD_SIZE), jnp.bfloat16)
    for head in range(heads):
        sums = jnp.dot(
            weights_ref[head * tok_dev : (head + 1) * tok_dev, :],
            value_ref[...],
            preferred_element_type=jnp.float32,
        )
        total = sums[:, HEAD_SIZE:]
        attended_ref[:, head * HEAD_SIZE : (head + 1) * HEAD_SIZE] = (
            sums[:, :HEAD_SIZE] / total
        ).astype(jnp.bfloat16)
        normalizer_ref[head : head + 1, :] = top_ref[head : head + 1, :] * math.log(2.0) + jnp.log(
            diagonal_row(total)
        )


def weigh_values(patterns, weights, top, kv, low_value, value_up):
    heads, tok_dev = top.shape
    key_count = kv.shape[0]
    width = heads * HEAD_SIZE
    vmem = pl.BlockSpec(memory_space=pltpu.VMEM)
    return pl.pallas_call(
        functools.partial(values_kernel, patterns),
        out_shape=(
            jax.ShapeDtypeStruct((tok_dev, width), jnp.bfloat16),
            jax.ShapeDtypeStruct((heads, tok_dev), jnp.float32),
        ),
        in_specs=[vmem] * 5,
        out_specs=(vmem, vmem),
        scratch_shapes=[pltpu.VMEM((key_count, 2 * HEAD_SIZE), jnp.bfloat16)],
        compiler_params=pltpu.CompilerParams(vmem_limit_bytes=VMEM_LIMIT),
        cost_estimate=pl.CostEstimate(
            flops=2 * tok_dev * width * key_count,
            bytes_accessed=2 * tok_dev * heads * key_count,
            transcendentals=0,
        ),
    )(weights, top, kv, low_value, value_up)


def attend_long(patterns, ctx, head, order, frozen_query, low, query_up, kv, low_value, value_up):
    tok_dev, width = frozen_query.shape
    span = tok_dev // 2
    heads = width // HEAD_SIZE
    blocks = len(patterns)
    side = head % 2
    group = head // (lax.axis_size("head") // KEY_VALUE_HEADS)
    value_up = lax.dynamic_slice_in_dim(value_up, group * HEAD_SIZE, HEAD_SIZE, 1)
    low = low.T
    low_value = low_value.reshape(blocks, ADAPTER_RANK, tok_dev).transpose(0, 2, 1)
    queries = (
        frozen_query.astype(jnp.float32)
        + ADAPTER_SCALE
        * jnp.dot(low[:, :ADAPTER_RANK], query_up, preferred_element_type=jnp.float32)
    ).astype(jnp.bfloat16)
    queries = queries.reshape(tok_dev, heads, HEAD_SIZE).transpose(1, 0, 2).reshape(-1, HEAD_SIZE)
    pattern = jnp.tile(jnp.array(patterns, jnp.int32), 2)
    parity = jnp.array([p.bit_count() for p in patterns] + [p.bit_count() + 1 for p in patterns])
    half = (side + parity.astype(jnp.int32)) % 2
    key_spans = order[2 * (ctx ^ pattern) + half]
    inner = jnp.arange(span, dtype=jnp.int32)
    key_pos = (key_spans[:, None] * span + inner).reshape(-1)
    query_spans = lax.dynamic_slice_in_dim(order, 2 * ctx, 2)
    query_pos = jnp.tile((query_spans[:, None] * span + inner).reshape(-1), heads)
    index = jnp.tile(jnp.arange(blocks, dtype=jnp.int32), 2)
    low_rows = low_value.reshape(2 * blocks, span, ADAPTER_RANK)[2 * index + half]
    values = (
        kv[:, HEAD_SIZE:].astype(jnp.float32)
        + ADAPTER_SCALE
        * jnp.dot(
            low_rows.reshape(-1, ADAPTER_RANK), value_up, preferred_element_type=jnp.float32
        )
    ).astype(jnp.bfloat16)
    chunk = math.gcd(kv.shape[0], 1024)

    def step(number, state):
        top, total, summed = state
        at = number * chunk
        keys = lax.dynamic_slice_in_dim(kv, at, chunk, 0)[:, :HEAD_SIZE]
        scores = lax.dot_general(
            queries, keys, (((1,), (1,)), ((), ())), preferred_element_type=jnp.float32
        ) * (1.0 / math.sqrt(HEAD_SIZE))
        visible = lax.dynamic_slice_in_dim(key_pos, at, chunk)[None, :] <= query_pos[:, None]
        new_top = jnp.maximum(top, jnp.max(jnp.where(visible, scores, MASKED), axis=1))
        scale = jnp.exp(top - new_top)
        weights = jnp.where(visible, jnp.exp(scores - new_top[:, None]), 0.0)
        summed = summed * scale[:, None] + jnp.dot(
            weights.astype(jnp.bfloat16),
            lax.dynamic_slice_in_dim(values, at, chunk, 0),
            preferred_element_type=jnp.float32,
        )
        return (new_top, total * scale + jnp.sum(weights, axis=1), summed)

    rows = heads * tok_dev
    top, total, summed = lax.fori_loop(
        0,
        kv.shape[0] // chunk,
        step,
        (
            jnp.full((rows,), MASKED, jnp.float32),
            jnp.zeros((rows,), jnp.float32),
            jnp.zeros((rows, HEAD_SIZE), jnp.float32),
        ),
    )
    attended = (summed / total[:, None]).astype(jnp.bfloat16)
    attended = attended.reshape(heads, tok_dev, HEAD_SIZE).transpose(1, 0, 2)
    return attended.reshape(tok_dev, width), (top + jnp.log(total)).reshape(heads, tok_dev)


def local(
    hidden,
    frozen_query_rows,
    frozen_key_rows,
    frozen_value_rows,
    adapter_down_factors,
    query_up_factor,
    value_up_factor,
    slot_span_order,
):
    ctx_count, head_count = lax.axis_size("ctx"), lax.axis_size("head")
    ctx, head = lax.axis_index("ctx"), lax.axis_index("head")
    bits = [ctx_count >> k for k in range(1, ctx_count.bit_length())]
    if len(bits) == 3:
        bits = [bits[0], bits[2], bits[1]]
    patterns = gather_patterns(bits)

    low, kv = prologue(hidden, adapter_down_factors, frozen_key_rows, frozen_value_rows)
    head_bit = 1
    while head_bit < head_count:
        other = exchange(low, 0, head_bit | 1)
        low = (low.astype(jnp.float32) + other.astype(jnp.float32)).astype(jnp.bfloat16)
        if head_bit == 1:
            low, kv = lax.optimization_barrier((low, kv))
        head_bit *= 2
    low_value = low[ADAPTER_RANK:]
    for bit in bits:
        low_value = jnp.concatenate([low_value, exchange(low_value, bit, 1)], axis=0)
        kv = jnp.concatenate([kv, exchange(kv, bit, 1)], axis=0)
    kv = jnp.concatenate([kv, exchange(kv, 0, 1)], axis=0)
    if kv.shape[0] > 1024:
        return attend_long(
            patterns, ctx, head, slot_span_order, frozen_query_rows, low, query_up_factor, kv, low_value, value_up_factor
        )
    weights, top = make_weights(
        patterns, slot_span_order, frozen_query_rows, low, query_up_factor, kv
    )
    return weigh_values(patterns, weights, top, kv, low_value, value_up_factor)


def solution(mesh):
    placed = (
        P("ctx", "head"),
        P("ctx", "head"),
        P("ctx", None),
        P("ctx", None),
        P("head", None),
        P(None, "head"),
        P(),
        P(),
    )
    return jax.shard_map(
        local,
        mesh=mesh,
        in_specs=placed,
        out_specs=(P("ctx", "head"), P("head", "ctx")),
        check_vma=False,
    )
```

time: 30.4 us -> 29.7 us (0.977)
  waiting for transfers between devices: 9.21 us -> 5.91 us
  Pallas kernels: 2.89 us -> 4.74 us
  starting transfers between devices: 12.2 us -> 13.9 us
  matrix products: 1.24 us -> 0 us
  local copies, waits for them, and re-layouts: 3.47 us -> 4 us
    ppermute x9, waiting for transfers between devices: 9.21 us -> 5.91 us  [exchange(): return lax.ppermute(value, AXES, pairs)]
    unnamed x13 -> x19, local copies, waits for them, and re-layouts: 1.94 us -> 3.98 us
    pallas_call x1 -> x3, Pallas kernels: 2.89 us -> 4.74 us  [the longest x1 1.71 us: make_weights(): pl.pallas_call(functools.partial(weights_kernel, patterns), out_shape=(ja...]
    ppermute x9, starting transfers between devices: 12.2 us -> 13.9 us  [exchange(): return lax.ppermute(value, AXES, pairs)]
    dynamic_slice x3 -> x0, local copies, waits for them, and re-layouts: 1.44 us -> none  [the longest x2 1.44 us: own_half(): lax.dynamic_slice(rows, (side * half, group * HEAD_SIZE), (half, HEAD_SIZE))]
    dot_general x1 -> x0, matrix products: 1.24 us -> none  [local(): jnp.dot(hidden, adapter_down_factors, preferred_element_type=jnp.float32)]
  transfers between devices with their start and end apart: 9 -> 9, of which waited for: 5 -> 5; matrix products, arithmetic and copies ran while one was open for 6% -> 0% of each run, Pallas kernels for 0% -> 0%
where the time goes in v2:
time: 29.7 us; the launch traced here: 29.4 us
  starting transfers between devices  13.9 us (47%)
  waiting for transfers between devices  5.91 us (20%)
  Pallas kernels  4.74 us (16%)
  local copies, waits for them, and re-layouts  4 us (13%)
  between operations  0.76 us (3%)
    ppermute x9, starting transfers between devices, exchange(): return lax.ppermute(value, AXES, pairs)  13.9 us
    ppermute x9, waiting for transfers between devices, exchange(): return lax.ppermute(value, AXES, pairs)  5.91 us
    unnamed x19, local copies, waits for them, and re-layouts  3.98 us
    pallas_call x1, Pallas kernels, make_weights(): pl.pallas_call(functools.partial(weights_kernel, patterns), out_shape=(ja...  1.71 us
    pallas_call x1, Pallas kernels, weigh_values(): pl.pallas_call(functools.partial(values_kernel, patterns), out_shape=(jax...  1.53 us
    pallas_call x1, Pallas kernels, prologue(): pl.pallas_call(prologue_kernel, out_shape=(jax.ShapeDtypeStruct((rank, to...  1.5 us
  transfers between devices with their start and end apart: 9, of which 5 were waited for; matrix products, arithmetic and copies ran while one was open for 0% of the time, Pallas kernels for 0%

profile of v2, /device:TPU:0, one launch (start us, length us, event | category | flops | bytes accessed | tf_op | source)
XLA Modules:
  0.0 29.4 jit_solution(17114116848919307920)
XLA Ops:
  0.6 1.2 %copy.10.down_ref = bf16[2048,64]{1,0:T(8,128)(2,1)S(1)} copy(bf16[2048,64]{0,1:T(8,128)(2,1)} %param.12) | data formatting | bytes 524288 | tf_op args[4]
  1.9 0.0 copy-start
  1.9 1.0 %copy-done = bf16[128,2048]{1,0:T(8,128)(2,1)S(1)} copy-done((bf16[128,2048]{1,0:T(8,128)(2,1)S(1)}, bf16[128,2048]{1,0:T(8,128)(2,1)}, u32[]{:S(2)}) %copy-start) | copy-done | bytes 524312
  2.9 0.0 copy-start.1
  2.9 0.8 %copy-done.1 = bf16[128,256]{1,0:T(8,128)(2,1)S(1)} copy-done((bf16[128,256]{1,0:T(8,128)(2,1)S(1)}, bf16[128,256]{1,0:T(8,128)(2,1)}, u32[]{:S(2)}) %copy-start.1) | copy-done | bytes 65560
  3.7 0.0 copy-start.2
  3.7 0.8 %copy-done.2 = bf16[128,256]{1,0:T(8,128)(2,1)S(1)} copy-done((bf16[128,256]{1,0:T(8,128)(2,1)S(1)}, bf16[128,256]{1,0:T(8,128)(2,1)}, u32[]{:S(2)}) %copy-start.2) | copy-done | bytes 65560
  4.6 0.0 copy-start.4
  4.6 0.0 copy-start.5
  4.6 0.0 copy-start.6
  4.6 1.5 %shard_map.95 = (bf16[64,128]{1,0:T(8,128)(2,1)S(1)}, bf16[64,256]{1,0:T(8,128)(2,1)S(1)}) custom-call(bf16[128,2048]{1,0:T(8,128)(2,1)S(1)} %copy-done, bf16[2048,64]{1,0:T(8,128)(2,1)S(1)} %copy.10.down_ref, bf16[128,256]{1,0:T(8,128)(2,1)S(1)} %copy-done.1, bf16[128,256]{1,0:T(8,128)(2,1)S(1)} %copy-done.2), custom_call_target="tpu_custom_call" | custom-call | flops 33554432 | bytes 1048576 | tf_op jit(solution)/shard_map/pallas_call | solution.py:102
  6.1 0.5 %collective-permute-start = (bf16[64,128]{1,0:T(8,128)(2,1)S(1)}, bf16[64,128]{1,0:T(8,128)(2,1)S(1)}, u32[]{:S(2)}, u32[]{:S(2)}) collective-permute-start(bf16[64,128]{1,0:T(8,128)(2,1)S(1)} %get-tuple-element.8), channel_id=1, source_target_pairs={{0,1},{1,0},{2,3},{3,2},{4,5},{5,4},{6,7},{7,6},{8,9},{9,8},{10,11... | collective-permute-start | bytes 49160 | tf_op jit(solution)/shard_map/ppermute | solution.py:28
  6.6 0.8 %collective-permute-done = bf16[64,128]{1,0:T(8,128)(2,1)S(1)} collective-permute-done((bf16[64,128]{1,0:T(8,128)(2,1)S(1)}, bf16[64,128]{1,0:T(8,128)(2,1)S(1)}, u32[]{:S(2)}, u32[]{:S(2)}) %collective-permute-start) | collective-permute-done | bytes 16416 | tf_op jit(solution)/shard_map/ppermute | solution.py:28
  7.5 2.7 %collective-permute-start.1 = (bf16[64,128]{1,0:T(8,128)(2,1)S(1)}, bf16[64,128]{1,0:T(8,128)(2,1)S(1)}, u32[]{:S(2)}, u32[]{:S(2)}) collective-permute-start(bf16[64,128]{1,0:T(8,128)(2,1)S(1)} %add_convert_fusion.1), channel_id=1, source_target_pairs={{0,3},{1,2},{2,1},{3,0},{4,7},{5,6},{6,5},{7,4},{8,11},{9,10},{10,... | collective-permute-start | bytes 49160 | tf_op jit(solution)/shard_map/ppermute | solution.py:28
  10.2 2.5 %collective-permute-start.2 = (bf16[64,256]{1,0:T(8,128)(2,1)S(1)}, bf16[64,256]{1,0:T(8,128)(2,1)S(1)}, u32[]{:S(2)}, u32[]{:S(2)}) collective-permute-start(bf16[64,256]{1,0:T(8,128)(2,1)S(1)} %get-tuple-element.11), channel_id=1, source_target_pairs={{0,17},{1,16},{2,19},{3,18},{4,21},{5,20},{6,23},{7,22},{8,25},{9,... | collective-permute-start | bytes 98312 | tf_op jit(solution)/shard_map/ppermute | solution.py:28
  12.7 0.0 collective-permute-done.1
  12.7 1.8 %collective-permute-start.6 = (bf16[32,128]{1,0:T(8,128)(2,1)S(1)}, bf16[32,128]{1,0:T(8,128)(2,1)S(1)}, u32[]{:S(2)}, u32[]{:S(2)}) collective-permute-start(bf16[32,128]{1,0:T(8,128)(2,1)S(1)} %slice.4), channel_id=1, source_target_pairs={{0,17},{1,16},{2,19},{3,18},{4,21},{5,20},{6,23},{7,22},{8,25},{9,... | collective-permute-start | bytes 24584 | tf_op jit(solution)/shard_map/ppermute | solution.py:28
  14.5 0.0 collective-permute-done.2
  14.5 1.5 %collective-permute-start.3 = (bf16[128,256]{1,0:T(8,128)(2,1)S(1)}, bf16[128,256]{1,0:T(8,128)(2,1)S(1)}, u32[]{:S(2)}, u32[]{:S(2)}) collective-permute-start(bf16[128,256]{1,0:T(8,128)(2,1)S(1)} %pad_maximum_fusion.2), channel_id=1, source_target_pairs={{0,5},{1,4},{2,7},{3,6},{4,1},{5,0},{6,3},{7,2},{8,13},{9,12},{10,... | collective-permute-start | bytes 196616 | tf_op jit(solution)/shard_map/ppermute | solution.py:28
  16.0 0.8 %collective-permute-done.6 = bf16[32,128]{1,0:T(8,128)(2,1)S(1)} collective-permute-done((bf16[32,128]{1,0:T(8,128)(2,1)S(1)}, bf16[32,128]{1,0:T(8,128)(2,1)S(1)}, u32[]{:S(2)}, u32[]{:S(2)}) %collective-permute-start.6) | collective-permute-done | bytes 8224 | tf_op jit(solution)/shard_map/ppermute | solution.py:28
  16.8 1.3 %collective-permute-start.7 = (bf16[64,128]{1,0:T(8,128)(2,1)S(1)}, bf16[64,128]{1,0:T(8,128)(2,1)S(1)}, u32[]{:S(2)}, u32[]{:S(2)}) collective-permute-start(bf16[64,128]{1,0:T(8,128)(2,1)S(1)} %pad_maximum_fusion.5), channel_id=1, source_target_pairs={{0,5},{1,4},{2,7},{3,6},{4,1},{5,0},{6,3},{7,2},{8,13},{9,12},{10,... | collective-permute-start | bytes 49160 | tf_op jit(solution)/shard_map/ppermute | solution.py:28
  18.0 0.5 %collective-permute-done.3 = bf16[128,256]{1,0:T(8,128)(2,1)S(1)} collective-permute-done((bf16[128,256]{1,0:T(8,128)(2,1)S(1)}, bf16[128,256]{1,0:T(8,128)(2,1)S(1)}, u32[]{:S(2)}, u32[]{:S(2)}) %collective-permute-start.3) | collective-permute-done | bytes 65568 | tf_op jit(solution)/shard_map/ppermute | solution.py:28
  18.5 1.5 %collective-permute-start.4 = (bf16[256,256]{1,0:T(8,128)(2,1)S(1)}, bf16[256,256]{1,0:T(8,128)(2,1)S(1)}, u32[]{:S(2)}, u32[]{:S(2)}) collective-permute-start(bf16[256,256]{1,0:T(8,128)(2,1)S(1)} %pad_maximum_fusion.1), channel_id=1, source_target_pairs={{0,9},{1,8},{2,11},{3,10},{4,13},{5,12},{6,15},{7,14},{8,1},{9,0},... | collective-permute-start | bytes 393224 | tf_op jit(solution)/shard_map/ppermute | solution.py:28
  20.1 0.0 copy-start.3
  20.1 0.0 collective-permute-done.7
  20.1 1.2 %collective-permute-start.8 = (bf16[128,128]{1,0:T(8,128)(2,1)S(1)}, bf16[128,128]{1,0:T(8,128)(2,1)S(1)}, u32[]{:S(2)}, u32[]{:S(2)}) collective-permute-start(bf16[128,128]{1,0:T(8,128)(2,1)S(1)} %pad_maximum_fusion.4), channel_id=1, source_target_pairs={{0,9},{1,8},{2,11},{3,10},{4,13},{5,12},{6,15},{7,14},{8,1},{9,0},... | collective-permute-start | bytes 98312 | tf_op jit(solution)/shard_map/ppermute | solution.py:28
  21.3 2.7 %collective-permute-done.4 = bf16[256,256]{1,0:T(8,128)(2,1)S(1)} collective-permute-done((bf16[256,256]{1,0:T(8,128)(2,1)S(1)}, bf16[256,256]{1,0:T(8,128)(2,1)S(1)}, u32[]{:S(2)}, u32[]{:S(2)}) %collective-permute-start.4) | collective-permute-done | bytes 131104 | tf_op jit(solution)/shard_map/ppermute | solution.py:28
  24.0 0.9 %collective-permute-start.5 = (bf16[512,256]{1,0:T(8,128)(2,1)S(1)}, bf16[512,256]{1,0:T(8,128)(2,1)S(1)}, u32[]{:S(2)}, u32[]{:S(2)}) collective-permute-start(bf16[512,256]{1,0:T(8,128)(2,1)S(1)} %pad_maximum_fusion), channel_id=1, source_target_pairs={{0,1},{1,0},{2,3},{3,2},{4,5},{5,4},{6,7},{7,6},{8,9},{9,8},{10,11... | collective-permute-start | bytes 786440 | tf_op jit(solution)/shard_map/ppermute | solution.py:28
  24.9 0.0 collective-permute-done.8
  25.0 1.1 %collective-permute-done.5 = bf16[512,256]{1,0:T(8,128)(2,1)S(1)} collective-permute-done((bf16[512,256]{1,0:T(8,128)(2,1)S(1)}, bf16[512,256]{1,0:T(8,128)(2,1)S(1)}, u32[]{:S(2)}, u32[]{:S(2)}) %collective-permute-start.5) | collective-permute-done | bytes 262176 | tf_op jit(solution)/shard_map/ppermute | solution.py:28
  26.1 0.0 copy-done.4
  26.1 0.0 copy-done.5
  26.1 0.0 copy-done.6
  26.1 1.7 %shard_map.96 = (bf16[768,1024]{1,0:T(8,128)(2,1)S(1)}, f32[6,128]{1,0:T(8,128)S(1)}) custom-call(s32[16]{0:T(128)S(1)} %copy-done.6, bf16[128,768]{1,0:T(8,128)(2,1)S(1)} %copy-done.4, bf16[64,128]{1,0:T(8,128)(2,1)S(1)} %add_convert_fusion.low_ref, bf16[32,768]{1,0:T(8,128)(2,1)S(1)} %copy-done.5, ...), custom_call_target="tpu_custom_call" | custom-call | flops 201326592 | bytes 1572864 | tf_op jit(solution)/shard_map/pallas_call | solution.py:178
  27.8 0.0 copy-done.3
  27.8 1.5 %shard_map.97 = (bf16[128,768]{1,0:T(8,128)(2,1)}, f32[6,128]{1,0:T(8,128)}) custom-call(bf16[768,1024]{1,0:T(8,128)(2,1)S(1)} %get-tuple-element.12.weights_ref, f32[6,128]{1,0:T(8,128)S(1)} %get-tuple-element.13.top_ref, bf16[1024,256]{1,0:T(8,128)(2,1)S(1)} %constant_dynamic-update-slice_fusion.kv_ref, ...), custom_call_target="tpu_custom_call" | custom-call | flops 201326592 | bytes 1572864 | tf_op jit(solution)/shard_map/pallas_call | solution.py:242
  (14 shorter events, 0.1 us)
Async XLA Ops:
  1.9 1.0 %copy-start = (bf16[128,2048]{1,0:T(8,128)(2,1)S(1)}, bf16[128,2048]{1,0:T(8,128)(2,1)}, u32[]{:S(2)}) copy-start(bf16[128,2048]{1,0:T(8,128)(2,1)} %hidden_ref.1) | copy-start | bytes 1572868
  2.9 0.8 %copy-start.1 = (bf16[128,256]{1,0:T(8,128)(2,1)S(1)}, bf16[128,256]{1,0:T(8,128)(2,1)}, u32[]{:S(2)}) copy-start(bf16[128,256]{1,0:T(8,128)(2,1)} %key_ref.1) | copy-start | bytes 196612
  3.7 0.8 %copy-start.2 = (bf16[128,256]{1,0:T(8,128)(2,1)S(1)}, bf16[128,256]{1,0:T(8,128)(2,1)}, u32[]{:S(2)}) copy-start(bf16[128,256]{1,0:T(8,128)(2,1)} %value_ref.1) | copy-start | bytes 196612
  4.6 21.5 %copy-start.4 = (bf16[128,768]{1,0:T(8,128)(2,1)S(1)}, bf16[128,768]{1,0:T(8,128)(2,1)}, u32[]{:S(2)}) copy-start(bf16[128,768]{1,0:T(8,128)(2,1)} %frozen_query_ref.1) | copy-start | bytes 589828
  4.6 21.5 %copy-start.5 = (bf16[32,768]{1,0:T(8,128)(2,1)S(1)}, bf16[32,768]{1,0:T(8,128)(2,1)}, u32[]{:S(2)}) copy-start(bf16[32,768]{1,0:T(8,128)(2,1)} %query_up_ref.1) | copy-start | bytes 147460
  4.6 21.5 %copy-start.6 = (s32[16]{0:T(128)S(1)}, s32[16]{0:T(128)}, u32[]{:S(2)}) copy-start(s32[16]{0:T(128)} %order_ref.1) | copy-start | bytes 196
  6.1 1.4 %collective-permute-start = (bf16[64,128]{1,0:T(8,128)(2,1)S(1)}, bf16[64,128]{1,0:T(8,128)(2,1)S(1)}, u32[]{:S(2)}, u32[]{:S(2)}) collective-permute-start(bf16[64,128]{1,0:T(8,128)(2,1)S(1)} %get-tuple-element.8), channel_id=1, source_target_pairs={{0,1},{1,0},{2,3},{3,2},{4,5},{5,4},{6,7},{7,6},{8,9},{9,8},{10,11... | collective-permute-start | bytes 49160 | tf_op jit(solution)/shard_map/ppermute | solution.py:28
  7.5 5.2 %collective-permute-start.1 = (bf16[64,128]{1,0:T(8,128)(2,1)S(1)}, bf16[64,128]{1,0:T(8,128)(2,1)S(1)}, u32[]{:S(2)}, u32[]{:S(2)}) collective-permute-start(bf16[64,128]{1,0:T(8,128)(2,1)S(1)} %add_convert_fusion.1), channel_id=1, source_target_pairs={{0,3},{1,2},{2,1},{3,0},{4,7},{5,6},{6,5},{7,4},{8,11},{9,10},{10,... | collective-permute-start | bytes 49160 | tf_op jit(solution)/shard_map/ppermute | solution.py:28
  10.2 4.3 %collective-permute-start.2 = (bf16[64,256]{1,0:T(8,128)(2,1)S(1)}, bf16[64,256]{1,0:T(8,128)(2,1)S(1)}, u32[]{:S(2)}, u32[]{:S(2)}) collective-permute-start(bf16[64,256]{1,0:T(8,128)(2,1)S(1)} %get-tuple-element.11), channel_id=1, source_target_pairs={{0,17},{1,16},{2,19},{3,18},{4,21},{5,20},{6,23},{7,22},{8,25},{9,... | collective-permute-start | bytes 98312 | tf_op jit(solution)/shard_map/ppermute | solution.py:28
  12.7 4.0 %collective-permute-start.6 = (bf16[32,128]{1,0:T(8,128)(2,1)S(1)}, bf16[32,128]{1,0:T(8,128)(2,1)S(1)}, u32[]{:S(2)}, u32[]{:S(2)}) collective-permute-start(bf16[32,128]{1,0:T(8,128)(2,1)S(1)} %slice.4), channel_id=1, source_target_pairs={{0,17},{1,16},{2,19},{3,18},{4,21},{5,20},{6,23},{7,22},{8,25},{9,... | collective-permute-start | bytes 24584 | tf_op jit(solution)/shard_map/ppermute | solution.py:28
  14.5 4.0 %collective-permute-start.3 = (bf16[128,256]{1,0:T(8,128)(2,1)S(1)}, bf16[128,256]{1,0:T(8,128)(2,1)S(1)}, u32[]{:S(2)}, u32[]{:S(2)}) collective-permute-start(bf16[128,256]{1,0:T(8,128)(2,1)S(1)} %pad_maximum_fusion.2), channel_id=1, source_target_pairs={{0,5},{1,4},{2,7},{3,6},{4,1},{5,0},{6,3},{7,2},{8,13},{9,12},{10,... | collective-permute-start | bytes 196616 | tf_op jit(solution)/shard_map/ppermute | solution.py:28
  16.8 3.3 %collective-permute-start.7 = (bf16[64,128]{1,0:T(8,128)(2,1)S(1)}, bf16[64,128]{1,0:T(8,128)(2,1)S(1)}, u32[]{:S(2)}, u32[]{:S(2)}) collective-permute-start(bf16[64,128]{1,0:T(8,128)(2,1)S(1)} %pad_maximum_fusion.5), channel_id=1, source_target_pairs={{0,5},{1,4},{2,7},{3,6},{4,1},{5,0},{6,3},{7,2},{8,13},{9,12},{10,... | collective-permute-start | bytes 49160 | tf_op jit(solution)/shard_map/ppermute | solution.py:28
  18.5 5.5 %collective-permute-start.4 = (bf16[256,256]{1,0:T(8,128)(2,1)S(1)}, bf16[256,256]{1,0:T(8,128)(2,1)S(1)}, u32[]{:S(2)}, u32[]{:S(2)}) collective-permute-start(bf16[256,256]{1,0:T(8,128)(2,1)S(1)} %pad_maximum_fusion.1), channel_id=1, source_target_pairs={{0,9},{1,8},{2,11},{3,10},{4,13},{5,12},{6,15},{7,14},{8,1},{9,0},... | collective-permute-start | bytes 393224 | tf_op jit(solution)/shard_map/ppermute | solution.py:28
  20.1 7.8 %copy-start.3 = (bf16[32,256]{1,0:T(8,128)(2,1)S(1)}, bf16[32,256]{1,0:T(8,128)(2,1)}, u32[]{:S(2)}) copy-start(bf16[32,256]{1,0:T(8,128)(2,1)} %value_up_ref.1) | copy-start | bytes 49156
  20.1 4.8 %collective-permute-start.8 = (bf16[128,128]{1,0:T(8,128)(2,1)S(1)}, bf16[128,128]{1,0:T(8,128)(2,1)S(1)}, u32[]{:S(2)}, u32[]{:S(2)}) collective-permute-start(bf16[128,128]{1,0:T(8,128)(2,1)S(1)} %pad_maximum_fusion.4), channel_id=1, source_target_pairs={{0,9},{1,8},{2,11},{3,10},{4,13},{5,12},{6,15},{7,14},{8,1},{9,0},... | collective-permute-start | bytes 98312 | tf_op jit(solution)/shard_map/ppermute | solution.py:28
  24.0 2.0 %collective-permute-start.5 = (bf16[512,256]{1,0:T(8,128)(2,1)S(1)}, bf16[512,256]{1,0:T(8,128)(2,1)S(1)}, u32[]{:S(2)}, u32[]{:S(2)}) collective-permute-start(bf16[512,256]{1,0:T(8,128)(2,1)S(1)} %pad_maximum_fusion), channel_id=1, source_target_pairs={{0,1},{1,0},{2,3},{3,2},{4,5},{5,4},{6,7},{7,6},{8,9},{9,8},{10,11... | collective-permute-start | bytes 786440 | tf_op jit(solution)/shard_map/ppermute | solution.py:28

commit v3 on v2

--- a/solution.py
+++ b/solution.py
@@ -61,13 +61,13 @@
     rows = pl.ds(pl.multiple_of(side * half, half), half)
     columns = pl.ds(pl.multiple_of(group * HEAD_SIZE, HEAD_SIZE), HEAD_SIZE)
     chunks = sems.shape[0]
-    depth = down_ref.shape[0] // chunks
+    depth = down_ref.shape[1] // chunks
     copies = []
     for chunk in range(chunks):
         part = pl.ds(chunk * depth, depth)
         pair = (
             pltpu.make_async_copy(hidden_ref.at[:, part], hidden_buf.at[:, part], sems.at[chunk, 0]),
-            pltpu.make_async_copy(down_ref.at[part, :], down_buf.at[part, :], sems.at[chunk, 1]),
+            pltpu.make_async_copy(down_ref.at[:, part], down_buf.at[:, part], sems.at[chunk, 1]),
         )
         for copy in pair:
             copy.start()
@@ -80,24 +80,27 @@
     ]
     for copy in kv_copies:
         copy.start()
-    total = jnp.zeros((hidden_ref.shape[0], down_ref.shape[1]), jnp.float32)
+    total = jnp.zeros(low_ref.shape, jnp.float32)
     for chunk in range(chunks):
         for copy in copies[chunk]:
             copy.wait()
         part = slice(chunk * depth, (chunk + 1) * depth)
-        total += jnp.dot(
-            hidden_buf[:, part], down_buf[part, :], preferred_element_type=jnp.float32
-        )
-    low_ref[...] = total.T.astype(jnp.bfloat16)
+        total += lax.dot_general(
+            down_buf[:, part],
+            hidden_buf[:, part],
+            (((1,), (1,)), ((), ())),
+            preferred_element_type=jnp.float32,
+        )
+    low_ref[...] = total.astype(jnp.bfloat16)
     for copy in kv_copies:
         copy.wait()
 
 
 def prologue(hidden, down, keys, values):
     tok_dev, depth = hidden.shape
-    rank = down.shape[1]
+    rank = down.shape[0]
     chunks = 4
-    any_space = pl.BlockSpec(memory_space=pl.ANY)
+    any_space = pl.BlockSpec(memory_space=pltpu.HBM)
     vmem = pl.BlockSpec(memory_space=pltpu.VMEM)
     return pl.pallas_call(
         prologue_kernel,
@@ -117,7 +120,7 @@
         cost_estimate=pl.CostEstimate(
             flops=2 * tok_dev * depth * rank, bytes_accessed=tok_dev * depth * 4, transcendentals=0
         ),
-    )(hidden, down, keys, values)
+    )(*(pltpu.with_memory_space_constraint(x, pltpu.HBM) for x in (hidden, down, keys, values)))
 
 
 def weights_kernel(
@@ -343,13 +346,11 @@
         bits = [bits[0], bits[2], bits[1]]
     patterns = gather_patterns(bits)
 
-    low, kv = prologue(hidden, adapter_down_factors, frozen_key_rows, frozen_value_rows)
+    low, kv = prologue(hidden, adapter_down_factors.T, frozen_key_rows, frozen_value_rows)
     head_bit = 1
     while head_bit < head_count:
         other = exchange(low, 0, head_bit | 1)
         low = (low.astype(jnp.float32) + other.astype(jnp.float32)).astype(jnp.bfloat16)
-        if head_bit == 1:
-            low, kv = lax.optimization_barrier((low, kv))
         head_bit *= 2
     low_value = low[ADAPTER_RANK:]
     for bit in bits:

time: 29.7 us -> 26 us (0.88)
  local copies, waits for them, and re-layouts: 4 us -> 0.06 us
  waiting for transfers between devices: 5.91 us -> 7.23 us
  starting transfers between devices: 13.9 us -> 12.8 us
    unnamed x19 -> x12, local copies, waits for them, and re-layouts: 3.98 us -> 0.04 us
    ppermute x9, waiting for transfers between devices: 5.91 us -> 7.23 us  [exchange(): return lax.ppermute(value, AXES, pairs)]
    ppermute x9, starting transfers between devices: 13.9 us -> 12.8 us  [exchange(): return lax.ppermute(value, AXES, pairs)]
where the time goes in v3:
time: 26 us; the launch traced here: 25.8 us
  starting transfers between devices  12.8 us (49%)
  waiting for transfers between devices  7.23 us (28%)
  Pallas kernels  4.94 us (19%)
  between operations  0.76 us (3%)
    ppermute x9, starting transfers between devices, exchange(): return lax.ppermute(value, AXES, pairs)  12.8 us
    ppermute x9, waiting for transfers between devices, exchange(): return lax.ppermute(value, AXES, pairs)  7.23 us
    pallas_call x1, Pallas kernels, make_weights(): pl.pallas_call(functools.partial(weights_kernel, patterns), out_shape=(ja...  1.71 us
    pallas_call x1, Pallas kernels, prologue(): pl.pallas_call(prologue_kernel, out_shape=(jax.ShapeDtypeStruct((rank, to...  1.7 us
    pallas_call x1, Pallas kernels, weigh_values(): pl.pallas_call(functools.partial(values_kernel, patterns), out_shape=(jax...  1.53 us
  transfers between devices with their start and end apart: 9, of which 5 were waited for; matrix products, arithmetic and copies ran while one was open for 0% of the time, Pallas kernels for 0%

profile of v3, /device:TPU:0, one launch (start us, length us, event | category | flops | bytes accessed | tf_op | source)
XLA Modules:
  0.0 25.8 jit_solution(10245970646672547292)
XLA Ops:
  0.6 0.0 copy-start.1
  0.6 0.0 copy-start.2
  0.7 0.0 copy-start.3
  0.7 1.7 %shard_map.95 = (bf16[64,128]{1,0:T(8,128)(2,1)S(1)}, bf16[64,256]{1,0:T(8,128)(2,1)S(1)}) custom-call(bf16[128,2048]{1,0:T(8,128)(2,1)} %hidden_ref.1, bf16[64,2048]{1,0:T(8,128)(2,1)} %bitcast.1, bf16[128,256]{1,0:T(8,128)(2,1)} %key_ref.1, bf16[128,256]{1,0:T(8,128)(2,1)} %value_ref.1), custom_call_target="tpu_custom_call" | custom-call | flops 33554432 | bytes 1048576 | tf_op jit(solution)/shard_map/pallas_call | solution.py:105
  2.4 0.5 %collective-permute-start = (bf16[64,128]{1,0:T(8,128)(2,1)S(1)}, bf16[64,128]{1,0:T(8,128)(2,1)S(1)}, u32[]{:S(2)}, u32[]{:S(2)}) collective-permute-start(bf16[64,128]{1,0:T(8,128)(2,1)S(1)} %get-tuple-element.6), channel_id=1, source_target_pairs={{0,1},{1,0},{2,3},{3,2},{4,5},{5,4},{6,7},{7,6},{8,9},{9,8},{10,11... | collective-permute-start | bytes 49160 | tf_op jit(solution)/shard_map/ppermute | solution.py:28
  2.9 3.7 %collective-permute-start.2 = (bf16[64,256]{1,0:T(8,128)(2,1)S(1)}, bf16[64,256]{1,0:T(8,128)(2,1)S(1)}, u32[]{:S(2)}, u32[]{:S(2)}) collective-permute-start(bf16[64,256]{1,0:T(8,128)(2,1)S(1)} %get-tuple-element.7), channel_id=1, source_target_pairs={{0,17},{1,16},{2,19},{3,18},{4,21},{5,20},{6,23},{7,22},{8,25},{9,... | collective-permute-start | bytes 98312 | tf_op jit(solution)/shard_map/ppermute | solution.py:28
  6.6 0.0 collective-permute-done
  6.6 1.3 %collective-permute-start.1 = (bf16[64,128]{1,0:T(8,128)(2,1)S(1)}, bf16[64,128]{1,0:T(8,128)(2,1)S(1)}, u32[]{:S(2)}, u32[]{:S(2)}) collective-permute-start(bf16[64,128]{1,0:T(8,128)(2,1)S(1)} %add_convert_fusion.1), channel_id=1, source_target_pairs={{0,3},{1,2},{2,1},{3,0},{4,7},{5,6},{6,5},{7,4},{8,11},{9,10},{10,... | collective-permute-start | bytes 49160 | tf_op jit(solution)/shard_map/ppermute | solution.py:28
  7.9 2.0 %collective-permute-done.1 = bf16[64,128]{1,0:T(8,128)(2,1)S(1)} collective-permute-done((bf16[64,128]{1,0:T(8,128)(2,1)S(1)}, bf16[64,128]{1,0:T(8,128)(2,1)S(1)}, u32[]{:S(2)}, u32[]{:S(2)}) %collective-permute-start.1) | collective-permute-done | bytes 16416 | tf_op jit(solution)/shard_map/ppermute | solution.py:28
  9.9 0.9 %collective-permute-start.6 = (bf16[32,128]{1,0:T(8,128)(2,1)S(1)}, bf16[32,128]{1,0:T(8,128)(2,1)S(1)}, u32[]{:S(2)}, u32[]{:S(2)}) collective-permute-start(bf16[32,128]{1,0:T(8,128)(2,1)S(1)} %slice.4), channel_id=1, source_target_pairs={{0,17},{1,16},{2,19},{3,18},{4,21},{5,20},{6,23},{7,22},{8,25},{9,... | collective-permute-start | bytes 24584 | tf_op jit(solution)/shard_map/ppermute | solution.py:28
  10.8 0.0 collective-permute-done.2
  10.8 1.5 %collective-permute-start.3 = (bf16[128,256]{1,0:T(8,128)(2,1)S(1)}, bf16[128,256]{1,0:T(8,128)(2,1)S(1)}, u32[]{:S(2)}, u32[]{:S(2)}) collective-permute-start(bf16[128,256]{1,0:T(8,128)(2,1)S(1)} %pad_maximum_fusion.2), channel_id=1, source_target_pairs={{0,5},{1,4},{2,7},{3,6},{4,1},{5,0},{6,3},{7,2},{8,13},{9,12},{10,... | collective-permute-start | bytes 196616 | tf_op jit(solution)/shard_map/ppermute | solution.py:28
  12.3 1.6 %collective-permute-done.6 = bf16[32,128]{1,0:T(8,128)(2,1)S(1)} collective-permute-done((bf16[32,128]{1,0:T(8,128)(2,1)S(1)}, bf16[32,128]{1,0:T(8,128)(2,1)S(1)}, u32[]{:S(2)}, u32[]{:S(2)}) %collective-permute-start.6) | collective-permute-done | bytes 8224 | tf_op jit(solution)/shard_map/ppermute | solution.py:28
  13.9 1.2 %collective-permute-start.7 = (bf16[64,128]{1,0:T(8,128)(2,1)S(1)}, bf16[64,128]{1,0:T(8,128)(2,1)S(1)}, u32[]{:S(2)}, u32[]{:S(2)}) collective-permute-start(bf16[64,128]{1,0:T(8,128)(2,1)S(1)} %pad_maximum_fusion.5), channel_id=1, source_target_pairs={{0,5},{1,4},{2,7},{3,6},{4,1},{5,0},{6,3},{7,2},{8,13},{9,12},{10,... | collective-permute-start | bytes 49160 | tf_op jit(solution)/shard_map/ppermute | solution.py:28
  15.1 0.0 collective-permute-done.3
  15.1 1.6 %collective-permute-start.4 = (bf16[256,256]{1,0:T(8,128)(2,1)S(1)}, bf16[256,256]{1,0:T(8,128)(2,1)S(1)}, u32[]{:S(2)}, u32[]{:S(2)}) collective-permute-start(bf16[256,256]{1,0:T(8,128)(2,1)S(1)} %pad_maximum_fusion.1), channel_id=1, source_target_pairs={{0,9},{1,8},{2,11},{3,10},{4,13},{5,12},{6,15},{7,14},{8,1},{9,0},... | collective-permute-start | bytes 393224 | tf_op jit(solution)/shard_map/ppermute | solution.py:28
  16.8 0.0 copy-start
  16.8 0.3 %collective-permute-done.7 = bf16[64,128]{1,0:T(8,128)(2,1)S(1)} collective-permute-done((bf16[64,128]{1,0:T(8,128)(2,1)S(1)}, bf16[64,128]{1,0:T(8,128)(2,1)S(1)}, u32[]{:S(2)}, u32[]{:S(2)}) %collective-permute-start.7) | collective-permute-done | bytes 16416 | tf_op jit(solution)/shard_map/ppermute | solution.py:28
  17.1 1.3 %collective-permute-start.8 = (bf16[128,128]{1,0:T(8,128)(2,1)S(1)}, bf16[128,128]{1,0:T(8,128)(2,1)S(1)}, u32[]{:S(2)}, u32[]{:S(2)}) collective-permute-start(bf16[128,128]{1,0:T(8,128)(2,1)S(1)} %pad_maximum_fusion.4), channel_id=1, source_target_pairs={{0,9},{1,8},{2,11},{3,10},{4,13},{5,12},{6,15},{7,14},{8,1},{9,0},... | collective-permute-start | bytes 98312 | tf_op jit(solution)/shard_map/ppermute | solution.py:28
  18.4 2.2 %collective-permute-done.4 = bf16[256,256]{1,0:T(8,128)(2,1)S(1)} collective-permute-done((bf16[256,256]{1,0:T(8,128)(2,1)S(1)}, bf16[256,256]{1,0:T(8,128)(2,1)S(1)}, u32[]{:S(2)}, u32[]{:S(2)}) %collective-permute-start.4) | collective-permute-done | bytes 131104 | tf_op jit(solution)/shard_map/ppermute | solution.py:28
  20.6 0.7 %collective-permute-start.5 = (bf16[512,256]{1,0:T(8,128)(2,1)S(1)}, bf16[512,256]{1,0:T(8,128)(2,1)S(1)}, u32[]{:S(2)}, u32[]{:S(2)}) collective-permute-start(bf16[512,256]{1,0:T(8,128)(2,1)S(1)} %pad_maximum_fusion), channel_id=1, source_target_pairs={{0,1},{1,0},{2,3},{3,2},{4,5},{5,4},{6,7},{7,6},{8,9},{9,8},{10,11... | collective-permute-start | bytes 786440 | tf_op jit(solution)/shard_map/ppermute | solution.py:28
  21.4 0.0 collective-permute-done.8
  21.4 1.1 %collective-permute-done.5 = bf16[512,256]{1,0:T(8,128)(2,1)S(1)} collective-permute-done((bf16[512,256]{1,0:T(8,128)(2,1)S(1)}, bf16[512,256]{1,0:T(8,128)(2,1)S(1)}, u32[]{:S(2)}, u32[]{:S(2)}) %collective-permute-start.5) | collective-permute-done | bytes 262176 | tf_op jit(solution)/shard_map/ppermute | solution.py:28
  22.5 0.0 copy-done.1
  22.5 0.0 copy-done.2
  22.6 0.0 copy-done.3
  22.6 1.7 %shard_map.96 = (bf16[768,1024]{1,0:T(8,128)(2,1)S(1)}, f32[6,128]{1,0:T(8,128)S(1)}) custom-call(s32[16]{0:T(128)S(1)} %copy-done.3, bf16[128,768]{1,0:T(8,128)(2,1)S(1)} %copy-done.1, bf16[64,128]{1,0:T(8,128)(2,1)S(1)} %add_convert_fusion.low_ref, bf16[32,768]{1,0:T(8,128)(2,1)S(1)} %copy-done.2, ...), custom_call_target="tpu_custom_call" | custom-call | flops 201326592 | bytes 1572864 | tf_op jit(solution)/shard_map/pallas_call | solution.py:181
  24.3 0.0 copy-done
  24.3 1.5 %shard_map.97 = (bf16[128,768]{1,0:T(8,128)(2,1)}, f32[6,128]{1,0:T(8,128)}) custom-call(bf16[768,1024]{1,0:T(8,128)(2,1)S(1)} %get-tuple-element.8.weights_ref, f32[6,128]{1,0:T(8,128)S(1)} %get-tuple-element.9.top_ref, bf16[1024,256]{1,0:T(8,128)(2,1)S(1)} %constant_dynamic-update-slice_fusion.kv_ref, ...), custom_call_target="tpu_custom_call" | custom-call | flops 201326592 | bytes 1572864 | tf_op jit(solution)/shard_map/pallas_call | solution.py:245
  (14 shorter events, 0.1 us)
Async XLA Ops:
  0.6 21.9 %copy-start.1 = (bf16[128,768]{1,0:T(8,128)(2,1)S(1)}, bf16[128,768]{1,0:T(8,128)(2,1)}, u32[]{:S(2)}) copy-start(bf16[128,768]{1,0:T(8,128)(2,1)} %frozen_query_ref.1) | copy-start | bytes 589828
  0.6 21.9 %copy-start.2 = (bf16[32,768]{1,0:T(8,128)(2,1)S(1)}, bf16[32,768]{1,0:T(8,128)(2,1)}, u32[]{:S(2)}) copy-start(bf16[32,768]{1,0:T(8,128)(2,1)} %query_up_ref.1) | copy-start | bytes 147460
  0.7 21.9 %copy-start.3 = (s32[16]{0:T(128)S(1)}, s32[16]{0:T(128)}, u32[]{:S(2)}) copy-start(s32[16]{0:T(128)} %order_ref.1) | copy-start | bytes 196
  2.4 4.2 %collective-permute-start = (bf16[64,128]{1,0:T(8,128)(2,1)S(1)}, bf16[64,128]{1,0:T(8,128)(2,1)S(1)}, u32[]{:S(2)}, u32[]{:S(2)}) collective-permute-start(bf16[64,128]{1,0:T(8,128)(2,1)S(1)} %get-tuple-element.6), channel_id=1, source_target_pairs={{0,1},{1,0},{2,3},{3,2},{4,5},{5,4},{6,7},{7,6},{8,9},{9,8},{10,11... | collective-permute-start | bytes 49160 | tf_op jit(solution)/shard_map/ppermute | solution.py:28
  2.9 7.9 %collective-permute-start.2 = (bf16[64,256]{1,0:T(8,128)(2,1)S(1)}, bf16[64,256]{1,0:T(8,128)(2,1)S(1)}, u32[]{:S(2)}, u32[]{:S(2)}) collective-permute-start(bf16[64,256]{1,0:T(8,128)(2,1)S(1)} %get-tuple-element.7), channel_id=1, source_target_pairs={{0,17},{1,16},{2,19},{3,18},{4,21},{5,20},{6,23},{7,22},{8,25},{9,... | collective-permute-start | bytes 98312 | tf_op jit(solution)/shard_map/ppermute | solution.py:28
  6.6 3.2 %collective-permute-start.1 = (bf16[64,128]{1,0:T(8,128)(2,1)S(1)}, bf16[64,128]{1,0:T(8,128)(2,1)S(1)}, u32[]{:S(2)}, u32[]{:S(2)}) collective-permute-start(bf16[64,128]{1,0:T(8,128)(2,1)S(1)} %add_convert_fusion.1), channel_id=1, source_target_pairs={{0,3},{1,2},{2,1},{3,0},{4,7},{5,6},{6,5},{7,4},{8,11},{9,10},{10,... | collective-permute-start | bytes 49160 | tf_op jit(solution)/shard_map/ppermute | solution.py:28
  9.9 4.0 %collective-permute-start.6 = (bf16[32,128]{1,0:T(8,128)(2,1)S(1)}, bf16[32,128]{1,0:T(8,128)(2,1)S(1)}, u32[]{:S(2)}, u32[]{:S(2)}) collective-permute-start(bf16[32,128]{1,0:T(8,128)(2,1)S(1)} %slice.4), channel_id=1, source_target_pairs={{0,17},{1,16},{2,19},{3,18},{4,21},{5,20},{6,23},{7,22},{8,25},{9,... | collective-permute-start | bytes 24584 | tf_op jit(solution)/shard_map/ppermute | solution.py:28
  10.8 4.4 %collective-permute-start.3 = (bf16[128,256]{1,0:T(8,128)(2,1)S(1)}, bf16[128,256]{1,0:T(8,128)(2,1)S(1)}, u32[]{:S(2)}, u32[]{:S(2)}) collective-permute-start(bf16[128,256]{1,0:T(8,128)(2,1)S(1)} %pad_maximum_fusion.2), channel_id=1, source_target_pairs={{0,5},{1,4},{2,7},{3,6},{4,1},{5,0},{6,3},{7,2},{8,13},{9,12},{10,... | collective-permute-start | bytes 196616 | tf_op jit(solution)/shard_map/ppermute | solution.py:28
  13.9 3.2 %collective-permute-start.7 = (bf16[64,128]{1,0:T(8,128)(2,1)S(1)}, bf16[64,128]{1,0:T(8,128)(2,1)S(1)}, u32[]{:S(2)}, u32[]{:S(2)}) collective-permute-start(bf16[64,128]{1,0:T(8,128)(2,1)S(1)} %pad_maximum_fusion.5), channel_id=1, source_target_pairs={{0,5},{1,4},{2,7},{3,6},{4,1},{5,0},{6,3},{7,2},{8,13},{9,12},{10,... | collective-permute-start | bytes 49160 | tf_op jit(solution)/shard_map/ppermute | solution.py:28
  15.1 5.4 %collective-permute-start.4 = (bf16[256,256]{1,0:T(8,128)(2,1)S(1)}, bf16[256,256]{1,0:T(8,128)(2,1)S(1)}, u32[]{:S(2)}, u32[]{:S(2)}) collective-permute-start(bf16[256,256]{1,0:T(8,128)(2,1)S(1)} %pad_maximum_fusion.1), channel_id=1, source_target_pairs={{0,9},{1,8},{2,11},{3,10},{4,13},{5,12},{6,15},{7,14},{8,1},{9,0},... | collective-permute-start | bytes 393224 | tf_op jit(solution)/shard_map/ppermute | solution.py:28
  16.8 7.5 %copy-start = (bf16[32,256]{1,0:T(8,128)(2,1)S(1)}, bf16[32,256]{1,0:T(8,128)(2,1)}, u32[]{:S(2)}) copy-start(bf16[32,256]{1,0:T(8,128)(2,1)} %value_up_ref.1) | copy-start | bytes 49156
  17.1 4.3 %collective-permute-start.8 = (bf16[128,128]{1,0:T(8,128)(2,1)S(1)}, bf16[128,128]{1,0:T(8,128)(2,1)S(1)}, u32[]{:S(2)}, u32[]{:S(2)}) collective-permute-start(bf16[128,128]{1,0:T(8,128)(2,1)S(1)} %pad_maximum_fusion.4), channel_id=1, source_target_pairs={{0,9},{1,8},{2,11},{3,10},{4,13},{5,12},{6,15},{7,14},{8,1},{9,0},... | collective-permute-start | bytes 98312 | tf_op jit(solution)/shard_map/ppermute | solution.py:28
  20.6 1.9 %collective-permute-start.5 = (bf16[512,256]{1,0:T(8,128)(2,1)S(1)}, bf16[512,256]{1,0:T(8,128)(2,1)S(1)}, u32[]{:S(2)}, u32[]{:S(2)}) collective-permute-start(bf16[512,256]{1,0:T(8,128)(2,1)S(1)} %pad_maximum_fusion), channel_id=1, source_target_pairs={{0,1},{1,0},{2,3},{3,2},{4,5},{5,4},{6,7},{7,6},{8,9},{9,8},{10,11... | collective-permute-start | bytes 786440 | tf_op jit(solution)/shard_map/ppermute | solution.py:28

commit v4 on v3

v4 whole, which is shorter than its diff:
```python
import functools
import math

import jax
import jax.numpy as jnp
from jax import lax
from jax.experimental import pallas as pl
from jax.experimental.pallas import tpu as pltpu
from jax.sharding import PartitionSpec as P

HEAD_SIZE = 128
KEY_VALUE_HEADS = 2
ADAPTER_RANK = 32
ADAPTER_SCALE = 0.5
MASKED = -1e30
AXES = ("ctx", "head")
SCORE_FACTOR = math.log2(math.e) / math.sqrt(HEAD_SIZE)
VMEM_LIMIT = 24 * 1024 * 1024


def exchange(value, ctx_bit, head_bits):
    ctx_count, head_count = lax.axis_size("ctx"), lax.axis_size("head")
    pairs = [
        (i * head_count + h, (i ^ ctx_bit) * head_count + (h ^ head_bits))
        for i in range(ctx_count)
        for h in range(head_count)
    ]
    return lax.ppermute(value, AXES, pairs)


def gather_patterns(bits):
    patterns = [0]
    for bit in bits:
        patterns += [p ^ bit for p in patterns]
    return patterns


def half_blocks(patterns, ctx, side):
    blocks = len(patterns)
    found = []
    for entry in range(2 * blocks):
        pattern = patterns[entry % blocks]
        half = (side + pattern.bit_count() + entry // blocks) % 2
        found.append((entry % blocks, half, 2 * (ctx ^ pattern) + half))
    return found


def prologue_kernel(
    patterns,
    hidden_hbm,
    down_hbm,
    key_hbm,
    value_hbm,
    order_hbm,
    frozen_query_hbm,
    query_up_hbm,
    value_up_hbm,
    low_ref,
    kv_ref,
    bias_ref,
    frozen_query_ref,
    query_up_ref,
    value_up_ref,
    hidden_ref,
    down_ref,
    order_ref,
    sems,
    other_sems,
):
    ctx, head = lax.axis_index("ctx"), lax.axis_index("head")
    side = head % 2
    group = head // (lax.axis_size("head") // KEY_VALUE_HEADS)
    tok_dev = hidden_hbm.shape[0]
    span = tok_dev // 2
    rows = pl.ds(pl.multiple_of(side * span, span), span)
    columns = pl.ds(pl.multiple_of(group * HEAD_SIZE, HEAD_SIZE), HEAD_SIZE)
    chunks = sems.shape[0]
    depth = down_hbm.shape[1] // chunks
    copies = []
    for chunk in range(chunks):
        part = pl.ds(chunk * depth, depth)
        pair = (
            pltpu.make_async_copy(hidden_hbm.at[:, part], hidden_ref.at[:, part], sems.at[chunk, 0]),
            pltpu.make_async_copy(down_hbm.at[:, part], down_ref.at[:, part], sems.at[chunk, 1]),
        )
        for copy in pair:
            copy.start()
        copies.append(pair)
    others = [
        pltpu.make_async_copy(*refs, other_sems.at[n])
        for n, refs in enumerate(
            (
                (order_hbm, order_ref),
                (key_hbm.at[rows, columns], kv_ref.at[:, pl.ds(0, HEAD_SIZE)]),
                (value_hbm.at[rows, columns], kv_ref.at[:, pl.ds(HEAD_SIZE, HEAD_SIZE)]),
                (frozen_query_hbm, frozen_query_ref),
                (query_up_hbm, query_up_ref),
                (value_up_hbm.at[:, columns], value_up_ref),
            )
        )
    ]
    for copy in others:
        copy.start()
    others[0].wait()
    row = lax.broadcasted_iota(jnp.int32, (tok_dev, tok_dev), 0)
    lane = lax.broadcasted_iota(jnp.int32, (tok_dev, tok_dev), 1)
    first_row, first_lane = row < span, lane < span
    inner = row % span - lane % span
    query_spans = jnp.where(first_row, order_ref[2 * ctx], order_ref[2 * ctx + 1])
    entries = half_blocks(patterns, ctx, side)
    for tile in range(len(patterns)):
        first, second = order_ref[entries[2 * tile][2]], order_ref[entries[2 * tile + 1][2]]
        ahead = jnp.where(first_lane, first, second) - query_spans
        bias_ref[:, tile * tok_dev : (tile + 1) * tok_dev] = jnp.where(
            ahead * span <= inner, 0.0, MASKED
        )
    total = jnp.zeros(low_ref.shape, jnp.float32)
    for chunk in range(chunks):
        for copy in copies[chunk]:
            copy.wait()
        part = slice(chunk * depth, (chunk + 1) * depth)
        total += lax.dot_general(
            down_ref[:, part],
            hidden_ref[:, part],
            (((1,), (1,)), ((), ())),
            preferred_element_type=jnp.float32,
        )
    low_ref[...] = total.astype(jnp.bfloat16)
    for copy in others[1:]:
        copy.wait()


def prologue(patterns, hidden, down, keys, values, order, frozen_query, query_up, value_up):
    tok_dev, depth = hidden.shape
    rank = down.shape[0]
    chunks = 4
    hbm = pl.BlockSpec(memory_space=pltpu.HBM)
    vmem = pl.BlockSpec(memory_space=pltpu.VMEM)
    operands = (hidden, down, keys, values, order, frozen_query, query_up, value_up)
    return pl.pallas_call(
        functools.partial(prologue_kernel, patterns),
        out_shape=(
            jax.ShapeDtypeStruct((rank, tok_dev), jnp.bfloat16),
            jax.ShapeDtypeStruct((tok_dev // 2, 2 * HEAD_SIZE), jnp.bfloat16),
            jax.ShapeDtypeStruct((tok_dev, tok_dev * len(patterns)), jnp.float32),
            jax.ShapeDtypeStruct(frozen_query.shape, jnp.bfloat16),
            jax.ShapeDtypeStruct(query_up.shape, jnp.bfloat16),
            jax.ShapeDtypeStruct((value_up.shape[0], HEAD_SIZE), jnp.bfloat16),
        ),
        in_specs=[hbm] * len(operands),
        out_specs=(vmem,) * 6,
        scratch_shapes=[
            pltpu.VMEM(hidden.shape, jnp.bfloat16),
            pltpu.VMEM(down.shape, jnp.bfloat16),
            pltpu.SMEM(order.shape, jnp.int32),
            pltpu.SemaphoreType.DMA((chunks, 2)),
            pltpu.SemaphoreType.DMA((6,)),
        ],
        compiler_params=pltpu.CompilerParams(vmem_limit_bytes=VMEM_LIMIT),
        cost_estimate=pl.CostEstimate(
            flops=2 * tok_dev * depth * rank, bytes_accessed=tok_dev * depth * 4, transcendentals=0
        ),
    )(*(pltpu.with_memory_space_constraint(x, pltpu.HBM) for x in operands))


def queries_kernel(frozen_query_ref, low_ref, query_up_ref, queries_ref):
    queries_ref[...] = (
        frozen_query_ref[...].astype(jnp.float32)
        + ADAPTER_SCALE
        * lax.dot_general(
            low_ref[:ADAPTER_RANK, :],
            query_up_ref[...],
            (((0,), (0,)), ((), ())),
            preferred_element_type=jnp.float32,
        )
    ).astype(jnp.bfloat16)


def adapt_queries(frozen_query, low, query_up):
    tok_dev, width = frozen_query.shape
    vmem = pl.BlockSpec(memory_space=pltpu.VMEM)
    return pl.pallas_call(
        queries_kernel,
        out_shape=jax.ShapeDtypeStruct((tok_dev, width), jnp.bfloat16),
        in_specs=[vmem] * 3,
        out_specs=vmem,
        compiler_params=pltpu.CompilerParams(vmem_limit_bytes=VMEM_LIMIT),
        cost_estimate=pl.CostEstimate(
            flops=2 * tok_dev * width * ADAPTER_RANK,
            bytes_accessed=4 * tok_dev * width,
            transcendentals=0,
        ),
    )(frozen_query, low, query_up)


def weights_kernel(queries_ref, bias_ref, kv_ref, other_kv_ref, weights_ref, top_ref):
    tok_dev, width = queries_ref.shape
    half = kv_ref.shape[0]
    for head in range(width // HEAD_SIZE):
        columns = slice(head * HEAD_SIZE, (head + 1) * HEAD_SIZE)
        rows = slice(head * tok_dev, (head + 1) * tok_dev)
        scores = [
            lax.dot_general(
                queries_ref[:, columns],
                ref[:, :HEAD_SIZE],
                (((1,), (1,)), ((), ())),
                preferred_element_type=jnp.float32,
            )
            * SCORE_FACTOR
            + bias_ref[:, n * half : (n + 1) * half]
            for n, ref in enumerate((kv_ref, other_kv_ref))
        ]
        top = jnp.maximum(
            jnp.max(scores[0], axis=1, keepdims=True), jnp.max(scores[1], axis=1, keepdims=True)
        )
        for n in range(2):
            weights_ref[rows, n * half : (n + 1) * half] = jnp.exp2(scores[n] - top).astype(
                jnp.bfloat16
            )
        top_ref[:, columns] = jnp.broadcast_to(top, (tok_dev, HEAD_SIZE))


def make_weights(queries, bias, kv, other_kv):
    tok_dev, width = queries.shape
    heads = width // HEAD_SIZE
    key_count = 2 * kv.shape[0]
    vmem = pl.BlockSpec(memory_space=pltpu.VMEM)
    return pl.pallas_call(
        weights_kernel,
        out_shape=(
            jax.ShapeDtypeStruct((heads * tok_dev, key_count), jnp.bfloat16),
            jax.ShapeDtypeStruct((tok_dev, width), jnp.float32),
        ),
        in_specs=[vmem] * 4,
        out_specs=(vmem, vmem),
        compiler_params=pltpu.CompilerParams(vmem_limit_bytes=VMEM_LIMIT),
        cost_estimate=pl.CostEstimate(
            flops=2 * tok_dev * width * key_count,
            bytes_accessed=2 * tok_dev * heads * key_count,
            transcendentals=heads * tok_dev * key_count,
        ),
    )(queries, bias, kv, other_kv)


def values_kernel(
    patterns,
    weights_ref,
    top_ref,
    kv_ref,
    other_kv_ref,
    low_value_ref,
    value_up_ref,
    attended_ref,
    normalizer_ref,
    value_ref,
):
    tok_dev, width = top_ref.shape
    span = tok_dev // 2
    blocks = len(patterns)
    half_count = blocks * span
    heads = width // HEAD_SIZE
    ctx, side = lax.axis_index("ctx"), lax.axis_index("head") % 2
    entries = half_blocks(patterns, ctx, side)
    value_ref[:, HEAD_SIZE:] = jnp.ones((2 * half_count, HEAD_SIZE), jnp.bfloat16)
    for block in range(blocks):
        update = ADAPTER_SCALE * lax.dot_general(
            low_value_ref[block * ADAPTER_RANK : (block + 1) * ADAPTER_RANK, :],
            value_up_ref[...],
            (((0,), (0,)), ((), ())),
            preferred_element_type=jnp.float32,
        )
        low_half = entries[block][1] == 0
        parts = (
            jnp.where(low_half, update[:span], update[span:]),
            jnp.where(low_half, update[span:], update[:span]),
        )
        here = slice(block * span, (block + 1) * span)
        for n, ref in enumerate((kv_ref, other_kv_ref)):
            value_ref[n * half_count + block * span : n * half_count + (block + 1) * span, :HEAD_SIZE] = (
                ref[here, HEAD_SIZE:].astype(jnp.float32) + parts[n]
            ).astype(jnp.bfloat16)
    row = lax.broadcasted_iota(jnp.int32, (tok_dev, tok_dev), 0)
    lane = lax.broadcasted_iota(jnp.int32, (tok_dev, tok_dev), 1)
    for head in range(heads):
        columns = slice(head * HEAD_SIZE, (head + 1) * HEAD_SIZE)
        sums = jnp.dot(
            weights_ref[head * tok_dev : (head + 1) * tok_dev, :],
            value_ref[...],
            preferred_element_type=jnp.float32,
        )
        total = sums[:, HEAD_SIZE:]
        attended_ref[:, columns] = (sums[:, :HEAD_SIZE] / total).astype(jnp.bfloat16)
        normalizer_ref[head : head + 1, :] = jnp.sum(
            jnp.where(row == lane, top_ref[:, columns] * math.log(2.0) + jnp.log(total), 0.0),
            axis=0,
            keepdims=True,
        )


def weigh_values(patterns, weights, top, kv, other_kv, low_value, value_up):
    tok_dev, width = top.shape
    heads = width // HEAD_SIZE
    key_count = 2 * kv.shape[0]
    vmem = pl.BlockSpec(memory_space=pltpu.VMEM)
    return pl.pallas_call(
        functools.partial(values_kernel, patterns),
        out_shape=(
            jax.ShapeDtypeStruct((tok_dev, width), jnp.bfloat16),
            jax.ShapeDtypeStruct((heads, tok_dev), jnp.float32),
        ),
        in_specs=[vmem] * 6,
        out_specs=(vmem, vmem),
        scratch_shapes=[
            pltpu.VMEM((key_count, 2 * HEAD_SIZE), jnp.bfloat16),
        ],
        compiler_params=pltpu.CompilerParams(vmem_limit_bytes=VMEM_LIMIT),
        cost_estimate=pl.CostEstimate(
            flops=4 * tok_dev * width * key_count,
            bytes_accessed=4 * tok_dev * heads * key_count,
            transcendentals=0,
        ),
    )(weights, top, kv, other_kv, low_value, value_up)


def attend_long(patterns, ctx, head, order, frozen_query, low, query_up, kv, low_value, value_up):
    tok_dev, width = frozen_query.shape
    span = tok_dev // 2
    heads = width // HEAD_SIZE
    blocks = len(patterns)
    side = head % 2
    group = head // (lax.axis_size("head") // KEY_VALUE_HEADS)
    value_up = lax.dynamic_slice_in_dim(value_up, group * HEAD_SIZE, HEAD_SIZE, 1)
    low = low.T
    low_value = low_value.reshape(blocks, ADAPTER_RANK, tok_dev).transpose(0, 2, 1)
    queries = (
        frozen_query.astype(jnp.float32)
        + ADAPTER_SCALE
        * jnp.dot(low[:, :ADAPTER_RANK], query_up, preferred_element_type=jnp.float32)
    ).astype(jnp.bfloat16)
    queries = queries.reshape(tok_dev, heads, HEAD_SIZE).transpose(1, 0, 2).reshape(-1, HEAD_SIZE)
    pattern = jnp.tile(jnp.array(patterns, jnp.int32), 2)
    parity = jnp.array([p.bit_count() for p in patterns] + [p.bit_count() + 1 for p in patterns])
    half = (side + parity.astype(jnp.int32)) % 2
    key_spans = order[2 * (ctx ^ pattern) + half]
    inner = jnp.arange(span, dtype=jnp.int32)
    key_pos = (key_spans[:, None] * span + inner).reshape(-1)
    query_spans = lax.dynamic_slice_in_dim(order, 2 * ctx, 2)
    query_pos = jnp.tile((query_spans[:, None] * span + inner).reshape(-1), heads)
    index = jnp.tile(jnp.arange(blocks, dtype=jnp.int32), 2)
    low_rows = low_value.reshape(2 * blocks, span, ADAPTER_RANK)[2 * index + half]
    values = (
        kv[:, HEAD_SIZE:].astype(jnp.float32)
        + ADAPTER_SCALE
        * jnp.dot(
            low_rows.reshape(-1, ADAPTER_RANK), value_up, preferred_element_type=jnp.float32
        )
    ).astype(jnp.bfloat16)
    chunk = math.gcd(kv.shape[0], 1024)

    def step(number, state):
        top, total, summed = state
        at = number * chunk
        keys = lax.dynamic_slice_in_dim(kv, at, chunk, 0)[:, :HEAD_SIZE]
        scores = lax.dot_general(
            queries, keys, (((1,), (1,)), ((), ())), preferred_element_type=jnp.float32
        ) * (1.0 / math.sqrt(HEAD_SIZE))
        visible = lax.dynamic_slice_in_dim(key_pos, at, chunk)[None, :] <= query_pos[:, None]
        new_top = jnp.maximum(top, jnp.max(jnp.where(visible, scores, MASKED), axis=1))
        scale = jnp.exp(top - new_top)
        weights = jnp.where(visible, jnp.exp(scores - new_top[:, None]), 0.0)
        summed = summed * scale[:, None] + jnp.dot(
            weights.astype(jnp.bfloat16),
            lax.dynamic_slice_in_dim(values, at, chunk, 0),
            preferred_element_type=jnp.float32,
        )
        return (new_top, total * scale + jnp.sum(weights, axis=1), summed)

    rows = heads * tok_dev
    top, total, summed = lax.fori_loop(
        0,
        kv.shape[0] // chunk,
        step,
        (
            jnp.full((rows,), MASKED, jnp.float32),
            jnp.zeros((rows,), jnp.float32),
            jnp.zeros((rows, HEAD_SIZE), jnp.float32),
        ),
    )
    attended = (summed / total[:, None]).astype(jnp.bfloat16)
    attended = attended.reshape(heads, tok_dev, HEAD_SIZE).transpose(1, 0, 2)
    return attended.reshape(tok_dev, width), (top + jnp.log(total)).reshape(heads, tok_dev)


def local(
    hidden,
    frozen_query_rows,
    frozen_key_rows,
    frozen_value_rows,
    adapter_down_factors,
    query_up_factor,
    value_up_factor,
    slot_span_order,
):
    ctx_count, head_count = lax.axis_size("ctx"), lax.axis_size("head")
    ctx, head = lax.axis_index("ctx"), lax.axis_index("head")
    bits = [ctx_count >> k for k in range(1, ctx_count.bit_length())]
    if len(bits) == 3:
        bits = [bits[0], bits[2], bits[1]]
    patterns = gather_patterns(bits)

    low, kv, bias, frozen_query, query_up, value_up = prologue(
        patterns,
        hidden,
        adapter_down_factors.T,
        frozen_key_rows,
        frozen_value_rows,
        slot_span_order,
        frozen_query_rows,
        query_up_factor,
        value_up_factor,
    )
    head_bit = 1
    while head_bit < head_count:
        other = exchange(low, 0, head_bit | 1)
        low = (low.astype(jnp.float32) + other.astype(jnp.float32)).astype(jnp.bfloat16)
        head_bit *= 2
    low_value = low[ADAPTER_RANK:]
    short = hidden.shape[0] * ctx_count <= 1024
    if short:
        queries = adapt_queries(frozen_query, low, query_up)
    for bit in bits:
        if short and bit == bits[-1]:
            kv, _ = lax.optimization_barrier((kv, queries))
        low_value = jnp.concatenate([low_value, exchange(low_value, bit, 1)], axis=0)
        kv = jnp.concatenate([kv, exchange(kv, bit, 1)], axis=0)
    other_kv = exchange(kv, 0, 1)
    if not short:
        return attend_long(
            patterns,
            ctx,
            head,
            slot_span_order,
            frozen_query_rows,
            low,
            query_up_factor,
            jnp.concatenate([kv, other_kv], axis=0),
            low_value,
            value_up_factor,
        )
    weights, top = make_weights(queries, bias, kv, other_kv)
    return weigh_values(patterns, weights, top, kv, other_kv, low_value, value_up)


def solution(mesh):
    placed = (
        P("ctx", "head"),
        P("ctx", "head"),
        P("ctx", None),
        P("ctx", None),
        P("head", None),
        P(None, "head"),
        P(),
        P(),
    )
    return jax.shard_map(
        local,
        mesh=mesh,
        in_specs=placed,
        out_specs=(P("ctx", "head"), P("head", "ctx")),
        check_vma=False,
    )
```

time: 26 us -> 24.6 us (0.946)
  waiting for transfers between devices: 7.23 us -> 4.86 us
  starting transfers between devices: 12.8 us -> 14.5 us
  Pallas kernels: 4.94 us -> 4.34 us
    ppermute x9, waiting for transfers between devices: 7.23 us -> 4.86 us  [exchange(): return lax.ppermute(value, AXES, pairs)]
    ppermute x9, starting transfers between devices: 12.8 us -> 14.5 us  [exchange(): return lax.ppermute(value, AXES, pairs)]
    pallas_call x2 -> x3, Pallas kernels: 3.41 us -> 2.82 us  [the longest x1 1.7 us: prologue(): pl.pallas_call(functools.partial(prologue_kernel, patterns), out_shape=(j...]
  transfers between devices with their start and end apart: 9 -> 9, of which waited for: 5 -> 4; matrix products, arithmetic and copies ran while one was open for 0% -> 0% of each run, Pallas kernels for 0% -> 1%
where the time goes in v4:
time: 24.6 us; the launch traced here: 24.5 us
  starting transfers between devices  14.5 us (59%)
  waiting for transfers between devices  4.86 us (20%)
  Pallas kernels  4.34 us (18%)
  between operations  0.71 us (3%)
    ppermute x9, starting transfers between devices, exchange(): return lax.ppermute(value, AXES, pairs)  14.5 us
    ppermute x9, waiting for transfers between devices, exchange(): return lax.ppermute(value, AXES, pairs)  4.86 us
    pallas_call x1, Pallas kernels, prologue(): pl.pallas_call(functools.partial(prologue_kernel, patterns), out_shape=(j...  1.7 us
    pallas_call x1, Pallas kernels, weigh_values(): pl.pallas_call(functools.partial(values_kernel, patterns), out_shape=(jax...  1.53 us
    pallas_call x1, Pallas kernels, make_weights(): pl.pallas_call(weights_kernel, out_shape=(jax.ShapeDtypeStruct((heads * t...  0.88 us
  transfers between devices with their start and end apart: 9, of which 4 were waited for; matrix products, arithmetic and copies ran while one was open for 0% of the time, Pallas kernels for 1%

profile of v4, /device:TPU:0, one launch (start us, length us, event | category | flops | bytes accessed | tf_op | source)
XLA Modules:
  0.0 24.5 jit_solution(2767855423672965185)
XLA Ops:
  0.6 1.7 %shard_map.95 = (bf16[64,128]{1,0:T(8,128)(2,1)S(1)}, bf16[64,256]{1,0:T(8,128)(2,1)S(1)}, f32[128,1024]{1,0:T(8,128)S(1)}, bf16[128,768]{1,0:T(8,128)(2,1)S(1)}...) custom-call(bf16[128,2048]{1,0:T(8,128)(2,1)} %hidden_hbm.1, bf16[64,2048]{1,0:T(8,128)(2,1)} %bitcast.1, ...), custom_call_target="tpu_custom_call" | custom-call | flops 33554432 | bytes 1048576 | tf_op jit(solution)/shard_map/pallas_call | solution.py:140
  2.3 0.5 %collective-permute-start = (bf16[64,128]{1,0:T(8,128)(2,1)S(1)}, bf16[64,128]{1,0:T(8,128)(2,1)S(1)}, u32[]{:S(2)}, u32[]{:S(2)}) collective-permute-start(bf16[64,128]{1,0:T(8,128)(2,1)S(1)} %get-tuple-element.12), channel_id=1, source_target_pairs={{0,1},{1,0},{2,3},{3,2},{4,5},{5,4},{6,7},{7,6},{8,9},{9,8},{10,11... | collective-permute-start | bytes 49160 | tf_op jit(solution)/shard_map/ppermute | solution.py:28
  2.9 3.7 %collective-permute-start.2 = (bf16[64,256]{1,0:T(8,128)(2,1)S(1)}, bf16[64,256]{1,0:T(8,128)(2,1)S(1)}, u32[]{:S(2)}, u32[]{:S(2)}) collective-permute-start(bf16[64,256]{1,0:T(8,128)(2,1)S(1)} %get-tuple-element.15), channel_id=1, source_target_pairs={{0,17},{1,16},{2,19},{3,18},{4,21},{5,20},{6,23},{7,22},{8,25},{9,... | collective-permute-start | bytes 98312 | tf_op jit(solution)/shard_map/ppermute | solution.py:28
  6.6 0.0 collective-permute-done
  6.6 1.3 %collective-permute-start.1 = (bf16[64,128]{1,0:T(8,128)(2,1)S(1)}, bf16[64,128]{1,0:T(8,128)(2,1)S(1)}, u32[]{:S(2)}, u32[]{:S(2)}) collective-permute-start(bf16[64,128]{1,0:T(8,128)(2,1)S(1)} %add_convert_fusion.1), channel_id=1, source_target_pairs={{0,3},{1,2},{2,1},{3,0},{4,7},{5,6},{6,5},{7,4},{8,11},{9,10},{10,... | collective-permute-start | bytes 49160 | tf_op jit(solution)/shard_map/ppermute | solution.py:28
  7.8 0.4 %collective-permute-done.2 = bf16[64,256]{1,0:T(8,128)(2,1)S(1)} collective-permute-done((bf16[64,256]{1,0:T(8,128)(2,1)S(1)}, bf16[64,256]{1,0:T(8,128)(2,1)S(1)}, u32[]{:S(2)}, u32[]{:S(2)}) %collective-permute-start.2) | collective-permute-done | bytes 32800 | tf_op jit(solution)/shard_map/ppermute | solution.py:28
  8.2 1.5 %collective-permute-start.3 = (bf16[128,256]{1,0:T(8,128)(2,1)S(1)}, bf16[128,256]{1,0:T(8,128)(2,1)S(1)}, u32[]{:S(2)}, u32[]{:S(2)}) collective-permute-start(bf16[128,256]{1,0:T(8,128)(2,1)S(1)} %pad_maximum_fusion.1), channel_id=1, source_target_pairs={{0,5},{1,4},{2,7},{3,6},{4,1},{5,0},{6,3},{7,2},{8,13},{9,12},{10,... | collective-permute-start | bytes 196616 | tf_op jit(solution)/shard_map/ppermute | solution.py:28
  9.7 0.1 collective-permute-done.1
  9.8 2.2 %collective-permute-start.6 = (bf16[32,128]{1,0:T(8,128)(2,1)S(1)}, bf16[32,128]{1,0:T(8,128)(2,1)S(1)}, u32[]{:S(2)}, u32[]{:S(2)}) collective-permute-start(bf16[32,128]{1,0:T(8,128)(2,1)S(1)} %slice.4), channel_id=1, source_target_pairs={{0,17},{1,16},{2,19},{3,18},{4,21},{5,20},{6,23},{7,22},{8,25},{9,... | collective-permute-start | bytes 24584 | tf_op jit(solution)/shard_map/ppermute | solution.py:28
  12.1 0.2 shard_map.96.queries_ref
  12.3 0.0 collective-permute-done.3
  12.4 2.0 %collective-permute-start.4 = (bf16[256,256]{1,0:T(8,128)(2,1)S(1)}, bf16[256,256]{1,0:T(8,128)(2,1)S(1)}, u32[]{:S(2)}, u32[]{:S(2)}) collective-permute-start(bf16[256,256]{1,0:T(8,128)(2,1)S(1)} %pad_maximum_fusion), channel_id=1, source_target_pairs={{0,9},{1,8},{2,11},{3,10},{4,13},{5,12},{6,15},{7,14},{8,1},{9,0},... | collective-permute-start | bytes 393224 | tf_op jit(solution)/shard_map/ppermute | solution.py:28
  14.4 0.0 collective-permute-done.6
  14.4 0.9 %collective-permute-start.7 = (bf16[64,128]{1,0:T(8,128)(2,1)S(1)}, bf16[64,128]{1,0:T(8,128)(2,1)S(1)}, u32[]{:S(2)}, u32[]{:S(2)}) collective-permute-start(bf16[64,128]{1,0:T(8,128)(2,1)S(1)} %pad_maximum_fusion.4), channel_id=1, source_target_pairs={{0,5},{1,4},{2,7},{3,6},{4,1},{5,0},{6,3},{7,2},{8,13},{9,12},{10,... | collective-permute-start | bytes 49160 | tf_op jit(solution)/shard_map/ppermute | solution.py:28
  15.3 2.7 %collective-permute-done.4 = bf16[256,256]{1,0:T(8,128)(2,1)S(1)} collective-permute-done((bf16[256,256]{1,0:T(8,128)(2,1)S(1)}, bf16[256,256]{1,0:T(8,128)(2,1)S(1)}, u32[]{:S(2)}, u32[]{:S(2)}) %collective-permute-start.4) | collective-permute-done | bytes 131104 | tf_op jit(solution)/shard_map/ppermute | solution.py:28
  18.0 0.3 %collective-permute-start.5 = (bf16[512,256]{1,0:T(8,128)(2,1)S(1)}, bf16[512,256]{1,0:T(8,128)(2,1)S(1)}, u32[]{:S(2)}, u32[]{:S(2)}) collective-permute-start(bf16[512,256]{1,0:T(8,128)(2,1)S(1)} %constant_dynamic-update-slice_fusion.kv_ref), channel_id=1, source_target_pairs={{0,1},{1,0},{2,3},{3,2},{4,5},{5,4},{6,7},{7,6},{8,9},{9,8},{10,11... | collective-permute-start | bytes 786440 | tf_op jit(solution)/shard_map/ppermute | solution.py:28
  18.3 0.0 collective-permute-done.7
  18.3 2.1 %collective-permute-start.8 = (bf16[128,128]{1,0:T(8,128)(2,1)S(1)}, bf16[128,128]{1,0:T(8,128)(2,1)S(1)}, u32[]{:S(2)}, u32[]{:S(2)}) collective-permute-start(bf16[128,128]{1,0:T(8,128)(2,1)S(1)} %pad_maximum_fusion.3), channel_id=1, source_target_pairs={{0,9},{1,8},{2,11},{3,10},{4,13},{5,12},{6,15},{7,14},{8,1},{9,0},... | collective-permute-start | bytes 98312 | tf_op jit(solution)/shard_map/ppermute | solution.py:28
  20.4 1.6 %collective-permute-done.8 = bf16[128,128]{1,0:T(8,128)(2,1)S(1)} collective-permute-done((bf16[128,128]{1,0:T(8,128)(2,1)S(1)}, bf16[128,128]{1,0:T(8,128)(2,1)S(1)}, u32[]{:S(2)}, u32[]{:S(2)}) %collective-permute-start.8) | collective-permute-done | bytes 32800 | tf_op jit(solution)/shard_map/ppermute | solution.py:28
  22.0 0.0 collective-permute-done.5.other_kv_ref
  22.1 0.9 %shard_map.97 = (bf16[768,1024]{1,0:T(8,128)(2,1)S(1)}, f32[128,768]{1,0:T(8,128)S(1)}) custom-call(bf16[128,768]{1,0:T(8,128)(2,1)S(1)} %shard_map.96.queries_ref, f32[128,1024]{1,0:T(8,128)S(1)} %get-tuple-element.14.bias_ref, bf16[512,256]{1,0:T(8,128)(2,1)S(1)} %constant_dynamic-update-slice_fusion.kv_ref, ...), custom_call_target="tpu_custom_call" | custom-call | flops 201326592 | bytes 1572864 | tf_op jit(solution)/shard_map/pallas_call | solution.py:228
  22.9 1.5 %shard_map.98 = (bf16[128,768]{1,0:T(8,128)(2,1)}, f32[6,128]{1,0:T(8,128)}) custom-call(bf16[768,1024]{1,0:T(8,128)(2,1)S(1)} %get-tuple-element.17.weights_ref, f32[128,768]{1,0:T(8,128)S(1)} %get-tuple-element.18.top_ref, bf16[512,256]{1,0:T(8,128)(2,1)S(1)} %constant_dynamic-update-slice_fusion.kv_ref, ...), custom_call_target="tpu_custom_call" | custom-call | flops 402653184 | bytes 3145728 | tf_op jit(solution)/shard_map/pallas_call | solution.py:305
  (10 shorter events, 0.1 us)
Async XLA Ops:
  2.3 4.2 %collective-permute-start = (bf16[64,128]{1,0:T(8,128)(2,1)S(1)}, bf16[64,128]{1,0:T(8,128)(2,1)S(1)}, u32[]{:S(2)}, u32[]{:S(2)}) collective-permute-start(bf16[64,128]{1,0:T(8,128)(2,1)S(1)} %get-tuple-element.12), channel_id=1, source_target_pairs={{0,1},{1,0},{2,3},{3,2},{4,5},{5,4},{6,7},{7,6},{8,9},{9,8},{10,11... | collective-permute-start | bytes 49160 | tf_op jit(solution)/shard_map/ppermute | solution.py:28
  2.9 5.4 %collective-permute-start.2 = (bf16[64,256]{1,0:T(8,128)(2,1)S(1)}, bf16[64,256]{1,0:T(8,128)(2,1)S(1)}, u32[]{:S(2)}, u32[]{:S(2)}) collective-permute-start(bf16[64,256]{1,0:T(8,128)(2,1)S(1)} %get-tuple-element.15), channel_id=1, source_target_pairs={{0,17},{1,16},{2,19},{3,18},{4,21},{5,20},{6,23},{7,22},{8,25},{9,... | collective-permute-start | bytes 98312 | tf_op jit(solution)/shard_map/ppermute | solution.py:28
  6.6 3.2 %collective-permute-start.1 = (bf16[64,128]{1,0:T(8,128)(2,1)S(1)}, bf16[64,128]{1,0:T(8,128)(2,1)S(1)}, u32[]{:S(2)}, u32[]{:S(2)}) collective-permute-start(bf16[64,128]{1,0:T(8,128)(2,1)S(1)} %add_convert_fusion.1), channel_id=1, source_target_pairs={{0,3},{1,2},{2,1},{3,0},{4,7},{5,6},{6,5},{7,4},{8,11},{9,10},{10,... | collective-permute-start | bytes 49160 | tf_op jit(solution)/shard_map/ppermute | solution.py:28
  8.2 4.1 %collective-permute-start.3 = (bf16[128,256]{1,0:T(8,128)(2,1)S(1)}, bf16[128,256]{1,0:T(8,128)(2,1)S(1)}, u32[]{:S(2)}, u32[]{:S(2)}) collective-permute-start(bf16[128,256]{1,0:T(8,128)(2,1)S(1)} %pad_maximum_fusion.1), channel_id=1, source_target_pairs={{0,5},{1,4},{2,7},{3,6},{4,1},{5,0},{6,3},{7,2},{8,13},{9,12},{10,... | collective-permute-start | bytes 196616 | tf_op jit(solution)/shard_map/ppermute | solution.py:28
  9.8 4.5 %collective-permute-start.6 = (bf16[32,128]{1,0:T(8,128)(2,1)S(1)}, bf16[32,128]{1,0:T(8,128)(2,1)S(1)}, u32[]{:S(2)}, u32[]{:S(2)}) collective-permute-start(bf16[32,128]{1,0:T(8,128)(2,1)S(1)} %slice.4), channel_id=1, source_target_pairs={{0,17},{1,16},{2,19},{3,18},{4,21},{5,20},{6,23},{7,22},{8,25},{9,... | collective-permute-start | bytes 24584 | tf_op jit(solution)/shard_map/ppermute | solution.py:28
  12.4 5.6 %collective-permute-start.4 = (bf16[256,256]{1,0:T(8,128)(2,1)S(1)}, bf16[256,256]{1,0:T(8,128)(2,1)S(1)}, u32[]{:S(2)}, u32[]{:S(2)}) collective-permute-start(bf16[256,256]{1,0:T(8,128)(2,1)S(1)} %pad_maximum_fusion), channel_id=1, source_target_pairs={{0,9},{1,8},{2,11},{3,10},{4,13},{5,12},{6,15},{7,14},{8,1},{9,0},... | collective-permute-start | bytes 393224 | tf_op jit(solution)/shard_map/ppermute | solution.py:28
  14.4 4.0 %collective-permute-start.7 = (bf16[64,128]{1,0:T(8,128)(2,1)S(1)}, bf16[64,128]{1,0:T(8,128)(2,1)S(1)}, u32[]{:S(2)}, u32[]{:S(2)}) collective-permute-start(bf16[64,128]{1,0:T(8,128)(2,1)S(1)} %pad_maximum_fusion.4), channel_id=1, source_target_pairs={{0,5},{1,4},{2,7},{3,6},{4,1},{5,0},{6,3},{7,2},{8,13},{9,12},{10,... | collective-permute-start | bytes 49160 | tf_op jit(solution)/shard_map/ppermute | solution.py:28
  18.0 4.0 %collective-permute-start.5 = (bf16[512,256]{1,0:T(8,128)(2,1)S(1)}, bf16[512,256]{1,0:T(8,128)(2,1)S(1)}, u32[]{:S(2)}, u32[]{:S(2)}) collective-permute-start(bf16[512,256]{1,0:T(8,128)(2,1)S(1)} %constant_dynamic-update-slice_fusion.kv_ref), channel_id=1, source_target_pairs={{0,1},{1,0},{2,3},{3,2},{4,5},{5,4},{6,7},{7,6},{8,9},{9,8},{10,11... | collective-permute-start | bytes 786440 | tf_op jit(solution)/shard_map/ppermute | solution.py:28
  18.3 3.7 %collective-permute-start.8 = (bf16[128,128]{1,0:T(8,128)(2,1)S(1)}, bf16[128,128]{1,0:T(8,128)(2,1)S(1)}, u32[]{:S(2)}, u32[]{:S(2)}) collective-permute-start(bf16[128,128]{1,0:T(8,128)(2,1)S(1)} %pad_maximum_fusion.3), channel_id=1, source_target_pairs={{0,9},{1,8},{2,11},{3,10},{4,13},{5,12},{6,15},{7,14},{8,1},{9,0},... | collective-permute-start | bytes 98312 | tf_op jit(solution)/shard_map/ppermute | solution.py:28

commit v5 on v4

--- a/solution.py
+++ b/solution.py
@@ -35,12 +35,12 @@
     return patterns
 
 
-def half_blocks(patterns, ctx, side):
+def half_blocks(patterns, ctx):
     blocks = len(patterns)
     found = []
     for entry in range(2 * blocks):
         pattern = patterns[entry % blocks]
-        half = (side + pattern.bit_count() + entry // blocks) % 2
+        half = (pattern.bit_count() + entry // blocks) % 2
         found.append((entry % blocks, half, 2 * (ctx ^ pattern) + half))
     return found
 
@@ -107,7 +107,7 @@
     first_row, first_lane = row < span, lane < span
     inner = row % span - lane % span
     query_spans = jnp.where(first_row, order_ref[2 * ctx], order_ref[2 * ctx + 1])
-    entries = half_blocks(patterns, ctx, side)
+    entries = half_blocks(patterns, ctx)
     for tile in range(len(patterns)):
         first, second = order_ref[entries[2 * tile][2]], order_ref[entries[2 * tile + 1][2]]
         ahead = jnp.where(first_lane, first, second) - query_spans
@@ -193,37 +193,31 @@
     )(frozen_query, low, query_up)
 
 
-def weights_kernel(queries_ref, bias_ref, kv_ref, other_kv_ref, weights_ref, top_ref):
+def weights_kernel(queries_ref, bias_ref, kv_ref, weights_ref, top_ref):
     tok_dev, width = queries_ref.shape
-    half = kv_ref.shape[0]
     for head in range(width // HEAD_SIZE):
         columns = slice(head * HEAD_SIZE, (head + 1) * HEAD_SIZE)
-        rows = slice(head * tok_dev, (head + 1) * tok_dev)
-        scores = [
+        scores = (
             lax.dot_general(
                 queries_ref[:, columns],
-                ref[:, :HEAD_SIZE],
+                kv_ref[:, :HEAD_SIZE],
                 (((1,), (1,)), ((), ())),
                 preferred_element_type=jnp.float32,
             )
             * SCORE_FACTOR
-            + bias_ref[:, n * half : (n + 1) * half]
-            for n, ref in enumerate((kv_ref, other_kv_ref))
-        ]
-        top = jnp.maximum(
-            jnp.max(scores[0], axis=1, keepdims=True), jnp.max(scores[1], axis=1, keepdims=True)
-        )
-        for n in range(2):
-            weights_ref[rows, n * half : (n + 1) * half] = jnp.exp2(scores[n] - top).astype(
-                jnp.bfloat16
-            )
+            + bias_ref[...]
+        )
+        top = jnp.max(scores, axis=1, keepdims=True)
+        weights_ref[head * tok_dev : (head + 1) * tok_dev, :] = jnp.exp2(scores - top).astype(
+            jnp.bfloat16
+        )
         top_ref[:, columns] = jnp.broadcast_to(top, (tok_dev, HEAD_SIZE))
 
 
-def make_weights(queries, bias, kv, other_kv):
+def make_weights(queries, bias, kv):
     tok_dev, width = queries.shape
     heads = width // HEAD_SIZE
-    key_count = 2 * kv.shape[0]
+    key_count = kv.shape[0]
     vmem = pl.BlockSpec(memory_space=pltpu.VMEM)
     return pl.pallas_call(
         weights_kernel,
@@ -231,7 +225,7 @@
             jax.ShapeDtypeStruct((heads * tok_dev, key_count), jnp.bfloat16),
             jax.ShapeDtypeStruct((tok_dev, width), jnp.float32),
         ),
-        in_specs=[vmem] * 4,
+        in_specs=[vmem] * 3,
         out_specs=(vmem, vmem),
         compiler_params=pltpu.CompilerParams(vmem_limit_bytes=VMEM_LIMIT),
         cost_estimate=pl.CostEstimate(
@@ -239,7 +233,7 @@
             bytes_accessed=2 * tok_dev * heads * key_count,
             transcendentals=heads * tok_dev * key_count,
         ),
-    )(queries, bias, kv, other_kv)
+    )(queries, bias, kv)
 
 
 def values_kernel(
@@ -247,7 +241,6 @@
     weights_ref,
     top_ref,
     kv_ref,
-    other_kv_ref,
     low_value_ref,
     value_up_ref,
     attended_ref,
@@ -256,29 +249,24 @@
 ):
     tok_dev, width = top_ref.shape
     span = tok_dev // 2
-    blocks = len(patterns)
-    half_count = blocks * span
     heads = width // HEAD_SIZE
-    ctx, side = lax.axis_index("ctx"), lax.axis_index("head") % 2
-    entries = half_blocks(patterns, ctx, side)
-    value_ref[:, HEAD_SIZE:] = jnp.ones((2 * half_count, HEAD_SIZE), jnp.bfloat16)
-    for block in range(blocks):
-        update = ADAPTER_SCALE * lax.dot_general(
+    value_ref[:, HEAD_SIZE:] = jnp.ones((value_ref.shape[0], HEAD_SIZE), jnp.bfloat16)
+    updates = [
+        ADAPTER_SCALE
+        * lax.dot_general(
             low_value_ref[block * ADAPTER_RANK : (block + 1) * ADAPTER_RANK, :],
             value_up_ref[...],
             (((0,), (0,)), ((), ())),
             preferred_element_type=jnp.float32,
         )
-        low_half = entries[block][1] == 0
-        parts = (
-            jnp.where(low_half, update[:span], update[span:]),
-            jnp.where(low_half, update[span:], update[:span]),
-        )
-        here = slice(block * span, (block + 1) * span)
-        for n, ref in enumerate((kv_ref, other_kv_ref)):
-            value_ref[n * half_count + block * span : n * half_count + (block + 1) * span, :HEAD_SIZE] = (
-                ref[here, HEAD_SIZE:].astype(jnp.float32) + parts[n]
-            ).astype(jnp.bfloat16)
+        for block in range(len(patterns))
+    ]
+    for entry, (block, half, _) in enumerate(half_blocks(patterns, 0)):
+        here = slice(entry * span, (entry + 1) * span)
+        value_ref[here, :HEAD_SIZE] = (
+            kv_ref[here, HEAD_SIZE:].astype(jnp.float32)
+            + updates[block][half * span : (half + 1) * span]
+        ).astype(jnp.bfloat16)
     row = lax.broadcasted_iota(jnp.int32, (tok_dev, tok_dev), 0)
     lane = lax.broadcasted_iota(jnp.int32, (tok_dev, tok_dev), 1)
     for head in range(heads):
@@ -297,10 +285,10 @@
         )
 
 
-def weigh_values(patterns, weights, top, kv, other_kv, low_value, value_up):
+def weigh_values(patterns, weights, top, kv, low_value, value_up):
     tok_dev, width = top.shape
     heads = width // HEAD_SIZE
-    key_count = 2 * kv.shape[0]
+    key_count = kv.shape[0]
     vmem = pl.BlockSpec(memory_space=pltpu.VMEM)
     return pl.pallas_call(
         functools.partial(values_kernel, patterns),
@@ -308,7 +296,7 @@
             jax.ShapeDtypeStruct((tok_dev, width), jnp.bfloat16),
             jax.ShapeDtypeStruct((heads, tok_dev), jnp.float32),
         ),
-        in_specs=[vmem] * 6,
+        in_specs=[vmem] * 5,
         out_specs=(vmem, vmem),
         scratch_shapes=[
             pltpu.VMEM((key_count, 2 * HEAD_SIZE), jnp.bfloat16),
@@ -319,7 +307,7 @@
             bytes_accessed=4 * tok_dev * heads * key_count,
             transcendentals=0,
         ),
-    )(weights, top, kv, other_kv, low_value, value_up)
+    )(weights, top, kv, low_value, value_up)
 
 
 def attend_long(patterns, ctx, head, order, frozen_query, low, query_up, kv, low_value, value_up):
@@ -327,7 +315,6 @@
     span = tok_dev // 2
     heads = width // HEAD_SIZE
     blocks = len(patterns)
-    side = head % 2
     group = head // (lax.axis_size("head") // KEY_VALUE_HEADS)
     value_up = lax.dynamic_slice_in_dim(value_up, group * HEAD_SIZE, HEAD_SIZE, 1)
     low = low.T
@@ -338,15 +325,15 @@
         * jnp.dot(low[:, :ADAPTER_RANK], query_up, preferred_element_type=jnp.float32)
     ).astype(jnp.bfloat16)
     queries = queries.reshape(tok_dev, heads, HEAD_SIZE).transpose(1, 0, 2).reshape(-1, HEAD_SIZE)
-    pattern = jnp.tile(jnp.array(patterns, jnp.int32), 2)
-    parity = jnp.array([p.bit_count() for p in patterns] + [p.bit_count() + 1 for p in patterns])
-    half = (side + parity.astype(jnp.int32)) % 2
+    entries = half_blocks(patterns, 0)
+    pattern = jnp.array([slot // 2 for _, _, slot in entries], jnp.int32)
+    index = jnp.array([block for block, _, _ in entries], jnp.int32)
+    half = jnp.array([half for _, half, _ in entries], jnp.int32)
     key_spans = order[2 * (ctx ^ pattern) + half]
     inner = jnp.arange(span, dtype=jnp.int32)
     key_pos = (key_spans[:, None] * span + inner).reshape(-1)
     query_spans = lax.dynamic_slice_in_dim(order, 2 * ctx, 2)
     query_pos = jnp.tile((query_spans[:, None] * span + inner).reshape(-1), heads)
-    index = jnp.tile(jnp.arange(blocks, dtype=jnp.int32), 2)
     low_rows = low_value.reshape(2 * blocks, span, ADAPTER_RANK)[2 * index + half]
     values = (
         kv[:, HEAD_SIZE:].astype(jnp.float32)
@@ -431,9 +418,12 @@
     for bit in bits:
         if short and bit == bits[-1]:
             kv, _ = lax.optimization_barrier((kv, queries))
-        low_value = jnp.concatenate([low_value, exchange(low_value, bit, 1)], axis=0)
+        last_low = exchange(low_value, bit, 1)
+        if not short or bit != bits[-1]:
+            low_value = jnp.concatenate([low_value, last_low], axis=0)
         kv = jnp.concatenate([kv, exchange(kv, bit, 1)], axis=0)
-    other_kv = exchange(kv, 0, 1)
+    pairs = [[h, h + 1] for h in range(0, head_count, 2)]
+    kv = lax.all_gather(kv, "head", axis=0, tiled=True, axis_index_groups=pairs)
     if not short:
         return attend_long(
             patterns,
@@ -443,12 +433,14 @@
             frozen_query_rows,
             low,
             query_up_factor,
-            jnp.concatenate([kv, other_kv], axis=0),
+            kv,
             low_value,
             value_up_factor,
         )
-    weights, top = make_weights(queries, bias, kv, other_kv)
-    return weigh_values(patterns, weights, top, kv, other_kv, low_value, value_up)
+    weights, top = make_weights(queries, bias, kv)
+    last_low, weights = lax.optimization_barrier((last_low, weights))
+    low_value = jnp.concatenate([low_value, last_low], axis=0)
+    return weigh_values(patterns, weights, top, kv, low_value, value_up)
 
 
 def solution(mesh):

time: 24.6 us -> 23.7 us (0.963)
  blocking collectives: 0 us -> 2.18 us
  waiting for transfers between devices: 4.86 us -> 2.79 us
  starting transfers between devices: 14.5 us -> 13.4 us
    all_gather x0 -> x1, blocking collectives: none -> 2.18 us  [local(): kv = lax.all_gather(kv, 'head', axis=0, tiled=True, axis_index_groups=pairs)]
    ppermute x9 -> x8, waiting for transfers between devices: 4.86 us -> 2.79 us  [exchange(): return lax.ppermute(value, AXES, pairs)]
    ppermute x9 -> x8, starting transfers between devices: 14.5 us -> 13.4 us  [exchange(): return lax.ppermute(value, AXES, pairs)]
  transfers between devices with their start and end apart: 9 -> 8, of which waited for: 4 -> 3; matrix products, arithmetic and copies ran while one was open for 0% -> 0% of each run, Pallas kernels for 1% -> 5%
where the time goes in v5:
time: 23.7 us; the launch traced here: 23.5 us
  starting transfers between devices  13.4 us (57%)
  Pallas kernels  4.38 us (18%)
  waiting for transfers between devices  2.79 us (12%)
  blocking collectives  2.18 us (9%)
  between operations  0.71 us (3%)
    ppermute x8, starting transfers between devices, exchange(): return lax.ppermute(value, AXES, pairs)  13.4 us
    ppermute x8, waiting for transfers between devices, exchange(): return lax.ppermute(value, AXES, pairs)  2.79 us
    all_gather x1, blocking collectives, local(): kv = lax.all_gather(kv, 'head', axis=0, tiled=True, axis_index_groups=pairs)  2.18 us
    pallas_call x1, Pallas kernels, prologue(): pl.pallas_call(functools.partial(prologue_kernel, patterns), out_shape=(j...  1.7 us
    pallas_call x1, Pallas kernels, weigh_values(): pl.pallas_call(functools.partial(values_kernel, patterns), out_shape=(jax...  1.49 us
    pallas_call x1, Pallas kernels, make_weights(): pl.pallas_call(weights_kernel, out_shape=(jax.ShapeDtypeStruct((heads * t...  0.94 us
  transfers between devices with their start and end apart: 8, of which 3 were waited for; matrix products, arithmetic and copies ran while one was open for 0% of the time, Pallas kernels for 5%

profile of v5, /device:TPU:0, one launch (start us, length us, event | category | flops | bytes accessed | tf_op | source)
XLA Modules:
  0.0 23.5 jit_solution(9868003212091245404)
XLA Ops:
  0.6 1.7 %shard_map.95 = (bf16[64,128]{1,0:T(8,128)(2,1)S(1)}, bf16[64,256]{1,0:T(8,128)(2,1)S(1)}, f32[128,1024]{1,0:T(8,128)S(1)}, bf16[128,768]{1,0:T(8,128)(2,1)S(1)}...) custom-call(bf16[128,2048]{1,0:T(8,128)(2,1)} %hidden_hbm.1, bf16[64,2048]{1,0:T(8,128)(2,1)} %bitcast.1, ...), custom_call_target="tpu_custom_call" | custom-call | flops 33554432 | bytes 1048576 | tf_op jit(solution)/shard_map/pallas_call | solution.py:140
  2.3 0.5 %collective-permute-start = (bf16[64,128]{1,0:T(8,128)(2,1)S(1)}, bf16[64,128]{1,0:T(8,128)(2,1)S(1)}, u32[]{:S(2)}, u32[]{:S(2)}) collective-permute-start(bf16[64,128]{1,0:T(8,128)(2,1)S(1)} %get-tuple-element.13), channel_id=1, source_target_pairs={{0,1},{1,0},{2,3},{3,2},{4,5},{5,4},{6,7},{7,6},{8,9},{9,8},{10,11... | collective-permute-start | bytes 49160 | tf_op jit(solution)/shard_map/ppermute | solution.py:28
  2.9 3.7 %collective-permute-start.5 = (bf16[64,256]{1,0:T(8,128)(2,1)S(1)}, bf16[64,256]{1,0:T(8,128)(2,1)S(1)}, u32[]{:S(2)}, u32[]{:S(2)}) collective-permute-start(bf16[64,256]{1,0:T(8,128)(2,1)S(1)} %get-tuple-element.17), channel_id=1, source_target_pairs={{0,17},{1,16},{2,19},{3,18},{4,21},{5,20},{6,23},{7,22},{8,25},{9,... | collective-permute-start | bytes 98312 | tf_op jit(solution)/shard_map/ppermute | solution.py:28
  6.6 0.0 collective-permute-done
  6.6 1.3 %collective-permute-start.1 = (bf16[64,128]{1,0:T(8,128)(2,1)S(1)}, bf16[64,128]{1,0:T(8,128)(2,1)S(1)}, u32[]{:S(2)}, u32[]{:S(2)}) collective-permute-start(bf16[64,128]{1,0:T(8,128)(2,1)S(1)} %add_convert_fusion.1), channel_id=1, source_target_pairs={{0,3},{1,2},{2,1},{3,0},{4,7},{5,6},{6,5},{7,4},{8,11},{9,10},{10,... | collective-permute-start | bytes 49160 | tf_op jit(solution)/shard_map/ppermute | solution.py:28
  7.8 0.4 %collective-permute-done.5 = bf16[64,256]{1,0:T(8,128)(2,1)S(1)} collective-permute-done((bf16[64,256]{1,0:T(8,128)(2,1)S(1)}, bf16[64,256]{1,0:T(8,128)(2,1)S(1)}, u32[]{:S(2)}, u32[]{:S(2)}) %collective-permute-start.5) | collective-permute-done | bytes 32800 | tf_op jit(solution)/shard_map/ppermute | solution.py:28
  8.2 1.5 %collective-permute-start.6 = (bf16[128,256]{1,0:T(8,128)(2,1)S(1)}, bf16[128,256]{1,0:T(8,128)(2,1)S(1)}, u32[]{:S(2)}, u32[]{:S(2)}) collective-permute-start(bf16[128,256]{1,0:T(8,128)(2,1)S(1)} %pad_maximum_fusion.2), channel_id=1, source_target_pairs={{0,5},{1,4},{2,7},{3,6},{4,1},{5,0},{6,3},{7,2},{8,13},{9,12},{10,... | collective-permute-start | bytes 196616 | tf_op jit(solution)/shard_map/ppermute | solution.py:28
  9.7 0.1 collective-permute-done.1
  9.8 2.2 %collective-permute-start.2 = (bf16[32,128]{1,0:T(8,128)(2,1)S(1)}, bf16[32,128]{1,0:T(8,128)(2,1)S(1)}, u32[]{:S(2)}, u32[]{:S(2)}) collective-permute-start(bf16[32,128]{1,0:T(8,128)(2,1)S(1)} %slice.4), channel_id=1, source_target_pairs={{0,17},{1,16},{2,19},{3,18},{4,21},{5,20},{6,23},{7,22},{8,25},{9,... | collective-permute-start | bytes 24584 | tf_op jit(solution)/shard_map/ppermute | solution.py:28
  12.1 0.2 %shard_map.96.queries_ref = bf16[128,768]{1,0:T(8,128)(2,1)S(1)} custom-call(bf16[128,768]{1,0:T(8,128)(2,1)S(1)} %get-tuple-element.14.frozen_query_ref, bf16[64,128]{1,0:T(8,128)(2,1)S(1)} %add_convert_fusion.low_ref, bf16[32,768]{1,0:T(8,128)(2,1)S(1)} %get-tuple-element.15.query_up_ref), custom_call_target="tpu_custom_call" | custom-call | flops 6291456 | bytes 393216 | tf_op jit(solution)/shard_map/pallas_call | solution.py:182
  12.3 0.0 collective-permute-done.6
  12.4 2.0 %collective-permute-start.7 = (bf16[256,256]{1,0:T(8,128)(2,1)S(1)}, bf16[256,256]{1,0:T(8,128)(2,1)S(1)}, u32[]{:S(2)}, u32[]{:S(2)}) collective-permute-start(bf16[256,256]{1,0:T(8,128)(2,1)S(1)} %pad_maximum_fusion.1), channel_id=1, source_target_pairs={{0,9},{1,8},{2,11},{3,10},{4,13},{5,12},{6,15},{7,14},{8,1},{9,0},... | collective-permute-start | bytes 393224 | tf_op jit(solution)/shard_map/ppermute | solution.py:28
  14.4 0.0 collective-permute-done.2
  14.4 0.9 %collective-permute-start.3 = (bf16[64,128]{1,0:T(8,128)(2,1)S(1)}, bf16[64,128]{1,0:T(8,128)(2,1)S(1)}, u32[]{:S(2)}, u32[]{:S(2)}) collective-permute-start(bf16[64,128]{1,0:T(8,128)(2,1)S(1)} %pad_maximum_fusion.5), channel_id=1, source_target_pairs={{0,5},{1,4},{2,7},{3,6},{4,1},{5,0},{6,3},{7,2},{8,13},{9,12},{10,... | collective-permute-start | bytes 49160 | tf_op jit(solution)/shard_map/ppermute | solution.py:28
  15.3 2.3 %collective-permute-done.3 = bf16[64,128]{1,0:T(8,128)(2,1)S(1)} collective-permute-done((bf16[64,128]{1,0:T(8,128)(2,1)S(1)}, bf16[64,128]{1,0:T(8,128)(2,1)S(1)}, u32[]{:S(2)}, u32[]{:S(2)}) %collective-permute-start.3) | collective-permute-done | bytes 16416 | tf_op jit(solution)/shard_map/ppermute | solution.py:28
  17.5 1.3 %collective-permute-start.4 = (bf16[128,128]{1,0:T(8,128)(2,1)S(1)}, bf16[128,128]{1,0:T(8,128)(2,1)S(1)}, u32[]{:S(2)}, u32[]{:S(2)}) collective-permute-start(bf16[128,128]{1,0:T(8,128)(2,1)S(1)} %pad_maximum_fusion.4), channel_id=1, source_target_pairs={{0,9},{1,8},{2,11},{3,10},{4,13},{5,12},{6,15},{7,14},{8,1},{9,0},... | collective-permute-start | bytes 98312 | tf_op jit(solution)/shard_map/ppermute | solution.py:28
  18.8 0.0 collective-permute-done.7
  18.9 2.2 %all_gather.3.kv_ref = bf16[1024,256]{1,0:T(8,128)(2,1)S(1)} all-gather(bf16[512,256]{1,0:T(8,128)(2,1)S(1)} %pad_maximum_fusion), channel_id=1, replica_groups={{0,1},{2,3},{4,5},{6,7},{8,9},{10,11},{12,13},{14,15},{16,17},{18,19},{..., dimensions={0}, use_global_device_ids=true | all-gather | bytes 786432 | tf_op jit(solution)/shard_map/all_gather | solution.py:426
  21.0 0.9 %shard_map.97 = (bf16[768,1024]{1,0:T(8,128)(2,1)S(1)}, f32[128,768]{1,0:T(8,128)S(1)}) custom-call(bf16[128,768]{1,0:T(8,128)(2,1)S(1)} %shard_map.96.queries_ref, f32[128,1024]{1,0:T(8,128)S(1)} %get-tuple-element.16.bias_ref, bf16[1024,256]{1,0:T(8,128)(2,1)S(1)} %all_gather.3.kv_ref), custom_call_target="tpu_custom_call" | custom-call | flops 201326592 | bytes 1572864 | tf_op jit(solution)/shard_map/pallas_call | solution.py:222
  22.0 0.0 collective-permute-done.4
  22.0 1.5 %shard_map.98 = (bf16[128,768]{1,0:T(8,128)(2,1)}, f32[6,128]{1,0:T(8,128)}) custom-call(bf16[768,1024]{1,0:T(8,128)(2,1)S(1)} %get-tuple-element.20.weights_ref, f32[128,768]{1,0:T(8,128)S(1)} %get-tuple-element.21.top_ref, bf16[1024,256]{1,0:T(8,128)(2,1)S(1)} %all_gather.3.kv_ref, bf16[256,128]{1,0:T(8,128)(2,1)S(1)} %pad_maximum_fusion.3.low_value_ref, ...), custom_call_target="tpu_custom_call" | custom-call | flops 402653184 | bytes 3145728 | tf_op jit(solution)/shard_map/pallas_call | solution.py:293
  (9 shorter events, 0.1 us)
Async XLA Ops:
  2.3 4.2 %collective-permute-start = (bf16[64,128]{1,0:T(8,128)(2,1)S(1)}, bf16[64,128]{1,0:T(8,128)(2,1)S(1)}, u32[]{:S(2)}, u32[]{:S(2)}) collective-permute-start(bf16[64,128]{1,0:T(8,128)(2,1)S(1)} %get-tuple-element.13), channel_id=1, source_target_pairs={{0,1},{1,0},{2,3},{3,2},{4,5},{5,4},{6,7},{7,6},{8,9},{9,8},{10,11... | collective-permute-start | bytes 49160 | tf_op jit(solution)/shard_map/ppermute | solution.py:28
  2.9 5.4 %collective-permute-start.5 = (bf16[64,256]{1,0:T(8,128)(2,1)S(1)}, bf16[64,256]{1,0:T(8,128)(2,1)S(1)}, u32[]{:S(2)}, u32[]{:S(2)}) collective-permute-start(bf16[64,256]{1,0:T(8,128)(2,1)S(1)} %get-tuple-element.17), channel_id=1, source_target_pairs={{0,17},{1,16},{2,19},{3,18},{4,21},{5,20},{6,23},{7,22},{8,25},{9,... | collective-permute-start | bytes 98312 | tf_op jit(solution)/shard_map/ppermute | solution.py:28
  6.6 3.2 %collective-permute-start.1 = (bf16[64,128]{1,0:T(8,128)(2,1)S(1)}, bf16[64,128]{1,0:T(8,128)(2,1)S(1)}, u32[]{:S(2)}, u32[]{:S(2)}) collective-permute-start(bf16[64,128]{1,0:T(8,128)(2,1)S(1)} %add_convert_fusion.1), channel_id=1, source_target_pairs={{0,3},{1,2},{2,1},{3,0},{4,7},{5,6},{6,5},{7,4},{8,11},{9,10},{10,... | collective-permute-start | bytes 49160 | tf_op jit(solution)/shard_map/ppermute | solution.py:28
  8.2 4.1 %collective-permute-start.6 = (bf16[128,256]{1,0:T(8,128)(2,1)S(1)}, bf16[128,256]{1,0:T(8,128)(2,1)S(1)}, u32[]{:S(2)}, u32[]{:S(2)}) collective-permute-start(bf16[128,256]{1,0:T(8,128)(2,1)S(1)} %pad_maximum_fusion.2), channel_id=1, source_target_pairs={{0,5},{1,4},{2,7},{3,6},{4,1},{5,0},{6,3},{7,2},{8,13},{9,12},{10,... | collective-permute-start | bytes 196616 | tf_op jit(solution)/shard_map/ppermute | solution.py:28
  9.8 4.5 %collective-permute-start.2 = (bf16[32,128]{1,0:T(8,128)(2,1)S(1)}, bf16[32,128]{1,0:T(8,128)(2,1)S(1)}, u32[]{:S(2)}, u32[]{:S(2)}) collective-permute-start(bf16[32,128]{1,0:T(8,128)(2,1)S(1)} %slice.4), channel_id=1, source_target_pairs={{0,17},{1,16},{2,19},{3,18},{4,21},{5,20},{6,23},{7,22},{8,25},{9,... | collective-permute-start | bytes 24584 | tf_op jit(solution)/shard_map/ppermute | solution.py:28
  12.4 6.5 %collective-permute-start.7 = (bf16[256,256]{1,0:T(8,128)(2,1)S(1)}, bf16[256,256]{1,0:T(8,128)(2,1)S(1)}, u32[]{:S(2)}, u32[]{:S(2)}) collective-permute-start(bf16[256,256]{1,0:T(8,128)(2,1)S(1)} %pad_maximum_fusion.1), channel_id=1, source_target_pairs={{0,9},{1,8},{2,11},{3,10},{4,13},{5,12},{6,15},{7,14},{8,1},{9,0},... | collective-permute-start | bytes 393224 | tf_op jit(solution)/shard_map/ppermute | solution.py:28
  14.4 3.2 %collective-permute-start.3 = (bf16[64,128]{1,0:T(8,128)(2,1)S(1)}, bf16[64,128]{1,0:T(8,128)(2,1)S(1)}, u32[]{:S(2)}, u32[]{:S(2)}) collective-permute-start(bf16[64,128]{1,0:T(8,128)(2,1)S(1)} %pad_maximum_fusion.5), channel_id=1, source_target_pairs={{0,5},{1,4},{2,7},{3,6},{4,1},{5,0},{6,3},{7,2},{8,13},{9,12},{10,... | collective-permute-start | bytes 49160 | tf_op jit(solution)/shard_map/ppermute | solution.py:28
  17.5 4.5 %collective-permute-start.4 = (bf16[128,128]{1,0:T(8,128)(2,1)S(1)}, bf16[128,128]{1,0:T(8,128)(2,1)S(1)}, u32[]{:S(2)}, u32[]{:S(2)}) collective-permute-start(bf16[128,128]{1,0:T(8,128)(2,1)S(1)} %pad_maximum_fusion.4), channel_id=1, source_target_pairs={{0,9},{1,8},{2,11},{3,10},{4,13},{5,12},{6,15},{7,14},{8,1},{9,0},... | collective-permute-start | bytes 98312 | tf_op jit(solution)/shard_map/ppermute | solution.py:28

commit v6 on v4

--- a/solution.py
+++ b/solution.py
@@ -36,12 +36,13 @@
 
 
 def half_blocks(patterns, ctx, side):
-    blocks = len(patterns)
+    half_count = len(patterns) // 2
     found = []
-    for entry in range(2 * blocks):
-        pattern = patterns[entry % blocks]
-        half = (side + pattern.bit_count() + entry // blocks) % 2
-        found.append((entry % blocks, half, 2 * (ctx ^ pattern) + half))
+    for first in (0, half_count):
+        for other in (0, 1):
+            for block in range(first, first + half_count):
+                half = (side + patterns[block].bit_count() + other) % 2
+                found.append((block, half, 2 * (ctx ^ patterns[block]) + half))
     return found
 
 
@@ -193,59 +194,120 @@
     )(frozen_query, low, query_up)
 
 
-def weights_kernel(queries_ref, bias_ref, kv_ref, other_kv_ref, weights_ref, top_ref):
+def fill_values(value_ref, patterns, kv_refs, low_value_ref, value_up_ref):
+    span = value_ref.shape[0] // (2 * len(patterns))
+    side = lax.axis_index("head") % 2
+    value_ref[:, HEAD_SIZE:] = jnp.ones((value_ref.shape[0], HEAD_SIZE), jnp.bfloat16)
+    for n, pattern in enumerate(patterns):
+        update = ADAPTER_SCALE * lax.dot_general(
+            low_value_ref[n * ADAPTER_RANK : (n + 1) * ADAPTER_RANK, :],
+            value_up_ref[...],
+            (((0,), (0,)), ((), ())),
+            preferred_element_type=jnp.float32,
+        )
+        own_half = (side + pattern.bit_count()) % 2 == 0
+        parts = (
+            jnp.where(own_half, update[:span], update[span:]),
+            jnp.where(own_half, update[span:], update[:span]),
+        )
+        for other, kv_ref in enumerate(kv_refs):
+            at = (other * len(patterns) + n) * span
+            value_ref[at : at + span, :HEAD_SIZE] = (
+                kv_ref[n * span : (n + 1) * span, HEAD_SIZE:].astype(jnp.float32) + parts[other]
+            ).astype(jnp.bfloat16)
+
+
+def scores_of(queries, kv_ref, bias):
+    return (
+        lax.dot_general(
+            queries,
+            kv_ref[:, :HEAD_SIZE],
+            (((1,), (1,)), ((), ())),
+            preferred_element_type=jnp.float32,
+        )
+        * SCORE_FACTOR
+        + bias
+    )
+
+
+def first_kernel(
+    patterns,
+    queries_ref,
+    bias_ref,
+    kv_ref,
+    other_kv_ref,
+    low_value_ref,
+    value_up_ref,
+    top_ref,
+    sums_ref,
+    weights_ref,
+    value_ref,
+):
     tok_dev, width = queries_ref.shape
-    half = kv_ref.shape[0]
+    heads = width // HEAD_SIZE
+    count = kv_ref.shape[0]
+    fill_values(
+        value_ref, patterns[: len(patterns) // 2], (kv_ref, other_kv_ref), low_value_ref, value_up_ref
+    )
+    for head in range(heads):
+        columns = slice(head * HEAD_SIZE, (head + 1) * HEAD_SIZE)
+        rows = slice(head * tok_dev, (head + 1) * tok_dev)
+        scores = [
+            scores_of(queries_ref[:, columns], ref, bias_ref[:, n * count : (n + 1) * count])
+            for n, ref in enumerate((kv_ref, other_kv_ref))
+        ]
+        top = jnp.maximum(
+            jnp.max(scores[0], axis=1, keepdims=True), jnp.max(scores[1], axis=1, keepdims=True)
+        )
+        for n in range(2):
+            weights_ref[rows, n * count : (n + 1) * count] = jnp.exp2(scores[n] - top).astype(
+                jnp.bfloat16
+            )
+        top_ref[:, columns] = jnp.broadcast_to(top, (tok_dev, HEAD_SIZE))
+    for head in range(heads):
+        rows = slice(head * tok_dev, (head + 1) * tok_dev)
+        sums_ref[rows, :] = jnp.dot(
+            weights_ref[rows, :], value_ref[...], preferred_element_type=jnp.float32
+        )
+
+
+def second_kernel(
+    patterns, queries_ref, bias_ref, kv_ref, other_kv_ref, first_top_ref, weights_ref, top_ref, scale_ref
+):
+    tok_dev, width = queries_ref.shape
+    count = kv_ref.shape[0]
+    before = bias_ref.shape[1] // 2
     for head in range(width // HEAD_SIZE):
         columns = slice(head * HEAD_SIZE, (head + 1) * HEAD_SIZE)
         rows = slice(head * tok_dev, (head + 1) * tok_dev)
         scores = [
-            lax.dot_general(
+            scores_of(
                 queries_ref[:, columns],
-                ref[:, :HEAD_SIZE],
-                (((1,), (1,)), ((), ())),
-                preferred_element_type=jnp.float32,
+                ref,
+                bias_ref[:, before + n * count : before + (n + 1) * count],
             )
-            * SCORE_FACTOR
-            + bias_ref[:, n * half : (n + 1) * half]
             for n, ref in enumerate((kv_ref, other_kv_ref))
         ]
-        top = jnp.maximum(
+        new_top = jnp.maximum(
             jnp.max(scores[0], axis=1, keepdims=True), jnp.max(scores[1], axis=1, keepdims=True)
         )
+        first_top = first_top_ref[:, columns]
+        top = jnp.maximum(first_top, new_top)
         for n in range(2):
-            weights_ref[rows, n * half : (n + 1) * half] = jnp.exp2(scores[n] - top).astype(
-                jnp.bfloat16
-            )
-        top_ref[:, columns] = jnp.broadcast_to(top, (tok_dev, HEAD_SIZE))
-
-
-def make_weights(queries, bias, kv, other_kv):
-    tok_dev, width = queries.shape
-    heads = width // HEAD_SIZE
-    key_count = 2 * kv.shape[0]
-    vmem = pl.BlockSpec(memory_space=pltpu.VMEM)
-    return pl.pallas_call(
-        weights_kernel,
-        out_shape=(
-            jax.ShapeDtypeStruct((heads * tok_dev, key_count), jnp.bfloat16),
-            jax.ShapeDtypeStruct((tok_dev, width), jnp.float32),
-        ),
-        in_specs=[vmem] * 4,
-        out_specs=(vmem, vmem),
-        compiler_params=pltpu.CompilerParams(vmem_limit_bytes=VMEM_LIMIT),
-        cost_estimate=pl.CostEstimate(
-            flops=2 * tok_dev * width * key_count,
-            bytes_accessed=2 * tok_dev * heads * key_count,
-            transcendentals=heads * tok_dev * key_count,
-        ),
-    )(queries, bias, kv, other_kv)
-
-
-def values_kernel(
+            for at in range(0, count, HEAD_SIZE):
+                weights_ref[rows, n * count + at : n * count + at + HEAD_SIZE] = jnp.exp2(
+                    scores[n][:, at : at + HEAD_SIZE] - top
+                ).astype(jnp.bfloat16)
+        top_ref[:, columns] = top
+        scale_ref[:, columns] = jnp.exp2(first_top - top)
+
+
+def third_kernel(
     patterns,
     weights_ref,
     top_ref,
+    scale_ref,
+    first_sums_ref,
     kv_ref,
     other_kv_ref,
     low_value_ref,
@@ -255,41 +317,20 @@
     value_ref,
 ):
     tok_dev, width = top_ref.shape
-    span = tok_dev // 2
-    blocks = len(patterns)
-    half_count = blocks * span
-    heads = width // HEAD_SIZE
-    ctx, side = lax.axis_index("ctx"), lax.axis_index("head") % 2
-    entries = half_blocks(patterns, ctx, side)
-    value_ref[:, HEAD_SIZE:] = jnp.ones((2 * half_count, HEAD_SIZE), jnp.bfloat16)
-    for block in range(blocks):
-        update = ADAPTER_SCALE * lax.dot_general(
-            low_value_ref[block * ADAPTER_RANK : (block + 1) * ADAPTER_RANK, :],
-            value_up_ref[...],
-            (((0,), (0,)), ((), ())),
-            preferred_element_type=jnp.float32,
-        )
-        low_half = entries[block][1] == 0
-        parts = (
-            jnp.where(low_half, update[:span], update[span:]),
-            jnp.where(low_half, update[span:], update[:span]),
-        )
-        here = slice(block * span, (block + 1) * span)
-        for n, ref in enumerate((kv_ref, other_kv_ref)):
-            value_ref[n * half_count + block * span : n * half_count + (block + 1) * span, :HEAD_SIZE] = (
-                ref[here, HEAD_SIZE:].astype(jnp.float32) + parts[n]
-            ).astype(jnp.bfloat16)
+    fill_values(
+        value_ref, patterns[len(patterns) // 2 :], (kv_ref, other_kv_ref), low_value_ref, value_up_ref
+    )
     row = lax.broadcasted_iota(jnp.int32, (tok_dev, tok_dev), 0)
     lane = lax.broadcasted_iota(jnp.int32, (tok_dev, tok_dev), 1)
-    for head in range(heads):
+    for head in range(width // HEAD_SIZE):
         columns = slice(head * HEAD_SIZE, (head + 1) * HEAD_SIZE)
-        sums = jnp.dot(
-            weights_ref[head * tok_dev : (head + 1) * tok_dev, :],
-            value_ref[...],
-            preferred_element_type=jnp.float32,
-        )
-        total = sums[:, HEAD_SIZE:]
-        attended_ref[:, columns] = (sums[:, :HEAD_SIZE] / total).astype(jnp.bfloat16)
+        rows = slice(head * tok_dev, (head + 1) * tok_dev)
+        sums = jnp.dot(weights_ref[rows, :], value_ref[...], preferred_element_type=jnp.float32)
+        scale = scale_ref[:, columns]
+        total = first_sums_ref[rows, HEAD_SIZE:] * scale + sums[:, HEAD_SIZE:]
+        attended_ref[:, columns] = (
+            (first_sums_ref[rows, :HEAD_SIZE] * scale + sums[:, :HEAD_SIZE]) / total
+        ).astype(jnp.bfloat16)
         normalizer_ref[head : head + 1, :] = jnp.sum(
             jnp.where(row == lane, top_ref[:, columns] * math.log(2.0) + jnp.log(total), 0.0),
             axis=0,
@@ -297,29 +338,19 @@
         )
 
 
-def weigh_values(patterns, weights, top, kv, other_kv, low_value, value_up):
-    tok_dev, width = top.shape
-    heads = width // HEAD_SIZE
-    key_count = 2 * kv.shape[0]
+def call(kernel, patterns, out_shape, scratch_shapes, work, *operands):
     vmem = pl.BlockSpec(memory_space=pltpu.VMEM)
     return pl.pallas_call(
-        functools.partial(values_kernel, patterns),
-        out_shape=(
-            jax.ShapeDtypeStruct((tok_dev, width), jnp.bfloat16),
-            jax.ShapeDtypeStruct((heads, tok_dev), jnp.float32),
-        ),
-        in_specs=[vmem] * 6,
-        out_specs=(vmem, vmem),
-        scratch_shapes=[
-            pltpu.VMEM((key_count, 2 * HEAD_SIZE), jnp.bfloat16),
-        ],
+        functools.partial(kernel, patterns),
+        out_shape=out_shape,
+        in_specs=[vmem] * len(operands),
+        out_specs=(vmem,) * len(out_shape),
+        scratch_shapes=scratch_shapes,
         compiler_params=pltpu.CompilerParams(vmem_limit_bytes=VMEM_LIMIT),
         cost_estimate=pl.CostEstimate(
-            flops=4 * tok_dev * width * key_count,
-            bytes_accessed=4 * tok_dev * heads * key_count,
-            transcendentals=0,
+            flops=work, bytes_accessed=work // 384, transcendentals=work // 768
         ),
-    )(weights, top, kv, other_kv, low_value, value_up)
+    )(*operands)
 
 
 def attend_long(patterns, ctx, head, order, frozen_query, low, query_up, kv, low_value, value_up):
@@ -327,7 +358,6 @@
     span = tok_dev // 2
     heads = width // HEAD_SIZE
     blocks = len(patterns)
-    side = head % 2
     group = head // (lax.axis_size("head") // KEY_VALUE_HEADS)
     value_up = lax.dynamic_slice_in_dim(value_up, group * HEAD_SIZE, HEAD_SIZE, 1)
     low = low.T
@@ -338,15 +368,16 @@
         * jnp.dot(low[:, :ADAPTER_RANK], query_up, preferred_element_type=jnp.float32)
     ).astype(jnp.bfloat16)
     queries = queries.reshape(tok_dev, heads, HEAD_SIZE).transpose(1, 0, 2).reshape(-1, HEAD_SIZE)
-    pattern = jnp.tile(jnp.array(patterns, jnp.int32), 2)
-    parity = jnp.array([p.bit_count() for p in patterns] + [p.bit_count() + 1 for p in patterns])
-    half = (side + parity.astype(jnp.int32)) % 2
+    side = head % 2
+    entries = half_blocks(patterns, 0, 0)
+    pattern = jnp.array([slot // 2 for _, _, slot in entries], jnp.int32)
+    index = jnp.array([block for block, _, _ in entries], jnp.int32)
+    half = (jnp.array([half for _, half, _ in entries], jnp.int32) + side) % 2
     key_spans = order[2 * (ctx ^ pattern) + half]
     inner = jnp.arange(span, dtype=jnp.int32)
     key_pos = (key_spans[:, None] * span + inner).reshape(-1)
     query_spans = lax.dynamic_slice_in_dim(order, 2 * ctx, 2)
     query_pos = jnp.tile((query_spans[:, None] * span + inner).reshape(-1), heads)
-    index = jnp.tile(jnp.arange(blocks, dtype=jnp.int32), 2)
     low_rows = low_value.reshape(2 * blocks, span, ADAPTER_RANK)[2 * index + half]
     values = (
         kv[:, HEAD_SIZE:].astype(jnp.float32)
@@ -428,12 +459,15 @@
     short = hidden.shape[0] * ctx_count <= 1024
     if short:
         queries = adapt_queries(frozen_query, low, query_up)
-    for bit in bits:
-        if short and bit == bits[-1]:
-            kv, _ = lax.optimization_barrier((kv, queries))
+    for bit in bits[:-1]:
         low_value = jnp.concatenate([low_value, exchange(low_value, bit, 1)], axis=0)
         kv = jnp.concatenate([kv, exchange(kv, bit, 1)], axis=0)
+    if short:
+        kv, _ = lax.optimization_barrier((kv, queries))
+    last_low = exchange(low_value, bits[-1], 1)
+    last_kv = exchange(kv, bits[-1], 1)
     other_kv = exchange(kv, 0, 1)
+    last_other_kv = exchange(last_kv, 0, 1)
     if not short:
         return attend_long(
             patterns,
@@ -443,12 +477,59 @@
             frozen_query_rows,
             low,
             query_up_factor,
-            jnp.concatenate([kv, other_kv], axis=0),
-            low_value,
+            jnp.concatenate([kv, other_kv, last_kv, last_other_kv], axis=0),
+            jnp.concatenate([low_value, last_low], axis=0),
             value_up_factor,
         )
-    weights, top = make_weights(queries, bias, kv, other_kv)
-    return weigh_values(patterns, weights, top, kv, other_kv, low_value, value_up)
+    tok_dev, width = queries.shape
+    rows = width // HEAD_SIZE * tok_dev
+    key_count = 2 * kv.shape[0]
+    work = 6 * tok_dev * width * key_count
+    wide = jax.ShapeDtypeStruct((tok_dev, width), jnp.float32)
+    value_scratch = pltpu.VMEM((key_count, 2 * HEAD_SIZE), jnp.bfloat16)
+    first_top, sums = call(
+        first_kernel,
+        patterns,
+        (wide, jax.ShapeDtypeStruct((rows, 2 * HEAD_SIZE), jnp.float32)),
+        [pltpu.VMEM((rows, key_count), jnp.bfloat16), value_scratch],
+        30 * work,
+        queries,
+        bias,
+        kv,
+        other_kv,
+        low_value,
+        value_up,
+    )
+    weights, top, scale = call(
+        second_kernel,
+        patterns,
+        (jax.ShapeDtypeStruct((rows, key_count), jnp.bfloat16), wide, wide),
+        [],
+        30 * work,
+        queries,
+        bias,
+        last_kv,
+        last_other_kv,
+        first_top,
+    )
+    return call(
+        third_kernel,
+        patterns,
+        (
+            jax.ShapeDtypeStruct((tok_dev, width), jnp.bfloat16),
+            jax.ShapeDtypeStruct((width // HEAD_SIZE, tok_dev), jnp.float32),
+        ),
+        [value_scratch],
+        work,
+        weights,
+        top,
+        scale,
+        sums,
+        last_kv,
+        last_other_kv,
+        last_low,
+        value_up,
+    )
 
 
 def solution(mesh):

time: 24.6 us -> 22.8 us (0.927)
  starting transfers between devices: 14.5 us -> 13.3 us
  waiting for transfers between devices: 4.86 us -> 4 us
  Pallas kernels: 4.34 us -> 4.61 us
    ppermute x9 -> x10, starting transfers between devices: 14.5 us -> 13.3 us  [exchange(): return lax.ppermute(value, AXES, pairs)]
    ppermute x9 -> x10, waiting for transfers between devices: 4.86 us -> 4 us  [exchange(): return lax.ppermute(value, AXES, pairs)]
    pallas_call x2 -> x3, Pallas kernels: 2.41 us -> 2.67 us  [call(): pl.pallas_call(functools.partial(kernel, patterns), out_shape=out_shape,...]
  transfers between devices with their start and end apart: 9 -> 10, of which waited for: 4 -> 5; matrix products, arithmetic and copies ran while one was open for 0% -> 0% of each run, Pallas kernels for 1% -> 7%
where the time goes in v6:
time: 22.8 us; the launch traced here: 22.6 us
  starting transfers between devices  13.3 us (58%)
  Pallas kernels  4.61 us (20%)
  waiting for transfers between devices  4 us (18%)
  between operations  0.7 us (3%)
    ppermute x10, starting transfers between devices, exchange(): return lax.ppermute(value, AXES, pairs)  13.3 us
    ppermute x10, waiting for transfers between devices, exchange(): return lax.ppermute(value, AXES, pairs)  4 us
    pallas_call x3, Pallas kernels, call(): pl.pallas_call(functools.partial(kernel, patterns), out_shape=out_shape,...  2.67 us
    pallas_call x1, Pallas kernels, prologue(): pl.pallas_call(functools.partial(prologue_kernel, patterns), out_shape=(j...  1.7 us
  transfers between devices with their start and end apart: 10, of which 5 were waited for; matrix products, arithmetic and copies ran while one was open for 0% of the time, Pallas kernels for 7%

profile of v6, /device:TPU:0, one launch (start us, length us, event | category | flops | bytes accessed | tf_op | source)
XLA Modules:
  0.0 22.6 jit_solution(12349555087453031321)
XLA Ops:
  0.6 1.7 %shard_map.95 = (bf16[64,128]{1,0:T(8,128)(2,1)S(1)}, bf16[64,256]{1,0:T(8,128)(2,1)S(1)}, f32[128,1024]{1,0:T(8,128)S(1)}, bf16[128,768]{1,0:T(8,128)(2,1)S(1)}...) custom-call(bf16[128,2048]{1,0:T(8,128)(2,1)} %hidden_hbm.1, bf16[64,2048]{1,0:T(8,128)(2,1)} %bitcast.1, ...), custom_call_target="tpu_custom_call" | custom-call | flops 33554432 | bytes 1048576 | tf_op jit(solution)/shard_map/pallas_call | solution.py:141
  2.3 0.5 %collective-permute-start = (bf16[64,128]{1,0:T(8,128)(2,1)S(1)}, bf16[64,128]{1,0:T(8,128)(2,1)S(1)}, u32[]{:S(2)}, u32[]{:S(2)}) collective-permute-start(bf16[64,128]{1,0:T(8,128)(2,1)S(1)} %get-tuple-element.15), channel_id=1, source_target_pairs={{0,1},{1,0},{2,3},{3,2},{4,5},{5,4},{6,7},{7,6},{8,9},{9,8},{10,11... | collective-permute-start | bytes 49160 | tf_op jit(solution)/shard_map/ppermute | solution.py:28
  2.9 3.7 %collective-permute-start.2 = (bf16[64,256]{1,0:T(8,128)(2,1)S(1)}, bf16[64,256]{1,0:T(8,128)(2,1)S(1)}, u32[]{:S(2)}, u32[]{:S(2)}) collective-permute-start(bf16[64,256]{1,0:T(8,128)(2,1)S(1)} %get-tuple-element.18), channel_id=1, source_target_pairs={{0,17},{1,16},{2,19},{3,18},{4,21},{5,20},{6,23},{7,22},{8,25},{9,... | collective-permute-start | bytes 98312 | tf_op jit(solution)/shard_map/ppermute | solution.py:28
  6.6 0.0 collective-permute-done
  6.6 1.3 %collective-permute-start.1 = (bf16[64,128]{1,0:T(8,128)(2,1)S(1)}, bf16[64,128]{1,0:T(8,128)(2,1)S(1)}, u32[]{:S(2)}, u32[]{:S(2)}) collective-permute-start(bf16[64,128]{1,0:T(8,128)(2,1)S(1)} %add_convert_fusion.1), channel_id=1, source_target_pairs={{0,3},{1,2},{2,1},{3,0},{4,7},{5,6},{6,5},{7,4},{8,11},{9,10},{10,... | collective-permute-start | bytes 49160 | tf_op jit(solution)/shard_map/ppermute | solution.py:28
  7.8 0.4 %collective-permute-done.2 = bf16[64,256]{1,0:T(8,128)(2,1)S(1)} collective-permute-done((bf16[64,256]{1,0:T(8,128)(2,1)S(1)}, bf16[64,256]{1,0:T(8,128)(2,1)S(1)}, u32[]{:S(2)}, u32[]{:S(2)}) %collective-permute-start.2) | collective-permute-done | bytes 32800 | tf_op jit(solution)/shard_map/ppermute | solution.py:28
  8.2 1.5 %collective-permute-start.3 = (bf16[128,256]{1,0:T(8,128)(2,1)S(1)}, bf16[128,256]{1,0:T(8,128)(2,1)S(1)}, u32[]{:S(2)}, u32[]{:S(2)}) collective-permute-start(bf16[128,256]{1,0:T(8,128)(2,1)S(1)} %pad_maximum_fusion.1), channel_id=1, source_target_pairs={{0,5},{1,4},{2,7},{3,6},{4,1},{5,0},{6,3},{7,2},{8,13},{9,12},{10,... | collective-permute-start | bytes 196616 | tf_op jit(solution)/shard_map/ppermute | solution.py:28
  9.7 0.1 collective-permute-done.1
  9.8 2.2 %collective-permute-start.7 = (bf16[32,128]{1,0:T(8,128)(2,1)S(1)}, bf16[32,128]{1,0:T(8,128)(2,1)S(1)}, u32[]{:S(2)}, u32[]{:S(2)}) collective-permute-start(bf16[32,128]{1,0:T(8,128)(2,1)S(1)} %slice.4), channel_id=1, source_target_pairs={{0,17},{1,16},{2,19},{3,18},{4,21},{5,20},{6,23},{7,22},{8,25},{9,... | collective-permute-start | bytes 24584 | tf_op jit(solution)/shard_map/ppermute | solution.py:28
  12.1 0.2 %shard_map.96.queries_ref = bf16[128,768]{1,0:T(8,128)(2,1)S(1)} custom-call(bf16[128,768]{1,0:T(8,128)(2,1)S(1)} %get-tuple-element.14.frozen_query_ref, bf16[64,128]{1,0:T(8,128)(2,1)S(1)} %add_convert_fusion.low_ref, bf16[32,768]{1,0:T(8,128)(2,1)S(1)} %get-tuple-element.16.query_up_ref), custom_call_target="tpu_custom_call" | custom-call | flops 6291456 | bytes 393216 | tf_op jit(solution)/shard_map/pallas_call | solution.py:183
  12.3 0.0 collective-permute-done.3
  12.4 0.5 %collective-permute-start.6 = (bf16[256,256]{1,0:T(8,128)(2,1)S(1)}, bf16[256,256]{1,0:T(8,128)(2,1)S(1)}, u32[]{:S(2)}, u32[]{:S(2)}) collective-permute-start(bf16[256,256]{1,0:T(8,128)(2,1)S(1)} %pad_maximum_fusion.kv_ref), channel_id=1, source_target_pairs={{0,1},{1,0},{2,3},{3,2},{4,5},{5,4},{6,7},{7,6},{8,9},{9,8},{10,11... | collective-permute-start | bytes 393224 | tf_op jit(solution)/shard_map/ppermute | solution.py:28
  12.9 1.9 %collective-permute-start.4 = (bf16[256,256]{1,0:T(8,128)(2,1)S(1)}, bf16[256,256]{1,0:T(8,128)(2,1)S(1)}, u32[]{:S(2)}, u32[]{:S(2)}) collective-permute-start(bf16[256,256]{1,0:T(8,128)(2,1)S(1)} %pad_maximum_fusion.kv_ref), channel_id=1, source_target_pairs={{0,9},{1,8},{2,11},{3,10},{4,13},{5,12},{6,15},{7,14},{8,1},{9,0},... | collective-permute-start | bytes 393224 | tf_op jit(solution)/shard_map/ppermute | solution.py:28
  14.8 0.0 collective-permute-done.7
  14.8 0.6 %collective-permute-start.8 = (bf16[64,128]{1,0:T(8,128)(2,1)S(1)}, bf16[64,128]{1,0:T(8,128)(2,1)S(1)}, u32[]{:S(2)}, u32[]{:S(2)}) collective-permute-start(bf16[64,128]{1,0:T(8,128)(2,1)S(1)} %pad_maximum_fusion.3), channel_id=1, source_target_pairs={{0,5},{1,4},{2,7},{3,6},{4,1},{5,0},{6,3},{7,2},{8,13},{9,12},{10,... | collective-permute-start | bytes 49160 | tf_op jit(solution)/shard_map/ppermute | solution.py:28
  15.4 2.5 %collective-permute-done.8 = bf16[64,128]{1,0:T(8,128)(2,1)S(1)} collective-permute-done((bf16[64,128]{1,0:T(8,128)(2,1)S(1)}, bf16[64,128]{1,0:T(8,128)(2,1)S(1)}, u32[]{:S(2)}, u32[]{:S(2)}) %collective-permute-start.8) | collective-permute-done | bytes 16416 | tf_op jit(solution)/shard_map/ppermute | solution.py:28
  18.0 0.8 %collective-permute-start.9 = (bf16[128,128]{1,0:T(8,128)(2,1)S(1)}, bf16[128,128]{1,0:T(8,128)(2,1)S(1)}, u32[]{:S(2)}, u32[]{:S(2)}) collective-permute-start(bf16[128,128]{1,0:T(8,128)(2,1)S(1)} %pad_maximum_fusion.2.low_value_ref), channel_id=1, source_target_pairs={{0,9},{1,8},{2,11},{3,10},{4,13},{5,12},{6,15},{7,14},{8,1},{9,0},... | collective-permute-start | bytes 98312 | tf_op jit(solution)/shard_map/ppermute | solution.py:28
  18.8 0.0 collective-permute-done.4.kv_ref
  18.8 0.2 collective-permute-start.5
  19.0 0.0 collective-permute-done.6.other_kv_ref
  19.0 0.8 %shard_map.97 = (f32[128,768]{1,0:T(8,128)S(1)}, f32[768,256]{1,0:T(8,128)S(1)}) custom-call(bf16[128,768]{1,0:T(8,128)(2,1)S(1)} %shard_map.96.queries_ref, f32[128,1024]{1,0:T(8,128)S(1)} %get-tuple-element.17.bias_ref, bf16[256,256]{1,0:T(8,128)(2,1)S(1)} %pad_maximum_fusion.kv_ref, bf16[256,256]{1,0:T(8,128)(2,1)S(1)} %collective-permute-done.6.other_kv_ref, ...), custom_call_target="tpu_custom_call" | custom-call | flops 9059696640 | bytes 23592960 | tf_op jit(solution)/shard_map/pallas_call | solution.py:343
  19.8 0.4 %collective-permute-done.5.other_kv_ref = bf16[256,256]{1,0:T(8,128)(2,1)S(1)} collective-permute-done((bf16[256,256]{1,0:T(8,128)(2,1)S(1)}, bf16[256,256]{1,0:T(8,128)(2,1)S(1)}, u32[]{:S(2)}, u32[]{:S(2)}) %collective-permute-start.5) | collective-permute-done | bytes 131104 | tf_op jit(solution)/shard_map/ppermute | solution.py:28
  20.2 0.6 %shard_map.98 = (bf16[768,512]{1,0:T(8,128)(2,1)S(1)}, f32[128,768]{1,0:T(8,128)S(1)}, f32[128,768]{1,0:T(8,128)S(1)}) custom-call(bf16[128,768]{1,0:T(8,128)(2,1)S(1)} %shard_map.96.queries_ref, f32[128,1024]{1,0:T(8,128)S(1)} %get-tuple-element.17.bias_ref, bf16[256,256]{1,0:T(8,128)(2,1)S(1)} %collective-permute-done.4.kv_ref, ...), custom_call_target="tpu_custom_call" | custom-call | flops 9059696640 | bytes 23592960 | tf_op jit(solution)/shard_map/pallas_call | solution.py:343
  20.8 0.6 %collective-permute-done.9.low_value_ref = bf16[128,128]{1,0:T(8,128)(2,1)S(1)} collective-permute-done((bf16[128,128]{1,0:T(8,128)(2,1)S(1)}, bf16[128,128]{1,0:T(8,128)(2,1)S(1)}, u32[]{:S(2)}, u32[]{:S(2)}) %collective-permute-start.9) | collective-permute-done | bytes 32800 | tf_op jit(solution)/shard_map/ppermute | solution.py:28
  21.3 1.3 %shard_map.99 = (bf16[128,768]{1,0:T(8,128)(2,1)}, f32[6,128]{1,0:T(8,128)}) custom-call(bf16[768,512]{1,0:T(8,128)(2,1)S(1)} %get-tuple-element.22.weights_ref, f32[128,768]{1,0:T(8,128)S(1)} %get-tuple-element.23.top_ref, f32[128,768]{1,0:T(8,128)S(1)} %get-tuple-element.24.scale_ref, f32[768,256]{1,0:T(8,128)S(1)} %get-tuple-element.25.first_sums_ref, ...), custom_call_target="tpu_custom_call" | custom-call | flops 301989888 | bytes 786432 | tf_op jit(solution)/shard_map/pallas_call | solution.py:343
  (7 shorter events, 0.0 us)
Async XLA Ops:
  2.3 4.2 %collective-permute-start = (bf16[64,128]{1,0:T(8,128)(2,1)S(1)}, bf16[64,128]{1,0:T(8,128)(2,1)S(1)}, u32[]{:S(2)}, u32[]{:S(2)}) collective-permute-start(bf16[64,128]{1,0:T(8,128)(2,1)S(1)} %get-tuple-element.15), channel_id=1, source_target_pairs={{0,1},{1,0},{2,3},{3,2},{4,5},{5,4},{6,7},{7,6},{8,9},{9,8},{10,11... | collective-permute-start | bytes 49160 | tf_op jit(solution)/shard_map/ppermute | solution.py:28
  2.9 5.4 %collective-permute-start.2 = (bf16[64,256]{1,0:T(8,128)(2,1)S(1)}, bf16[64,256]{1,0:T(8,128)(2,1)S(1)}, u32[]{:S(2)}, u32[]{:S(2)}) collective-permute-start(bf16[64,256]{1,0:T(8,128)(2,1)S(1)} %get-tuple-element.18), channel_id=1, source_target_pairs={{0,17},{1,16},{2,19},{3,18},{4,21},{5,20},{6,23},{7,22},{8,25},{9,... | collective-permute-start | bytes 98312 | tf_op jit(solution)/shard_map/ppermute | solution.py:28
  6.6 3.2 %collective-permute-start.1 = (bf16[64,128]{1,0:T(8,128)(2,1)S(1)}, bf16[64,128]{1,0:T(8,128)(2,1)S(1)}, u32[]{:S(2)}, u32[]{:S(2)}) collective-permute-start(bf16[64,128]{1,0:T(8,128)(2,1)S(1)} %add_convert_fusion.1), channel_id=1, source_target_pairs={{0,3},{1,2},{2,1},{3,0},{4,7},{5,6},{6,5},{7,4},{8,11},{9,10},{10,... | collective-permute-start | bytes 49160 | tf_op jit(solution)/shard_map/ppermute | solution.py:28
  8.2 4.1 %collective-permute-start.3 = (bf16[128,256]{1,0:T(8,128)(2,1)S(1)}, bf16[128,256]{1,0:T(8,128)(2,1)S(1)}, u32[]{:S(2)}, u32[]{:S(2)}) collective-permute-start(bf16[128,256]{1,0:T(8,128)(2,1)S(1)} %pad_maximum_fusion.1), channel_id=1, source_target_pairs={{0,5},{1,4},{2,7},{3,6},{4,1},{5,0},{6,3},{7,2},{8,13},{9,12},{10,... | collective-permute-start | bytes 196616 | tf_op jit(solution)/shard_map/ppermute | solution.py:28
  9.8 5.0 %collective-permute-start.7 = (bf16[32,128]{1,0:T(8,128)(2,1)S(1)}, bf16[32,128]{1,0:T(8,128)(2,1)S(1)}, u32[]{:S(2)}, u32[]{:S(2)}) collective-permute-start(bf16[32,128]{1,0:T(8,128)(2,1)S(1)} %slice.4), channel_id=1, source_target_pairs={{0,17},{1,16},{2,19},{3,18},{4,21},{5,20},{6,23},{7,22},{8,25},{9,... | collective-permute-start | bytes 24584 | tf_op jit(solution)/shard_map/ppermute | solution.py:28
  12.4 6.6 %collective-permute-start.6 = (bf16[256,256]{1,0:T(8,128)(2,1)S(1)}, bf16[256,256]{1,0:T(8,128)(2,1)S(1)}, u32[]{:S(2)}, u32[]{:S(2)}) collective-permute-start(bf16[256,256]{1,0:T(8,128)(2,1)S(1)} %pad_maximum_fusion.kv_ref), channel_id=1, source_target_pairs={{0,1},{1,0},{2,3},{3,2},{4,5},{5,4},{6,7},{7,6},{8,9},{9,8},{10,11... | collective-permute-start | bytes 393224 | tf_op jit(solution)/shard_map/ppermute | solution.py:28
  12.9 6.0 %collective-permute-start.4 = (bf16[256,256]{1,0:T(8,128)(2,1)S(1)}, bf16[256,256]{1,0:T(8,128)(2,1)S(1)}, u32[]{:S(2)}, u32[]{:S(2)}) collective-permute-start(bf16[256,256]{1,0:T(8,128)(2,1)S(1)} %pad_maximum_fusion.kv_ref), channel_id=1, source_target_pairs={{0,9},{1,8},{2,11},{3,10},{4,13},{5,12},{6,15},{7,14},{8,1},{9,0},... | collective-permute-start | bytes 393224 | tf_op jit(solution)/shard_map/ppermute | solution.py:28
  14.8 3.2 %collective-permute-start.8 = (bf16[64,128]{1,0:T(8,128)(2,1)S(1)}, bf16[64,128]{1,0:T(8,128)(2,1)S(1)}, u32[]{:S(2)}, u32[]{:S(2)}) collective-permute-start(bf16[64,128]{1,0:T(8,128)(2,1)S(1)} %pad_maximum_fusion.3), channel_id=1, source_target_pairs={{0,5},{1,4},{2,7},{3,6},{4,1},{5,0},{6,3},{7,2},{8,13},{9,12},{10,... | collective-permute-start | bytes 49160 | tf_op jit(solution)/shard_map/ppermute | solution.py:28
  18.0 3.4 %collective-permute-start.9 = (bf16[128,128]{1,0:T(8,128)(2,1)S(1)}, bf16[128,128]{1,0:T(8,128)(2,1)S(1)}, u32[]{:S(2)}, u32[]{:S(2)}) collective-permute-start(bf16[128,128]{1,0:T(8,128)(2,1)S(1)} %pad_maximum_fusion.2.low_value_ref), channel_id=1, source_target_pairs={{0,9},{1,8},{2,11},{3,10},{4,13},{5,12},{6,15},{7,14},{8,1},{9,0},... | collective-permute-start | bytes 98312 | tf_op jit(solution)/shard_map/ppermute | solution.py:28
  18.8 1.3 %collective-permute-start.5 = (bf16[256,256]{1,0:T(8,128)(2,1)S(1)}, bf16[256,256]{1,0:T(8,128)(2,1)S(1)}, u32[]{:S(2)}, u32[]{:S(2)}) collective-permute-start(bf16[256,256]{1,0:T(8,128)(2,1)S(1)} %collective-permute-done.4.kv_ref), channel_id=1, source_target_pairs={{0,1},{1,0},{2,3},{3,2},{4,5},{5,4},{6,7},{7,6},{8,9},{9,8},{10,11... | collective-permute-start | bytes 393224 | tf_op jit(solution)/shard_map/ppermute | solution.py:28

commit v7 on v6

--- a/solution.py
+++ b/solution.py
@@ -164,36 +164,6 @@
     )(*(pltpu.with_memory_space_constraint(x, pltpu.HBM) for x in operands))
 
 
-def queries_kernel(frozen_query_ref, low_ref, query_up_ref, queries_ref):
-    queries_ref[...] = (
-        frozen_query_ref[...].astype(jnp.float32)
-        + ADAPTER_SCALE
-        * lax.dot_general(
-            low_ref[:ADAPTER_RANK, :],
-            query_up_ref[...],
-            (((0,), (0,)), ((), ())),
-            preferred_element_type=jnp.float32,
-        )
-    ).astype(jnp.bfloat16)
-
-
-def adapt_queries(frozen_query, low, query_up):
-    tok_dev, width = frozen_query.shape
-    vmem = pl.BlockSpec(memory_space=pltpu.VMEM)
-    return pl.pallas_call(
-        queries_kernel,
-        out_shape=jax.ShapeDtypeStruct((tok_dev, width), jnp.bfloat16),
-        in_specs=[vmem] * 3,
-        out_specs=vmem,
-        compiler_params=pltpu.CompilerParams(vmem_limit_bytes=VMEM_LIMIT),
-        cost_estimate=pl.CostEstimate(
-            flops=2 * tok_dev * width * ADAPTER_RANK,
-            bytes_accessed=4 * tok_dev * width,
-            transcendentals=0,
-        ),
-    )(frozen_query, low, query_up)
-
-
 def fill_values(value_ref, patterns, kv_refs, low_value_ref, value_up_ref):
     span = value_ref.shape[0] // (2 * len(patterns))
     side = lax.axis_index("head") % 2
@@ -232,17 +202,30 @@
 
 def first_kernel(
     patterns,
-    queries_ref,
+    frozen_query_ref,
+    low_ref,
+    query_up_ref,
     bias_ref,
     kv_ref,
     other_kv_ref,
     low_value_ref,
     value_up_ref,
+    queries_ref,
     top_ref,
     sums_ref,
     weights_ref,
     value_ref,
 ):
+    queries_ref[...] = (
+        frozen_query_ref[...].astype(jnp.float32)
+        + ADAPTER_SCALE
+        * lax.dot_general(
+            low_ref[:ADAPTER_RANK, :],
+            query_up_ref[...],
+            (((0,), (0,)), ((), ())),
+            preferred_element_type=jnp.float32,
+        )
+    ).astype(jnp.bfloat16)
     tok_dev, width = queries_ref.shape
     heads = width // HEAD_SIZE
     count = kv_ref.shape[0]
@@ -457,13 +440,11 @@
         head_bit *= 2
     low_value = low[ADAPTER_RANK:]
     short = hidden.shape[0] * ctx_count <= 1024
-    if short:
-        queries = adapt_queries(frozen_query, low, query_up)
     for bit in bits[:-1]:
         low_value = jnp.concatenate([low_value, exchange(low_value, bit, 1)], axis=0)
         kv = jnp.concatenate([kv, exchange(kv, bit, 1)], axis=0)
     if short:
-        kv, _ = lax.optimization_barrier((kv, queries))
+        kv, _ = lax.optimization_barrier((kv, low))
     last_low = exchange(low_value, bits[-1], 1)
     last_kv = exchange(kv, bits[-1], 1)
     other_kv = exchange(kv, 0, 1)
@@ -481,19 +462,21 @@
             jnp.concatenate([low_value, last_low], axis=0),
             value_up_factor,
         )
-    tok_dev, width = queries.shape
+    tok_dev, width = frozen_query.shape
     rows = width // HEAD_SIZE * tok_dev
     key_count = 2 * kv.shape[0]
     work = 6 * tok_dev * width * key_count
     wide = jax.ShapeDtypeStruct((tok_dev, width), jnp.float32)
     value_scratch = pltpu.VMEM((key_count, 2 * HEAD_SIZE), jnp.bfloat16)
-    first_top, sums = call(
+    queries, first_top, sums = call(
         first_kernel,
         patterns,
-        (wide, jax.ShapeDtypeStruct((rows, 2 * HEAD_SIZE), jnp.float32)),
+        (jax.ShapeDtypeStruct((tok_dev, width), jnp.bfloat16), wide, jax.ShapeDtypeStruct((rows, 2 * HEAD_SIZE), jnp.float32)),
         [pltpu.VMEM((rows, key_count), jnp.bfloat16), value_scratch],
         30 * work,
-        queries,
+        frozen_query,
+        low,
+        query_up,
         bias,
         kv,
         other_kv,

time: 22.8 us -> 22.6 us (level)
  waiting for transfers between devices: 4 us -> 3.65 us
  starting transfers between devices: 13.3 us -> 13.6 us
    ppermute x10, waiting for transfers between devices: 4 us -> 3.65 us  [exchange(): return lax.ppermute(value, AXES, pairs)]
    ppermute x10, starting transfers between devices: 13.3 us -> 13.6 us  [exchange(): return lax.ppermute(value, AXES, pairs)]
    pallas_call x1 -> x0, Pallas kernels: 0.24 us -> none  [adapt_queries(): pl.pallas_call(queries_kernel, out_shape=jax.ShapeDtypeStruct((tok_dev, w...]
  transfers between devices with their start and end apart: 10 -> 10, of which waited for: 5 -> 6; matrix products, arithmetic and copies ran while one was open for 0% -> 0% of each run, Pallas kernels for 7% -> 7%
where the time goes in v7:
time: 22.6 us; the launch traced here: 22.4 us
  starting transfers between devices  13.6 us (60%)
  Pallas kernels  4.47 us (20%)
  waiting for transfers between devices  3.65 us (16%)
  between operations  0.69 us (3%)
    ppermute x10, starting transfers between devices, exchange(): return lax.ppermute(value, AXES, pairs)  13.6 us
    ppermute x10, waiting for transfers between devices, exchange(): return lax.ppermute(value, AXES, pairs)  3.65 us
    pallas_call x3, Pallas kernels, call(): pl.pallas_call(functools.partial(kernel, patterns), out_shape=out_shape,...  2.77 us
    pallas_call x1, Pallas kernels, prologue(): pl.pallas_call(functools.partial(prologue_kernel, patterns), out_shape=(j...  1.7 us
  transfers between devices with their start and end apart: 10, of which 6 were waited for; matrix products, arithmetic and copies ran while one was open for 0% of the time, Pallas kernels for 7%

profile of v7, /device:TPU:0, one launch (start us, length us, event | category | flops | bytes accessed | tf_op | source)
XLA Modules:
  0.0 22.4 jit_solution(14598923262664929459)
XLA Ops:
  0.6 1.7 %shard_map.95 = (bf16[64,128]{1,0:T(8,128)(2,1)S(1)}, bf16[64,256]{1,0:T(8,128)(2,1)S(1)}, f32[128,1024]{1,0:T(8,128)S(1)}, bf16[128,768]{1,0:T(8,128)(2,1)S(1)}...) custom-call(bf16[128,2048]{1,0:T(8,128)(2,1)} %hidden_hbm.1, bf16[64,2048]{1,0:T(8,128)(2,1)} %bitcast.1, ...), custom_call_target="tpu_custom_call" | custom-call | flops 33554432 | bytes 1048576 | tf_op jit(solution)/shard_map/pallas_call | solution.py:141
  2.3 0.5 %collective-permute-start = (bf16[64,128]{1,0:T(8,128)(2,1)S(1)}, bf16[64,128]{1,0:T(8,128)(2,1)S(1)}, u32[]{:S(2)}, u32[]{:S(2)}) collective-permute-start(bf16[64,128]{1,0:T(8,128)(2,1)S(1)} %get-tuple-element.16), channel_id=1, source_target_pairs={{0,1},{1,0},{2,3},{3,2},{4,5},{5,4},{6,7},{7,6},{8,9},{9,8},{10,11... | collective-permute-start | bytes 49160 | tf_op jit(solution)/shard_map/ppermute | solution.py:28
  2.9 3.7 %collective-permute-start.2 = (bf16[64,256]{1,0:T(8,128)(2,1)S(1)}, bf16[64,256]{1,0:T(8,128)(2,1)S(1)}, u32[]{:S(2)}, u32[]{:S(2)}) collective-permute-start(bf16[64,256]{1,0:T(8,128)(2,1)S(1)} %get-tuple-element.19), channel_id=1, source_target_pairs={{0,17},{1,16},{2,19},{3,18},{4,21},{5,20},{6,23},{7,22},{8,25},{9,... | collective-permute-start | bytes 98312 | tf_op jit(solution)/shard_map/ppermute | solution.py:28
  6.6 0.0 collective-permute-done
  6.6 1.3 %collective-permute-start.1 = (bf16[64,128]{1,0:T(8,128)(2,1)S(1)}, bf16[64,128]{1,0:T(8,128)(2,1)S(1)}, u32[]{:S(2)}, u32[]{:S(2)}) collective-permute-start(bf16[64,128]{1,0:T(8,128)(2,1)S(1)} %add_convert_fusion.1), channel_id=1, source_target_pairs={{0,3},{1,2},{2,1},{3,0},{4,7},{5,6},{6,5},{7,4},{8,11},{9,10},{10,... | collective-permute-start | bytes 49160 | tf_op jit(solution)/shard_map/ppermute | solution.py:28
  7.8 0.4 %collective-permute-done.2 = bf16[64,256]{1,0:T(8,128)(2,1)S(1)} collective-permute-done((bf16[64,256]{1,0:T(8,128)(2,1)S(1)}, bf16[64,256]{1,0:T(8,128)(2,1)S(1)}, u32[]{:S(2)}, u32[]{:S(2)}) %collective-permute-start.2) | collective-permute-done | bytes 32800 | tf_op jit(solution)/shard_map/ppermute | solution.py:28
  8.2 1.5 %collective-permute-start.3 = (bf16[128,256]{1,0:T(8,128)(2,1)S(1)}, bf16[128,256]{1,0:T(8,128)(2,1)S(1)}, u32[]{:S(2)}, u32[]{:S(2)}) collective-permute-start(bf16[128,256]{1,0:T(8,128)(2,1)S(1)} %pad_maximum_fusion.1), channel_id=1, source_target_pairs={{0,5},{1,4},{2,7},{3,6},{4,1},{5,0},{6,3},{7,2},{8,13},{9,12},{10,... | collective-permute-start | bytes 196616 | tf_op jit(solution)/shard_map/ppermute | solution.py:28
  9.7 0.1 collective-permute-done.1
  9.8 2.2 %collective-permute-start.5 = (bf16[32,128]{1,0:T(8,128)(2,1)S(1)}, bf16[32,128]{1,0:T(8,128)(2,1)S(1)}, u32[]{:S(2)}, u32[]{:S(2)}) collective-permute-start(bf16[32,128]{1,0:T(8,128)(2,1)S(1)} %slice.4), channel_id=1, source_target_pairs={{0,17},{1,16},{2,19},{3,18},{4,21},{5,20},{6,23},{7,22},{8,25},{9,... | collective-permute-start | bytes 24584 | tf_op jit(solution)/shard_map/ppermute | solution.py:28
  12.1 0.2 %collective-permute-done.3 = bf16[128,256]{1,0:T(8,128)(2,1)S(1)} collective-permute-done((bf16[128,256]{1,0:T(8,128)(2,1)S(1)}, bf16[128,256]{1,0:T(8,128)(2,1)S(1)}, u32[]{:S(2)}, u32[]{:S(2)}) %collective-permute-start.3) | collective-permute-done | bytes 65568 | tf_op jit(solution)/shard_map/ppermute | solution.py:28
  12.3 1.8 %collective-permute-start.7 = (bf16[256,256]{1,0:T(8,128)(2,1)S(1)}, bf16[256,256]{1,0:T(8,128)(2,1)S(1)}, u32[]{:S(2)}, u32[]{:S(2)}) collective-permute-start(bf16[256,256]{1,0:T(8,128)(2,1)S(1)} %pad_maximum_fusion.kv_ref), channel_id=1, source_target_pairs={{0,9},{1,8},{2,11},{3,10},{4,13},{5,12},{6,15},{7,14},{8,1},{9,0},... | collective-permute-start | bytes 393224 | tf_op jit(solution)/shard_map/ppermute | solution.py:28
  14.1 0.4 %collective-permute-start.4 = (bf16[256,256]{1,0:T(8,128)(2,1)S(1)}, bf16[256,256]{1,0:T(8,128)(2,1)S(1)}, u32[]{:S(2)}, u32[]{:S(2)}) collective-permute-start(bf16[256,256]{1,0:T(8,128)(2,1)S(1)} %pad_maximum_fusion.kv_ref), channel_id=1, source_target_pairs={{0,1},{1,0},{2,3},{3,2},{4,5},{5,4},{6,7},{7,6},{8,9},{9,8},{10,11... | collective-permute-start | bytes 393224 | tf_op jit(solution)/shard_map/ppermute | solution.py:28
  14.5 0.0 collective-permute-done.5
  14.5 0.9 %collective-permute-start.6 = (bf16[64,128]{1,0:T(8,128)(2,1)S(1)}, bf16[64,128]{1,0:T(8,128)(2,1)S(1)}, u32[]{:S(2)}, u32[]{:S(2)}) collective-permute-start(bf16[64,128]{1,0:T(8,128)(2,1)S(1)} %pad_maximum_fusion.3), channel_id=1, source_target_pairs={{0,5},{1,4},{2,7},{3,6},{4,1},{5,0},{6,3},{7,2},{8,13},{9,12},{10,... | collective-permute-start | bytes 49160 | tf_op jit(solution)/shard_map/ppermute | solution.py:28
  15.4 2.3 %collective-permute-done.6 = bf16[64,128]{1,0:T(8,128)(2,1)S(1)} collective-permute-done((bf16[64,128]{1,0:T(8,128)(2,1)S(1)}, bf16[64,128]{1,0:T(8,128)(2,1)S(1)}, u32[]{:S(2)}, u32[]{:S(2)}) %collective-permute-start.6) | collective-permute-done | bytes 16416 | tf_op jit(solution)/shard_map/ppermute | solution.py:28
  17.7 1.1 %collective-permute-start.9 = (bf16[128,128]{1,0:T(8,128)(2,1)S(1)}, bf16[128,128]{1,0:T(8,128)(2,1)S(1)}, u32[]{:S(2)}, u32[]{:S(2)}) collective-permute-start(bf16[128,128]{1,0:T(8,128)(2,1)S(1)} %pad_maximum_fusion.2.low_value_ref), channel_id=1, source_target_pairs={{0,9},{1,8},{2,11},{3,10},{4,13},{5,12},{6,15},{7,14},{8,1},{9,0},... | collective-permute-start | bytes 98312 | tf_op jit(solution)/shard_map/ppermute | solution.py:28
  18.8 0.0 collective-permute-done.7.kv_ref
  18.8 0.2 collective-permute-start.8
  19.0 0.0 collective-permute-done.4.other_kv_ref
  19.0 0.9 %shard_map.96 = (bf16[128,768]{1,0:T(8,128)(2,1)S(1)}, f32[128,768]{1,0:T(8,128)S(1)}, f32[768,256]{1,0:T(8,128)S(1)}) custom-call(bf16[128,768]{1,0:T(8,128)(2,1)S(1)} %get-tuple-element.15.frozen_query_ref, bf16[64,128]{1,0:T(8,128)(2,1)S(1)} %add_convert_fusion.low_ref, bf16[32,768]{1,0:T(8,128)(2,1)S(1)} %get-tuple-element.17.query_up_ref, ...), custom_call_target="tpu_custom_call" | custom-call | flops 9059696640 | bytes 23592960 | tf_op jit(solution)/shard_map/pallas_call | solution.py:326
  19.9 0.3 %collective-permute-done.8.other_kv_ref = bf16[256,256]{1,0:T(8,128)(2,1)S(1)} collective-permute-done((bf16[256,256]{1,0:T(8,128)(2,1)S(1)}, bf16[256,256]{1,0:T(8,128)(2,1)S(1)}, u32[]{:S(2)}, u32[]{:S(2)}) %collective-permute-start.8) | collective-permute-done | bytes 131104 | tf_op jit(solution)/shard_map/ppermute | solution.py:28
  20.2 0.6 %shard_map.97 = (bf16[768,512]{1,0:T(8,128)(2,1)S(1)}, f32[128,768]{1,0:T(8,128)S(1)}, f32[128,768]{1,0:T(8,128)S(1)}) custom-call(bf16[128,768]{1,0:T(8,128)(2,1)S(1)} %get-tuple-element.22.queries_ref, f32[128,1024]{1,0:T(8,128)S(1)} %get-tuple-element.18.bias_ref, bf16[256,256]{1,0:T(8,128)(2,1)S(1)} %collective-permute-done.7.kv_ref, ...), custom_call_target="tpu_custom_call" | custom-call | flops 9059696640 | bytes 23592960 | tf_op jit(solution)/shard_map/pallas_call | solution.py:326
  20.8 0.3 %collective-permute-done.9.low_value_ref = bf16[128,128]{1,0:T(8,128)(2,1)S(1)} collective-permute-done((bf16[128,128]{1,0:T(8,128)(2,1)S(1)}, bf16[128,128]{1,0:T(8,128)(2,1)S(1)}, u32[]{:S(2)}, u32[]{:S(2)}) %collective-permute-start.9) | collective-permute-done | bytes 32800 | tf_op jit(solution)/shard_map/ppermute | solution.py:28
  21.1 1.3 %shard_map.98 = (bf16[128,768]{1,0:T(8,128)(2,1)}, f32[6,128]{1,0:T(8,128)}) custom-call(bf16[768,512]{1,0:T(8,128)(2,1)S(1)} %get-tuple-element.24.weights_ref, f32[128,768]{1,0:T(8,128)S(1)} %get-tuple-element.25.top_ref, f32[128,768]{1,0:T(8,128)S(1)} %get-tuple-element.26.scale_ref, f32[768,256]{1,0:T(8,128)S(1)} %get-tuple-element.27.first_sums_ref, ...), custom_call_target="tpu_custom_call" | custom-call | flops 301989888 | bytes 786432 | tf_op jit(solution)/shard_map/pallas_call | solution.py:326
  (7 shorter events, 0.0 us)
Async XLA Ops:
  2.3 4.2 %collective-permute-start = (bf16[64,128]{1,0:T(8,128)(2,1)S(1)}, bf16[64,128]{1,0:T(8,128)(2,1)S(1)}, u32[]{:S(2)}, u32[]{:S(2)}) collective-permute-start(bf16[64,128]{1,0:T(8,128)(2,1)S(1)} %get-tuple-element.16), channel_id=1, source_target_pairs={{0,1},{1,0},{2,3},{3,2},{4,5},{5,4},{6,7},{7,6},{8,9},{9,8},{10,11... | collective-permute-start | bytes 49160 | tf_op jit(solution)/shard_map/ppermute | solution.py:28
  2.9 5.4 %collective-permute-start.2 = (bf16[64,256]{1,0:T(8,128)(2,1)S(1)}, bf16[64,256]{1,0:T(8,128)(2,1)S(1)}, u32[]{:S(2)}, u32[]{:S(2)}) collective-permute-start(bf16[64,256]{1,0:T(8,128)(2,1)S(1)} %get-tuple-element.19), channel_id=1, source_target_pairs={{0,17},{1,16},{2,19},{3,18},{4,21},{5,20},{6,23},{7,22},{8,25},{9,... | collective-permute-start | bytes 98312 | tf_op jit(solution)/shard_map/ppermute | solution.py:28
  6.6 3.2 %collective-permute-start.1 = (bf16[64,128]{1,0:T(8,128)(2,1)S(1)}, bf16[64,128]{1,0:T(8,128)(2,1)S(1)}, u32[]{:S(2)}, u32[]{:S(2)}) collective-permute-start(bf16[64,128]{1,0:T(8,128)(2,1)S(1)} %add_convert_fusion.1), channel_id=1, source_target_pairs={{0,3},{1,2},{2,1},{3,0},{4,7},{5,6},{6,5},{7,4},{8,11},{9,10},{10,... | collective-permute-start | bytes 49160 | tf_op jit(solution)/shard_map/ppermute | solution.py:28
  8.2 4.1 %collective-permute-start.3 = (bf16[128,256]{1,0:T(8,128)(2,1)S(1)}, bf16[128,256]{1,0:T(8,128)(2,1)S(1)}, u32[]{:S(2)}, u32[]{:S(2)}) collective-permute-start(bf16[128,256]{1,0:T(8,128)(2,1)S(1)} %pad_maximum_fusion.1), channel_id=1, source_target_pairs={{0,5},{1,4},{2,7},{3,6},{4,1},{5,0},{6,3},{7,2},{8,13},{9,12},{10,... | collective-permute-start | bytes 196616 | tf_op jit(solution)/shard_map/ppermute | solution.py:28
  9.8 4.7 %collective-permute-start.5 = (bf16[32,128]{1,0:T(8,128)(2,1)S(1)}, bf16[32,128]{1,0:T(8,128)(2,1)S(1)}, u32[]{:S(2)}, u32[]{:S(2)}) collective-permute-start(bf16[32,128]{1,0:T(8,128)(2,1)S(1)} %slice.4), channel_id=1, source_target_pairs={{0,17},{1,16},{2,19},{3,18},{4,21},{5,20},{6,23},{7,22},{8,25},{9,... | collective-permute-start | bytes 24584 | tf_op jit(solution)/shard_map/ppermute | solution.py:28
  12.3 6.5 %collective-permute-start.7 = (bf16[256,256]{1,0:T(8,128)(2,1)S(1)}, bf16[256,256]{1,0:T(8,128)(2,1)S(1)}, u32[]{:S(2)}, u32[]{:S(2)}) collective-permute-start(bf16[256,256]{1,0:T(8,128)(2,1)S(1)} %pad_maximum_fusion.kv_ref), channel_id=1, source_target_pairs={{0,9},{1,8},{2,11},{3,10},{4,13},{5,12},{6,15},{7,14},{8,1},{9,0},... | collective-permute-start | bytes 393224 | tf_op jit(solution)/shard_map/ppermute | solution.py:28
  14.1 4.9 %collective-permute-start.4 = (bf16[256,256]{1,0:T(8,128)(2,1)S(1)}, bf16[256,256]{1,0:T(8,128)(2,1)S(1)}, u32[]{:S(2)}, u32[]{:S(2)}) collective-permute-start(bf16[256,256]{1,0:T(8,128)(2,1)S(1)} %pad_maximum_fusion.kv_ref), channel_id=1, source_target_pairs={{0,1},{1,0},{2,3},{3,2},{4,5},{5,4},{6,7},{7,6},{8,9},{9,8},{10,11... | collective-permute-start | bytes 393224 | tf_op jit(solution)/shard_map/ppermute | solution.py:28
  14.5 3.2 %collective-permute-start.6 = (bf16[64,128]{1,0:T(8,128)(2,1)S(1)}, bf16[64,128]{1,0:T(8,128)(2,1)S(1)}, u32[]{:S(2)}, u32[]{:S(2)}) collective-permute-start(bf16[64,128]{1,0:T(8,128)(2,1)S(1)} %pad_maximum_fusion.3), channel_id=1, source_target_pairs={{0,5},{1,4},{2,7},{3,6},{4,1},{5,0},{6,3},{7,2},{8,13},{9,12},{10,... | collective-permute-start | bytes 49160 | tf_op jit(solution)/shard_map/ppermute | solution.py:28
  17.7 3.4 %collective-permute-start.9 = (bf16[128,128]{1,0:T(8,128)(2,1)S(1)}, bf16[128,128]{1,0:T(8,128)(2,1)S(1)}, u32[]{:S(2)}, u32[]{:S(2)}) collective-permute-start(bf16[128,128]{1,0:T(8,128)(2,1)S(1)} %pad_maximum_fusion.2.low_value_ref), channel_id=1, source_target_pairs={{0,9},{1,8},{2,11},{3,10},{4,13},{5,12},{6,15},{7,14},{8,1},{9,0},... | collective-permute-start | bytes 98312 | tf_op jit(solution)/shard_map/ppermute | solution.py:28
  18.8 1.3 %collective-permute-start.8 = (bf16[256,256]{1,0:T(8,128)(2,1)S(1)}, bf16[256,256]{1,0:T(8,128)(2,1)S(1)}, u32[]{:S(2)}, u32[]{:S(2)}) collective-permute-start(bf16[256,256]{1,0:T(8,128)(2,1)S(1)} %collective-permute-done.7.kv_ref), channel_id=1, source_target_pairs={{0,1},{1,0},{2,3},{3,2},{4,5},{5,4},{6,7},{7,6},{8,9},{9,8},{10,11... | collective-permute-start | bytes 393224 | tf_op jit(solution)/shard_map/ppermute | solution.py:28

commit v8 on v7

--- a/solution.py
+++ b/solution.py
@@ -418,8 +418,6 @@
     ctx_count, head_count = lax.axis_size("ctx"), lax.axis_size("head")
     ctx, head = lax.axis_index("ctx"), lax.axis_index("head")
     bits = [ctx_count >> k for k in range(1, ctx_count.bit_length())]
-    if len(bits) == 3:
-        bits = [bits[0], bits[2], bits[1]]
     patterns = gather_patterns(bits)
 
     low, kv, bias, frozen_query, query_up, value_up = prologue(

time: 22.6 us -> 22.5 us (level)
  waiting for transfers between devices: 3.65 us -> 3.29 us
  starting transfers between devices: 13.6 us -> 13.9 us
    ppermute x10, waiting for transfers between devices: 3.65 us -> 3.29 us  [exchange(): return lax.ppermute(value, AXES, pairs)]
    ppermute x10, starting transfers between devices: 13.6 us -> 13.9 us  [exchange(): return lax.ppermute(value, AXES, pairs)]
  transfers between devices with their start and end apart: 10 -> 10, of which waited for: 6 -> 4; matrix products, arithmetic and copies ran while one was open for 0% -> 0% of each run, Pallas kernels for 7% -> 7%
where the time goes in v8:
time: 22.5 us; the launch traced here: 22.4 us
  starting transfers between devices  13.9 us (62%)
  Pallas kernels  4.46 us (20%)
  waiting for transfers between devices  3.29 us (15%)
  between operations  0.69 us (3%)
    ppermute x10, starting transfers between devices, exchange(): return lax.ppermute(value, AXES, pairs)  13.9 us
    ppermute x10, waiting for transfers between devices, exchange(): return lax.ppermute(value, AXES, pairs)  3.29 us
    pallas_call x3, Pallas kernels, call(): pl.pallas_call(functools.partial(kernel, patterns), out_shape=out_shape,...  2.76 us
    pallas_call x1, Pallas kernels, prologue(): pl.pallas_call(functools.partial(prologue_kernel, patterns), out_shape=(j...  1.7 us
  transfers between devices with their start and end apart: 10, of which 4 were waited for; matrix products, arithmetic and copies ran while one was open for 0% of the time, Pallas kernels for 7%

profile of v8, /device:TPU:0, one launch (start us, length us, event | category | flops | bytes accessed | tf_op | source)
XLA Modules:
  0.0 22.4 jit_solution(5010198765129827749)
XLA Ops:
  0.6 1.7 %shard_map.95 = (bf16[64,128]{1,0:T(8,128)(2,1)S(1)}, bf16[64,256]{1,0:T(8,128)(2,1)S(1)}, f32[128,1024]{1,0:T(8,128)S(1)}, bf16[128,768]{1,0:T(8,128)(2,1)S(1)}...) custom-call(bf16[128,2048]{1,0:T(8,128)(2,1)} %hidden_hbm.1, bf16[64,2048]{1,0:T(8,128)(2,1)} %bitcast.1, ...), custom_call_target="tpu_custom_call" | custom-call | flops 33554432 | bytes 1048576 | tf_op jit(solution)/shard_map/pallas_call | solution.py:141
  2.3 0.5 %collective-permute-start = (bf16[64,128]{1,0:T(8,128)(2,1)S(1)}, bf16[64,128]{1,0:T(8,128)(2,1)S(1)}, u32[]{:S(2)}, u32[]{:S(2)}) collective-permute-start(bf16[64,128]{1,0:T(8,128)(2,1)S(1)} %get-tuple-element.16), channel_id=1, source_target_pairs={{0,1},{1,0},{2,3},{3,2},{4,5},{5,4},{6,7},{7,6},{8,9},{9,8},{10,11... | collective-permute-start | bytes 49160 | tf_op jit(solution)/shard_map/ppermute | solution.py:28
  2.9 3.7 %collective-permute-start.2 = (bf16[64,256]{1,0:T(8,128)(2,1)S(1)}, bf16[64,256]{1,0:T(8,128)(2,1)S(1)}, u32[]{:S(2)}, u32[]{:S(2)}) collective-permute-start(bf16[64,256]{1,0:T(8,128)(2,1)S(1)} %get-tuple-element.19), channel_id=1, source_target_pairs={{0,17},{1,16},{2,19},{3,18},{4,21},{5,20},{6,23},{7,22},{8,25},{9,... | collective-permute-start | bytes 98312 | tf_op jit(solution)/shard_map/ppermute | solution.py:28
  6.6 0.0 collective-permute-done
  6.6 1.3 %collective-permute-start.1 = (bf16[64,128]{1,0:T(8,128)(2,1)S(1)}, bf16[64,128]{1,0:T(8,128)(2,1)S(1)}, u32[]{:S(2)}, u32[]{:S(2)}) collective-permute-start(bf16[64,128]{1,0:T(8,128)(2,1)S(1)} %add_convert_fusion.1), channel_id=1, source_target_pairs={{0,3},{1,2},{2,1},{3,0},{4,7},{5,6},{6,5},{7,4},{8,11},{9,10},{10,... | collective-permute-start | bytes 49160 | tf_op jit(solution)/shard_map/ppermute | solution.py:28
  7.8 0.4 %collective-permute-done.2 = bf16[64,256]{1,0:T(8,128)(2,1)S(1)} collective-permute-done((bf16[64,256]{1,0:T(8,128)(2,1)S(1)}, bf16[64,256]{1,0:T(8,128)(2,1)S(1)}, u32[]{:S(2)}, u32[]{:S(2)}) %collective-permute-start.2) | collective-permute-done | bytes 32800 | tf_op jit(solution)/shard_map/ppermute | solution.py:28
  8.2 1.6 %collective-permute-start.3 = (bf16[128,256]{1,0:T(8,128)(2,1)S(1)}, bf16[128,256]{1,0:T(8,128)(2,1)S(1)}, u32[]{:S(2)}, u32[]{:S(2)}) collective-permute-start(bf16[128,256]{1,0:T(8,128)(2,1)S(1)} %pad_maximum_fusion.1), channel_id=1, source_target_pairs={{0,9},{1,8},{2,11},{3,10},{4,13},{5,12},{6,15},{7,14},{8,1},{9,0},... | collective-permute-start | bytes 196616 | tf_op jit(solution)/shard_map/ppermute | solution.py:28
  9.8 0.0 collective-permute-done.1
  9.8 3.0 %collective-permute-start.5 = (bf16[32,128]{1,0:T(8,128)(2,1)S(1)}, bf16[32,128]{1,0:T(8,128)(2,1)S(1)}, u32[]{:S(2)}, u32[]{:S(2)}) collective-permute-start(bf16[32,128]{1,0:T(8,128)(2,1)S(1)} %slice.4), channel_id=1, source_target_pairs={{0,17},{1,16},{2,19},{3,18},{4,21},{5,20},{6,23},{7,22},{8,25},{9,... | collective-permute-start | bytes 24584 | tf_op jit(solution)/shard_map/ppermute | solution.py:28
  12.9 0.0 collective-permute-done.3
  12.9 1.2 %collective-permute-start.7 = (bf16[256,256]{1,0:T(8,128)(2,1)S(1)}, bf16[256,256]{1,0:T(8,128)(2,1)S(1)}, u32[]{:S(2)}, u32[]{:S(2)}) collective-permute-start(bf16[256,256]{1,0:T(8,128)(2,1)S(1)} %pad_maximum_fusion.kv_ref), channel_id=1, source_target_pairs={{0,5},{1,4},{2,7},{3,6},{4,1},{5,0},{6,3},{7,2},{8,13},{9,12},{10,... | collective-permute-start | bytes 393224 | tf_op jit(solution)/shard_map/ppermute | solution.py:28
  14.1 0.4 %collective-permute-start.4 = (bf16[256,256]{1,0:T(8,128)(2,1)S(1)}, bf16[256,256]{1,0:T(8,128)(2,1)S(1)}, u32[]{:S(2)}, u32[]{:S(2)}) collective-permute-start(bf16[256,256]{1,0:T(8,128)(2,1)S(1)} %pad_maximum_fusion.kv_ref), channel_id=1, source_target_pairs={{0,1},{1,0},{2,3},{3,2},{4,5},{5,4},{6,7},{7,6},{8,9},{9,8},{10,11... | collective-permute-start | bytes 393224 | tf_op jit(solution)/shard_map/ppermute | solution.py:28
  14.5 0.0 collective-permute-done.5
  14.5 0.9 %collective-permute-start.6 = (bf16[64,128]{1,0:T(8,128)(2,1)S(1)}, bf16[64,128]{1,0:T(8,128)(2,1)S(1)}, u32[]{:S(2)}, u32[]{:S(2)}) collective-permute-start(bf16[64,128]{1,0:T(8,128)(2,1)S(1)} %pad_maximum_fusion.3), channel_id=1, source_target_pairs={{0,9},{1,8},{2,11},{3,10},{4,13},{5,12},{6,15},{7,14},{8,1},{9,0},... | collective-permute-start | bytes 49160 | tf_op jit(solution)/shard_map/ppermute | solution.py:28
  15.4 2.3 %collective-permute-done.6 = bf16[64,128]{1,0:T(8,128)(2,1)S(1)} collective-permute-done((bf16[64,128]{1,0:T(8,128)(2,1)S(1)}, bf16[64,128]{1,0:T(8,128)(2,1)S(1)}, u32[]{:S(2)}, u32[]{:S(2)}) %collective-permute-start.6) | collective-permute-done | bytes 16416 | tf_op jit(solution)/shard_map/ppermute | solution.py:28
  17.7 1.1 %collective-permute-start.9 = (bf16[128,128]{1,0:T(8,128)(2,1)S(1)}, bf16[128,128]{1,0:T(8,128)(2,1)S(1)}, u32[]{:S(2)}, u32[]{:S(2)}) collective-permute-start(bf16[128,128]{1,0:T(8,128)(2,1)S(1)} %pad_maximum_fusion.2.low_value_ref), channel_id=1, source_target_pairs={{0,5},{1,4},{2,7},{3,6},{4,1},{5,0},{6,3},{7,2},{8,13},{9,12},{10,... | collective-permute-start | bytes 98312 | tf_op jit(solution)/shard_map/ppermute | solution.py:28
  18.8 0.0 collective-permute-done.7.kv_ref
  18.8 0.2 collective-permute-start.8
  19.0 0.0 collective-permute-done.4.other_kv_ref
  19.0 0.9 %shard_map.96 = (bf16[128,768]{1,0:T(8,128)(2,1)S(1)}, f32[128,768]{1,0:T(8,128)S(1)}, f32[768,256]{1,0:T(8,128)S(1)}) custom-call(bf16[128,768]{1,0:T(8,128)(2,1)S(1)} %get-tuple-element.15.frozen_query_ref, bf16[64,128]{1,0:T(8,128)(2,1)S(1)} %add_convert_fusion.low_ref, bf16[32,768]{1,0:T(8,128)(2,1)S(1)} %get-tuple-element.17.query_up_ref, ...), custom_call_target="tpu_custom_call" | custom-call | flops 9059696640 | bytes 23592960 | tf_op jit(solution)/shard_map/pallas_call | solution.py:326
  19.9 0.3 %collective-permute-done.8.other_kv_ref = bf16[256,256]{1,0:T(8,128)(2,1)S(1)} collective-permute-done((bf16[256,256]{1,0:T(8,128)(2,1)S(1)}, bf16[256,256]{1,0:T(8,128)(2,1)S(1)}, u32[]{:S(2)}, u32[]{:S(2)}) %collective-permute-start.8) | collective-permute-done | bytes 131104 | tf_op jit(solution)/shard_map/ppermute | solution.py:28
  20.2 0.6 %shard_map.97 = (bf16[768,512]{1,0:T(8,128)(2,1)S(1)}, f32[128,768]{1,0:T(8,128)S(1)}, f32[128,768]{1,0:T(8,128)S(1)}) custom-call(bf16[128,768]{1,0:T(8,128)(2,1)S(1)} %get-tuple-element.22.queries_ref, f32[128,1024]{1,0:T(8,128)S(1)} %get-tuple-element.18.bias_ref, bf16[256,256]{1,0:T(8,128)(2,1)S(1)} %collective-permute-done.7.kv_ref, ...), custom_call_target="tpu_custom_call" | custom-call | flops 9059696640 | bytes 23592960 | tf_op jit(solution)/shard_map/pallas_call | solution.py:326
  20.8 0.3 %collective-permute-done.9.low_value_ref = bf16[128,128]{1,0:T(8,128)(2,1)S(1)} collective-permute-done((bf16[128,128]{1,0:T(8,128)(2,1)S(1)}, bf16[128,128]{1,0:T(8,128)(2,1)S(1)}, u32[]{:S(2)}, u32[]{:S(2)}) %collective-permute-start.9) | collective-permute-done | bytes 32800 | tf_op jit(solution)/shard_map/ppermute | solution.py:28
  21.1 1.3 %shard_map.98 = (bf16[128,768]{1,0:T(8,128)(2,1)}, f32[6,128]{1,0:T(8,128)}) custom-call(bf16[768,512]{1,0:T(8,128)(2,1)S(1)} %get-tuple-element.24.weights_ref, f32[128,768]{1,0:T(8,128)S(1)} %get-tuple-element.25.top_ref, f32[128,768]{1,0:T(8,128)S(1)} %get-tuple-element.26.scale_ref, f32[768,256]{1,0:T(8,128)S(1)} %get-tuple-element.27.first_sums_ref, ...), custom_call_target="tpu_custom_call" | custom-call | flops 301989888 | bytes 786432 | tf_op jit(solution)/shard_map/pallas_call | solution.py:326
  (7 shorter events, 0.0 us)
Async XLA Ops:
  2.3 4.2 %collective-permute-start = (bf16[64,128]{1,0:T(8,128)(2,1)S(1)}, bf16[64,128]{1,0:T(8,128)(2,1)S(1)}, u32[]{:S(2)}, u32[]{:S(2)}) collective-permute-start(bf16[64,128]{1,0:T(8,128)(2,1)S(1)} %get-tuple-element.16), channel_id=1, source_target_pairs={{0,1},{1,0},{2,3},{3,2},{4,5},{5,4},{6,7},{7,6},{8,9},{9,8},{10,11... | collective-permute-start | bytes 49160 | tf_op jit(solution)/shard_map/ppermute | solution.py:28
  2.9 5.4 %collective-permute-start.2 = (bf16[64,256]{1,0:T(8,128)(2,1)S(1)}, bf16[64,256]{1,0:T(8,128)(2,1)S(1)}, u32[]{:S(2)}, u32[]{:S(2)}) collective-permute-start(bf16[64,256]{1,0:T(8,128)(2,1)S(1)} %get-tuple-element.19), channel_id=1, source_target_pairs={{0,17},{1,16},{2,19},{3,18},{4,21},{5,20},{6,23},{7,22},{8,25},{9,... | collective-permute-start | bytes 98312 | tf_op jit(solution)/shard_map/ppermute | solution.py:28
  6.6 3.2 %collective-permute-start.1 = (bf16[64,128]{1,0:T(8,128)(2,1)S(1)}, bf16[64,128]{1,0:T(8,128)(2,1)S(1)}, u32[]{:S(2)}, u32[]{:S(2)}) collective-permute-start(bf16[64,128]{1,0:T(8,128)(2,1)S(1)} %add_convert_fusion.1), channel_id=1, source_target_pairs={{0,3},{1,2},{2,1},{3,0},{4,7},{5,6},{6,5},{7,4},{8,11},{9,10},{10,... | collective-permute-start | bytes 49160 | tf_op jit(solution)/shard_map/ppermute | solution.py:28
  8.2 4.6 %collective-permute-start.3 = (bf16[128,256]{1,0:T(8,128)(2,1)S(1)}, bf16[128,256]{1,0:T(8,128)(2,1)S(1)}, u32[]{:S(2)}, u32[]{:S(2)}) collective-permute-start(bf16[128,256]{1,0:T(8,128)(2,1)S(1)} %pad_maximum_fusion.1), channel_id=1, source_target_pairs={{0,9},{1,8},{2,11},{3,10},{4,13},{5,12},{6,15},{7,14},{8,1},{9,0},... | collective-permute-start | bytes 196616 | tf_op jit(solution)/shard_map/ppermute | solution.py:28
  9.8 4.7 %collective-permute-start.5 = (bf16[32,128]{1,0:T(8,128)(2,1)S(1)}, bf16[32,128]{1,0:T(8,128)(2,1)S(1)}, u32[]{:S(2)}, u32[]{:S(2)}) collective-permute-start(bf16[32,128]{1,0:T(8,128)(2,1)S(1)} %slice.4), channel_id=1, source_target_pairs={{0,17},{1,16},{2,19},{3,18},{4,21},{5,20},{6,23},{7,22},{8,25},{9,... | collective-permute-start | bytes 24584 | tf_op jit(solution)/shard_map/ppermute | solution.py:28
  12.9 6.0 %collective-permute-start.7 = (bf16[256,256]{1,0:T(8,128)(2,1)S(1)}, bf16[256,256]{1,0:T(8,128)(2,1)S(1)}, u32[]{:S(2)}, u32[]{:S(2)}) collective-permute-start(bf16[256,256]{1,0:T(8,128)(2,1)S(1)} %pad_maximum_fusion.kv_ref), channel_id=1, source_target_pairs={{0,5},{1,4},{2,7},{3,6},{4,1},{5,0},{6,3},{7,2},{8,13},{9,12},{10,... | collective-permute-start | bytes 393224 | tf_op jit(solution)/shard_map/ppermute | solution.py:28
  14.1 4.9 %collective-permute-start.4 = (bf16[256,256]{1,0:T(8,128)(2,1)S(1)}, bf16[256,256]{1,0:T(8,128)(2,1)S(1)}, u32[]{:S(2)}, u32[]{:S(2)}) collective-permute-start(bf16[256,256]{1,0:T(8,128)(2,1)S(1)} %pad_maximum_fusion.kv_ref), channel_id=1, source_target_pairs={{0,1},{1,0},{2,3},{3,2},{4,5},{5,4},{6,7},{7,6},{8,9},{9,8},{10,11... | collective-permute-start | bytes 393224 | tf_op jit(solution)/shard_map/ppermute | solution.py:28
  14.5 3.2 %collective-permute-start.6 = (bf16[64,128]{1,0:T(8,128)(2,1)S(1)}, bf16[64,128]{1,0:T(8,128)(2,1)S(1)}, u32[]{:S(2)}, u32[]{:S(2)}) collective-permute-start(bf16[64,128]{1,0:T(8,128)(2,1)S(1)} %pad_maximum_fusion.3), channel_id=1, source_target_pairs={{0,9},{1,8},{2,11},{3,10},{4,13},{5,12},{6,15},{7,14},{8,1},{9,0},... | collective-permute-start | bytes 49160 | tf_op jit(solution)/shard_map/ppermute | solution.py:28
  17.7 3.4 %collective-permute-start.9 = (bf16[128,128]{1,0:T(8,128)(2,1)S(1)}, bf16[128,128]{1,0:T(8,128)(2,1)S(1)}, u32[]{:S(2)}, u32[]{:S(2)}) collective-permute-start(bf16[128,128]{1,0:T(8,128)(2,1)S(1)} %pad_maximum_fusion.2.low_value_ref), channel_id=1, source_target_pairs={{0,5},{1,4},{2,7},{3,6},{4,1},{5,0},{6,3},{7,2},{8,13},{9,12},{10,... | collective-permute-start | bytes 98312 | tf_op jit(solution)/shard_map/ppermute | solution.py:28
  18.8 1.3 %collective-permute-start.8 = (bf16[256,256]{1,0:T(8,128)(2,1)S(1)}, bf16[256,256]{1,0:T(8,128)(2,1)S(1)}, u32[]{:S(2)}, u32[]{:S(2)}) collective-permute-start(bf16[256,256]{1,0:T(8,128)(2,1)S(1)} %collective-permute-done.7.kv_ref), channel_id=1, source_target_pairs={{0,1},{1,0},{2,3},{3,2},{4,5},{5,4},{6,7},{7,6},{8,9},{9,8},{10,11... | collective-permute-start | bytes 393224 | tf_op jit(solution)/shard_map/ppermute | solution.py:28

commit v9 on v8

--- a/solution.py
+++ b/solution.py
@@ -75,18 +75,12 @@
     span = tok_dev // 2
     rows = pl.ds(pl.multiple_of(side * span, span), span)
     columns = pl.ds(pl.multiple_of(group * HEAD_SIZE, HEAD_SIZE), HEAD_SIZE)
-    chunks = sems.shape[0]
-    depth = down_hbm.shape[1] // chunks
-    copies = []
-    for chunk in range(chunks):
-        part = pl.ds(chunk * depth, depth)
-        pair = (
-            pltpu.make_async_copy(hidden_hbm.at[:, part], hidden_ref.at[:, part], sems.at[chunk, 0]),
-            pltpu.make_async_copy(down_hbm.at[:, part], down_ref.at[:, part], sems.at[chunk, 1]),
-        )
-        for copy in pair:
-            copy.start()
-        copies.append(pair)
+    copies = (
+        pltpu.make_async_copy(hidden_hbm, hidden_ref, sems.at[0]),
+        pltpu.make_async_copy(down_hbm, down_ref, sems.at[1]),
+    )
+    for copy in copies:
+        copy.start()
     others = [
         pltpu.make_async_copy(*refs, other_sems.at[n])
         for n, refs in enumerate(
@@ -115,18 +109,14 @@
         bias_ref[:, tile * tok_dev : (tile + 1) * tok_dev] = jnp.where(
             ahead * span <= inner, 0.0, MASKED
         )
-    total = jnp.zeros(low_ref.shape, jnp.float32)
-    for chunk in range(chunks):
-        for copy in copies[chunk]:
-            copy.wait()
-        part = slice(chunk * depth, (chunk + 1) * depth)
-        total += lax.dot_general(
-            down_ref[:, part],
-            hidden_ref[:, part],
-            (((1,), (1,)), ((), ())),
-            preferred_element_type=jnp.float32,
-        )
-    low_ref[...] = total.astype(jnp.bfloat16)
+    for copy in copies:
+        copy.wait()
+    low_ref[...] = lax.dot_general(
+        down_ref[...],
+        hidden_ref[...],
+        (((1,), (1,)), ((), ())),
+        preferred_element_type=jnp.float32,
+    ).astype(jnp.bfloat16)
     for copy in others[1:]:
         copy.wait()
 
@@ -134,7 +124,6 @@
 def prologue(patterns, hidden, down, keys, values, order, frozen_query, query_up, value_up):
     tok_dev, depth = hidden.shape
     rank = down.shape[0]
-    chunks = 4
     hbm = pl.BlockSpec(memory_space=pltpu.HBM)
     vmem = pl.BlockSpec(memory_space=pltpu.VMEM)
     operands = (hidden, down, keys, values, order, frozen_query, query_up, value_up)
@@ -154,7 +143,7 @@
             pltpu.VMEM(hidden.shape, jnp.bfloat16),
             pltpu.VMEM(down.shape, jnp.bfloat16),
             pltpu.SMEM(order.shape, jnp.int32),
-            pltpu.SemaphoreType.DMA((chunks, 2)),
+            pltpu.SemaphoreType.DMA((2,)),
             pltpu.SemaphoreType.DMA((6,)),
         ],
         compiler_params=pltpu.CompilerParams(vmem_limit_bytes=VMEM_LIMIT),

time: 22.5 us -> 22.3 us (level)
  no operation moved by 1% of the time
where the time goes in v9:
time: 22.3 us; the launch traced here: 22.2 us
  starting transfers between devices  13.9 us (62%)
  Pallas kernels  4.27 us (19%)
  waiting for transfers between devices  3.29 us (15%)
  between operations  0.69 us (3%)
    ppermute x10, starting transfers between devices, exchange(): return lax.ppermute(value, AXES, pairs)  13.9 us
    ppermute x10, waiting for transfers between devices, exchange(): return lax.ppermute(value, AXES, pairs)  3.29 us
    pallas_call x3, Pallas kernels, call(): pl.pallas_call(functools.partial(kernel, patterns), out_shape=out_shape,...  2.76 us
    pallas_call x1, Pallas kernels, prologue(): pl.pallas_call(functools.partial(prologue_kernel, patterns), out_shape=(j...  1.5 us
  transfers between devices with their start and end apart: 10, of which 4 were waited for; matrix products, arithmetic and copies ran while one was open for 0% of the time, Pallas kernels for 7%

profile of v9, /device:TPU:0, one launch (start us, length us, event | category | flops | bytes accessed | tf_op | source)
XLA Modules:
  0.0 22.2 jit_solution(14864167701318946601)
XLA Ops:
  0.6 1.5 %shard_map.95 = (bf16[64,128]{1,0:T(8,128)(2,1)S(1)}, bf16[64,256]{1,0:T(8,128)(2,1)S(1)}, f32[128,1024]{1,0:T(8,128)S(1)}, bf16[128,768]{1,0:T(8,128)(2,1)S(1)}...) custom-call(bf16[128,2048]{1,0:T(8,128)(2,1)} %hidden_hbm.1, bf16[64,2048]{1,0:T(8,128)(2,1)} %bitcast.1, ...), custom_call_target="tpu_custom_call" | custom-call | flops 33554432 | bytes 1048576 | tf_op jit(solution)/shard_map/pallas_call | solution.py:130
  2.1 0.5 %collective-permute-start = (bf16[64,128]{1,0:T(8,128)(2,1)S(1)}, bf16[64,128]{1,0:T(8,128)(2,1)S(1)}, u32[]{:S(2)}, u32[]{:S(2)}) collective-permute-start(bf16[64,128]{1,0:T(8,128)(2,1)S(1)} %get-tuple-element.16), channel_id=1, source_target_pairs={{0,1},{1,0},{2,3},{3,2},{4,5},{5,4},{6,7},{7,6},{8,9},{9,8},{10,11... | collective-permute-start | bytes 49160 | tf_op jit(solution)/shard_map/ppermute | solution.py:28
  2.7 3.7 %collective-permute-start.2 = (bf16[64,256]{1,0:T(8,128)(2,1)S(1)}, bf16[64,256]{1,0:T(8,128)(2,1)S(1)}, u32[]{:S(2)}, u32[]{:S(2)}) collective-permute-start(bf16[64,256]{1,0:T(8,128)(2,1)S(1)} %get-tuple-element.19), channel_id=1, source_target_pairs={{0,17},{1,16},{2,19},{3,18},{4,21},{5,20},{6,23},{7,22},{8,25},{9,... | collective-permute-start | bytes 98312 | tf_op jit(solution)/shard_map/ppermute | solution.py:28
  6.4 0.0 collective-permute-done
  6.4 1.3 %collective-permute-start.1 = (bf16[64,128]{1,0:T(8,128)(2,1)S(1)}, bf16[64,128]{1,0:T(8,128)(2,1)S(1)}, u32[]{:S(2)}, u32[]{:S(2)}) collective-permute-start(bf16[64,128]{1,0:T(8,128)(2,1)S(1)} %add_convert_fusion.1), channel_id=1, source_target_pairs={{0,3},{1,2},{2,1},{3,0},{4,7},{5,6},{6,5},{7,4},{8,11},{9,10},{10,... | collective-permute-start | bytes 49160 | tf_op jit(solution)/shard_map/ppermute | solution.py:28
  7.6 0.4 %collective-permute-done.2 = bf16[64,256]{1,0:T(8,128)(2,1)S(1)} collective-permute-done((bf16[64,256]{1,0:T(8,128)(2,1)S(1)}, bf16[64,256]{1,0:T(8,128)(2,1)S(1)}, u32[]{:S(2)}, u32[]{:S(2)}) %collective-permute-start.2) | collective-permute-done | bytes 32800 | tf_op jit(solution)/shard_map/ppermute | solution.py:28
  8.1 1.6 %collective-permute-start.3 = (bf16[128,256]{1,0:T(8,128)(2,1)S(1)}, bf16[128,256]{1,0:T(8,128)(2,1)S(1)}, u32[]{:S(2)}, u32[]{:S(2)}) collective-permute-start(bf16[128,256]{1,0:T(8,128)(2,1)S(1)} %pad_maximum_fusion.1), channel_id=1, source_target_pairs={{0,9},{1,8},{2,11},{3,10},{4,13},{5,12},{6,15},{7,14},{8,1},{9,0},... | collective-permute-start | bytes 196616 | tf_op jit(solution)/shard_map/ppermute | solution.py:28
  9.6 0.0 collective-permute-done.1
  9.6 3.0 %collective-permute-start.5 = (bf16[32,128]{1,0:T(8,128)(2,1)S(1)}, bf16[32,128]{1,0:T(8,128)(2,1)S(1)}, u32[]{:S(2)}, u32[]{:S(2)}) collective-permute-start(bf16[32,128]{1,0:T(8,128)(2,1)S(1)} %slice.4), channel_id=1, source_target_pairs={{0,17},{1,16},{2,19},{3,18},{4,21},{5,20},{6,23},{7,22},{8,25},{9,... | collective-permute-start | bytes 24584 | tf_op jit(solution)/shard_map/ppermute | solution.py:28
  12.7 0.0 collective-permute-done.3
  12.7 1.2 %collective-permute-start.7 = (bf16[256,256]{1,0:T(8,128)(2,1)S(1)}, bf16[256,256]{1,0:T(8,128)(2,1)S(1)}, u32[]{:S(2)}, u32[]{:S(2)}) collective-permute-start(bf16[256,256]{1,0:T(8,128)(2,1)S(1)} %pad_maximum_fusion.kv_ref), channel_id=1, source_target_pairs={{0,5},{1,4},{2,7},{3,6},{4,1},{5,0},{6,3},{7,2},{8,13},{9,12},{10,... | collective-permute-start | bytes 393224 | tf_op jit(solution)/shard_map/ppermute | solution.py:28
  13.9 0.4 %collective-permute-start.4 = (bf16[256,256]{1,0:T(8,128)(2,1)S(1)}, bf16[256,256]{1,0:T(8,128)(2,1)S(1)}, u32[]{:S(2)}, u32[]{:S(2)}) collective-permute-start(bf16[256,256]{1,0:T(8,128)(2,1)S(1)} %pad_maximum_fusion.kv_ref), channel_id=1, source_target_pairs={{0,1},{1,0},{2,3},{3,2},{4,5},{5,4},{6,7},{7,6},{8,9},{9,8},{10,11... | collective-permute-start | bytes 393224 | tf_op jit(solution)/shard_map/ppermute | solution.py:28
  14.3 0.0 collective-permute-done.5
  14.4 0.9 %collective-permute-start.6 = (bf16[64,128]{1,0:T(8,128)(2,1)S(1)}, bf16[64,128]{1,0:T(8,128)(2,1)S(1)}, u32[]{:S(2)}, u32[]{:S(2)}) collective-permute-start(bf16[64,128]{1,0:T(8,128)(2,1)S(1)} %pad_maximum_fusion.3), channel_id=1, source_target_pairs={{0,9},{1,8},{2,11},{3,10},{4,13},{5,12},{6,15},{7,14},{8,1},{9,0},... | collective-permute-start | bytes 49160 | tf_op jit(solution)/shard_map/ppermute | solution.py:28
  15.2 2.3 %collective-permute-done.6 = bf16[64,128]{1,0:T(8,128)(2,1)S(1)} collective-permute-done((bf16[64,128]{1,0:T(8,128)(2,1)S(1)}, bf16[64,128]{1,0:T(8,128)(2,1)S(1)}, u32[]{:S(2)}, u32[]{:S(2)}) %collective-permute-start.6) | collective-permute-done | bytes 16416 | tf_op jit(solution)/shard_map/ppermute | solution.py:28
  17.5 1.1 %collective-permute-start.9 = (bf16[128,128]{1,0:T(8,128)(2,1)S(1)}, bf16[128,128]{1,0:T(8,128)(2,1)S(1)}, u32[]{:S(2)}, u32[]{:S(2)}) collective-permute-start(bf16[128,128]{1,0:T(8,128)(2,1)S(1)} %pad_maximum_fusion.2.low_value_ref), channel_id=1, source_target_pairs={{0,5},{1,4},{2,7},{3,6},{4,1},{5,0},{6,3},{7,2},{8,13},{9,12},{10,... | collective-permute-start | bytes 98312 | tf_op jit(solution)/shard_map/ppermute | solution.py:28
  18.6 0.0 collective-permute-done.7.kv_ref
  18.6 0.2 collective-permute-start.8
  18.8 0.0 collective-permute-done.4.other_kv_ref
  18.8 0.9 %shard_map.96 = (bf16[128,768]{1,0:T(8,128)(2,1)S(1)}, f32[128,768]{1,0:T(8,128)S(1)}, f32[768,256]{1,0:T(8,128)S(1)}) custom-call(bf16[128,768]{1,0:T(8,128)(2,1)S(1)} %get-tuple-element.15.frozen_query_ref, bf16[64,128]{1,0:T(8,128)(2,1)S(1)} %add_convert_fusion.low_ref, bf16[32,768]{1,0:T(8,128)(2,1)S(1)} %get-tuple-element.17.query_up_ref, ...), custom_call_target="tpu_custom_call" | custom-call | flops 9059696640 | bytes 23592960 | tf_op jit(solution)/shard_map/pallas_call | solution.py:315
  19.7 0.3 %collective-permute-done.8.other_kv_ref = bf16[256,256]{1,0:T(8,128)(2,1)S(1)} collective-permute-done((bf16[256,256]{1,0:T(8,128)(2,1)S(1)}, bf16[256,256]{1,0:T(8,128)(2,1)S(1)}, u32[]{:S(2)}, u32[]{:S(2)}) %collective-permute-start.8) | collective-permute-done | bytes 131104 | tf_op jit(solution)/shard_map/ppermute | solution.py:28
  20.0 0.6 %shard_map.97 = (bf16[768,512]{1,0:T(8,128)(2,1)S(1)}, f32[128,768]{1,0:T(8,128)S(1)}, f32[128,768]{1,0:T(8,128)S(1)}) custom-call(bf16[128,768]{1,0:T(8,128)(2,1)S(1)} %get-tuple-element.22.queries_ref, f32[128,1024]{1,0:T(8,128)S(1)} %get-tuple-element.18.bias_ref, bf16[256,256]{1,0:T(8,128)(2,1)S(1)} %collective-permute-done.7.kv_ref, ...), custom_call_target="tpu_custom_call" | custom-call | flops 9059696640 | bytes 23592960 | tf_op jit(solution)/shard_map/pallas_call | solution.py:315
  20.6 0.3 %collective-permute-done.9.low_value_ref = bf16[128,128]{1,0:T(8,128)(2,1)S(1)} collective-permute-done((bf16[128,128]{1,0:T(8,128)(2,1)S(1)}, bf16[128,128]{1,0:T(8,128)(2,1)S(1)}, u32[]{:S(2)}, u32[]{:S(2)}) %collective-permute-start.9) | collective-permute-done | bytes 32800 | tf_op jit(solution)/shard_map/ppermute | solution.py:28
  20.9 1.3 %shard_map.98 = (bf16[128,768]{1,0:T(8,128)(2,1)}, f32[6,128]{1,0:T(8,128)}) custom-call(bf16[768,512]{1,0:T(8,128)(2,1)S(1)} %get-tuple-element.24.weights_ref, f32[128,768]{1,0:T(8,128)S(1)} %get-tuple-element.25.top_ref, f32[128,768]{1,0:T(8,128)S(1)} %get-tuple-element.26.scale_ref, f32[768,256]{1,0:T(8,128)S(1)} %get-tuple-element.27.first_sums_ref, ...), custom_call_target="tpu_custom_call" | custom-call | flops 301989888 | bytes 786432 | tf_op jit(solution)/shard_map/pallas_call | solution.py:315
  (7 shorter events, 0.0 us)
Async XLA Ops:
  2.1 4.2 %collective-permute-start = (bf16[64,128]{1,0:T(8,128)(2,1)S(1)}, bf16[64,128]{1,0:T(8,128)(2,1)S(1)}, u32[]{:S(2)}, u32[]{:S(2)}) collective-permute-start(bf16[64,128]{1,0:T(8,128)(2,1)S(1)} %get-tuple-element.16), channel_id=1, source_target_pairs={{0,1},{1,0},{2,3},{3,2},{4,5},{5,4},{6,7},{7,6},{8,9},{9,8},{10,11... | collective-permute-start | bytes 49160 | tf_op jit(solution)/shard_map/ppermute | solution.py:28
  2.7 5.4 %collective-permute-start.2 = (bf16[64,256]{1,0:T(8,128)(2,1)S(1)}, bf16[64,256]{1,0:T(8,128)(2,1)S(1)}, u32[]{:S(2)}, u32[]{:S(2)}) collective-permute-start(bf16[64,256]{1,0:T(8,128)(2,1)S(1)} %get-tuple-element.19), channel_id=1, source_target_pairs={{0,17},{1,16},{2,19},{3,18},{4,21},{5,20},{6,23},{7,22},{8,25},{9,... | collective-permute-start | bytes 98312 | tf_op jit(solution)/shard_map/ppermute | solution.py:28
  6.4 3.2 %collective-permute-start.1 = (bf16[64,128]{1,0:T(8,128)(2,1)S(1)}, bf16[64,128]{1,0:T(8,128)(2,1)S(1)}, u32[]{:S(2)}, u32[]{:S(2)}) collective-permute-start(bf16[64,128]{1,0:T(8,128)(2,1)S(1)} %add_convert_fusion.1), channel_id=1, source_target_pairs={{0,3},{1,2},{2,1},{3,0},{4,7},{5,6},{6,5},{7,4},{8,11},{9,10},{10,... | collective-permute-start | bytes 49160 | tf_op jit(solution)/shard_map/ppermute | solution.py:28
  8.1 4.6 %collective-permute-start.3 = (bf16[128,256]{1,0:T(8,128)(2,1)S(1)}, bf16[128,256]{1,0:T(8,128)(2,1)S(1)}, u32[]{:S(2)}, u32[]{:S(2)}) collective-permute-start(bf16[128,256]{1,0:T(8,128)(2,1)S(1)} %pad_maximum_fusion.1), channel_id=1, source_target_pairs={{0,9},{1,8},{2,11},{3,10},{4,13},{5,12},{6,15},{7,14},{8,1},{9,0},... | collective-permute-start | bytes 196616 | tf_op jit(solution)/shard_map/ppermute | solution.py:28
  9.6 4.7 %collective-permute-start.5 = (bf16[32,128]{1,0:T(8,128)(2,1)S(1)}, bf16[32,128]{1,0:T(8,128)(2,1)S(1)}, u32[]{:S(2)}, u32[]{:S(2)}) collective-permute-start(bf16[32,128]{1,0:T(8,128)(2,1)S(1)} %slice.4), channel_id=1, source_target_pairs={{0,17},{1,16},{2,19},{3,18},{4,21},{5,20},{6,23},{7,22},{8,25},{9,... | collective-permute-start | bytes 24584 | tf_op jit(solution)/shard_map/ppermute | solution.py:28
  12.7 6.0 %collective-permute-start.7 = (bf16[256,256]{1,0:T(8,128)(2,1)S(1)}, bf16[256,256]{1,0:T(8,128)(2,1)S(1)}, u32[]{:S(2)}, u32[]{:S(2)}) collective-permute-start(bf16[256,256]{1,0:T(8,128)(2,1)S(1)} %pad_maximum_fusion.kv_ref), channel_id=1, source_target_pairs={{0,5},{1,4},{2,7},{3,6},{4,1},{5,0},{6,3},{7,2},{8,13},{9,12},{10,... | collective-permute-start | bytes 393224 | tf_op jit(solution)/shard_map/ppermute | solution.py:28
  13.9 4.9 %collective-permute-start.4 = (bf16[256,256]{1,0:T(8,128)(2,1)S(1)}, bf16[256,256]{1,0:T(8,128)(2,1)S(1)}, u32[]{:S(2)}, u32[]{:S(2)}) collective-permute-start(bf16[256,256]{1,0:T(8,128)(2,1)S(1)} %pad_maximum_fusion.kv_ref), channel_id=1, source_target_pairs={{0,1},{1,0},{2,3},{3,2},{4,5},{5,4},{6,7},{7,6},{8,9},{9,8},{10,11... | collective-permute-start | bytes 393224 | tf_op jit(solution)/shard_map/ppermute | solution.py:28
  14.4 3.2 %collective-permute-start.6 = (bf16[64,128]{1,0:T(8,128)(2,1)S(1)}, bf16[64,128]{1,0:T(8,128)(2,1)S(1)}, u32[]{:S(2)}, u32[]{:S(2)}) collective-permute-start(bf16[64,128]{1,0:T(8,128)(2,1)S(1)} %pad_maximum_fusion.3), channel_id=1, source_target_pairs={{0,9},{1,8},{2,11},{3,10},{4,13},{5,12},{6,15},{7,14},{8,1},{9,0},... | collective-permute-start | bytes 49160 | tf_op jit(solution)/shard_map/ppermute | solution.py:28
  17.5 3.4 %collective-permute-start.9 = (bf16[128,128]{1,0:T(8,128)(2,1)S(1)}, bf16[128,128]{1,0:T(8,128)(2,1)S(1)}, u32[]{:S(2)}, u32[]{:S(2)}) collective-permute-start(bf16[128,128]{1,0:T(8,128)(2,1)S(1)} %pad_maximum_fusion.2.low_value_ref), channel_id=1, source_target_pairs={{0,5},{1,4},{2,7},{3,6},{4,1},{5,0},{6,3},{7,2},{8,13},{9,12},{10,... | collective-permute-start | bytes 98312 | tf_op jit(solution)/shard_map/ppermute | solution.py:28
  18.6 1.3 %collective-permute-start.8 = (bf16[256,256]{1,0:T(8,128)(2,1)S(1)}, bf16[256,256]{1,0:T(8,128)(2,1)S(1)}, u32[]{:S(2)}, u32[]{:S(2)}) collective-permute-start(bf16[256,256]{1,0:T(8,128)(2,1)S(1)} %collective-permute-done.7.kv_ref), channel_id=1, source_target_pairs={{0,1},{1,0},{2,3},{3,2},{4,5},{5,4},{6,7},{7,6},{8,9},{9,8},{10,11... | collective-permute-start | bytes 393224 | tf_op jit(solution)/shard_map/ppermute | solution.py:28

commit v10 on v9

--- a/solution.py
+++ b/solution.py
@@ -244,41 +244,32 @@
 
 
 def second_kernel(
-    patterns, queries_ref, bias_ref, kv_ref, other_kv_ref, first_top_ref, weights_ref, top_ref, scale_ref
+    part, queries_ref, bias_ref, kv_ref, old_top_ref, weights_ref, top_ref, scale_ref
 ):
     tok_dev, width = queries_ref.shape
     count = kv_ref.shape[0]
-    before = bias_ref.shape[1] // 2
+    before = bias_ref.shape[1] // 2 + part * count
     for head in range(width // HEAD_SIZE):
         columns = slice(head * HEAD_SIZE, (head + 1) * HEAD_SIZE)
         rows = slice(head * tok_dev, (head + 1) * tok_dev)
-        scores = [
-            scores_of(
-                queries_ref[:, columns],
-                ref,
-                bias_ref[:, before + n * count : before + (n + 1) * count],
-            )
-            for n, ref in enumerate((kv_ref, other_kv_ref))
-        ]
-        new_top = jnp.maximum(
-            jnp.max(scores[0], axis=1, keepdims=True), jnp.max(scores[1], axis=1, keepdims=True)
-        )
-        first_top = first_top_ref[:, columns]
-        top = jnp.maximum(first_top, new_top)
-        for n in range(2):
-            for at in range(0, count, HEAD_SIZE):
-                weights_ref[rows, n * count + at : n * count + at + HEAD_SIZE] = jnp.exp2(
-                    scores[n][:, at : at + HEAD_SIZE] - top
-                ).astype(jnp.bfloat16)
+        scores = scores_of(queries_ref[:, columns], kv_ref, bias_ref[:, before : before + count])
+        old_top = old_top_ref[:, columns]
+        top = jnp.maximum(old_top, jnp.max(scores, axis=1, keepdims=True))
+        for at in range(0, count, HEAD_SIZE):
+            weights_ref[rows, at : at + HEAD_SIZE] = jnp.exp2(
+                scores[:, at : at + HEAD_SIZE] - top
+            ).astype(jnp.bfloat16)
         top_ref[:, columns] = top
-        scale_ref[:, columns] = jnp.exp2(first_top - top)
+        scale_ref[:, columns] = jnp.exp2(old_top - top)
 
 
 def third_kernel(
     patterns,
     weights_ref,
+    other_weights_ref,
     top_ref,
     scale_ref,
+    other_scale_ref,
     first_sums_ref,
     kv_ref,
     other_kv_ref,
@@ -297,12 +288,17 @@
     for head in range(width // HEAD_SIZE):
         columns = slice(head * HEAD_SIZE, (head + 1) * HEAD_SIZE)
         rows = slice(head * tok_dev, (head + 1) * tok_dev)
-        sums = jnp.dot(weights_ref[rows, :], value_ref[...], preferred_element_type=jnp.float32)
-        scale = scale_ref[:, columns]
-        total = first_sums_ref[rows, HEAD_SIZE:] * scale + sums[:, HEAD_SIZE:]
-        attended_ref[:, columns] = (
-            (first_sums_ref[rows, :HEAD_SIZE] * scale + sums[:, :HEAD_SIZE]) / total
-        ).astype(jnp.bfloat16)
+        half = value_ref.shape[0] // 2
+        sums = jnp.dot(weights_ref[rows, :], value_ref[:half, :], preferred_element_type=jnp.float32)
+        other_sums = jnp.dot(
+            other_weights_ref[rows, :], value_ref[half:, :], preferred_element_type=jnp.float32
+        )
+        scale, other_scale = scale_ref[:, columns], other_scale_ref[:, columns]
+        weighted, total = (
+            (first_sums_ref[rows, part] * scale + sums[:, part]) * other_scale + other_sums[:, part]
+            for part in (slice(0, HEAD_SIZE), slice(HEAD_SIZE, 2 * HEAD_SIZE))
+        )
+        attended_ref[:, columns] = (weighted / total).astype(jnp.bfloat16)
         normalizer_ref[head : head + 1, :] = jnp.sum(
             jnp.where(row == lane, top_ref[:, columns] * math.log(2.0) + jnp.log(total), 0.0),
             axis=0,
@@ -470,18 +466,22 @@
         low_value,
         value_up,
     )
-    weights, top, scale = call(
-        second_kernel,
-        patterns,
-        (jax.ShapeDtypeStruct((rows, key_count), jnp.bfloat16), wide, wide),
-        [],
-        30 * work,
-        queries,
-        bias,
-        last_kv,
-        last_other_kv,
-        first_top,
-    )
+    parts = []
+    top = first_top
+    for part, rows_of_part in enumerate((last_kv, last_other_kv)):
+        weights, top, scale = call(
+            second_kernel,
+            part,
+            (jax.ShapeDtypeStruct((rows, key_count // 2), jnp.bfloat16), wide, wide),
+            [],
+            15 * work,
+            queries,
+            bias,
+            rows_of_part,
+            top,
+        )
+        parts.append((weights, scale))
+    (weights, scale), (other_weights, other_scale) = parts
     return call(
         third_kernel,
         patterns,
@@ -492,8 +492,10 @@
         [value_scratch],
         work,
         weights,
+        other_weights,
         top,
         scale,
+        other_scale,
         sums,
         last_kv,
         last_other_kv,

time: 22.3 us -> 22.4 us (level)
  Pallas kernels: 4.27 us -> 4.62 us
  waiting for transfers between devices: 3.29 us -> 2.97 us
    pallas_call x3 -> x4, Pallas kernels: 2.76 us -> 3.12 us  [call(): pl.pallas_call(functools.partial(kernel, patterns), out_shape=out_shape,...]
    ppermute x10, waiting for transfers between devices: 3.29 us -> 2.97 us  [exchange(): return lax.ppermute(value, AXES, pairs)]
  transfers between devices with their start and end apart: 10 -> 10, of which waited for: 4 -> 3; matrix products, arithmetic and copies ran while one was open for 0% -> 0% of each run, Pallas kernels for 7% -> 8%
where the time goes in v10:
time: 22.4 us; the launch traced here: 22.2 us
  starting transfers between devices  13.9 us (62%)
  Pallas kernels  4.62 us (21%)
  waiting for transfers between devices  2.97 us (13%)
  between operations  0.7 us (3%)
    ppermute x10, starting transfers between devices, exchange(): return lax.ppermute(value, AXES, pairs)  13.9 us
    pallas_call x4, Pallas kernels, call(): pl.pallas_call(functools.partial(kernel, patterns), out_shape=out_shape,...  3.12 us
    ppermute x10, waiting for transfers between devices, exchange(): return lax.ppermute(value, AXES, pairs)  2.97 us
    pallas_call x1, Pallas kernels, prologue(): pl.pallas_call(functools.partial(prologue_kernel, patterns), out_shape=(j...  1.5 us
  transfers between devices with their start and end apart: 10, of which 3 were waited for; matrix products, arithmetic and copies ran while one was open for 0% of the time, Pallas kernels for 8%

profile of v10, /device:TPU:0, one launch (start us, length us, event | category | flops | bytes accessed | tf_op | source)
XLA Modules:
  0.0 22.2 jit_solution(16995761452276879043)
XLA Ops:
  0.6 1.5 %shard_map.95 = (bf16[64,128]{1,0:T(8,128)(2,1)S(1)}, bf16[64,256]{1,0:T(8,128)(2,1)S(1)}, f32[128,1024]{1,0:T(8,128)S(1)}, bf16[128,768]{1,0:T(8,128)(2,1)S(1)}...) custom-call(bf16[128,2048]{1,0:T(8,128)(2,1)} %hidden_hbm.1, bf16[64,2048]{1,0:T(8,128)(2,1)} %bitcast.1, ...), custom_call_target="tpu_custom_call" | custom-call | flops 33554432 | bytes 1048576 | tf_op jit(solution)/shard_map/pallas_call | solution.py:130
  2.1 0.5 %collective-permute-start = (bf16[64,128]{1,0:T(8,128)(2,1)S(1)}, bf16[64,128]{1,0:T(8,128)(2,1)S(1)}, u32[]{:S(2)}, u32[]{:S(2)}) collective-permute-start(bf16[64,128]{1,0:T(8,128)(2,1)S(1)} %get-tuple-element.19), channel_id=1, source_target_pairs={{0,1},{1,0},{2,3},{3,2},{4,5},{5,4},{6,7},{7,6},{8,9},{9,8},{10,11... | collective-permute-start | bytes 49160 | tf_op jit(solution)/shard_map/ppermute | solution.py:28
  2.7 3.7 %collective-permute-start.2 = (bf16[64,256]{1,0:T(8,128)(2,1)S(1)}, bf16[64,256]{1,0:T(8,128)(2,1)S(1)}, u32[]{:S(2)}, u32[]{:S(2)}) collective-permute-start(bf16[64,256]{1,0:T(8,128)(2,1)S(1)} %get-tuple-element.22), channel_id=1, source_target_pairs={{0,17},{1,16},{2,19},{3,18},{4,21},{5,20},{6,23},{7,22},{8,25},{9,... | collective-permute-start | bytes 98312 | tf_op jit(solution)/shard_map/ppermute | solution.py:28
  6.4 0.0 collective-permute-done
  6.4 1.3 %collective-permute-start.1 = (bf16[64,128]{1,0:T(8,128)(2,1)S(1)}, bf16[64,128]{1,0:T(8,128)(2,1)S(1)}, u32[]{:S(2)}, u32[]{:S(2)}) collective-permute-start(bf16[64,128]{1,0:T(8,128)(2,1)S(1)} %add_convert_fusion.1), channel_id=1, source_target_pairs={{0,3},{1,2},{2,1},{3,0},{4,7},{5,6},{6,5},{7,4},{8,11},{9,10},{10,... | collective-permute-start | bytes 49160 | tf_op jit(solution)/shard_map/ppermute | solution.py:28
  7.6 0.4 %collective-permute-done.2 = bf16[64,256]{1,0:T(8,128)(2,1)S(1)} collective-permute-done((bf16[64,256]{1,0:T(8,128)(2,1)S(1)}, bf16[64,256]{1,0:T(8,128)(2,1)S(1)}, u32[]{:S(2)}, u32[]{:S(2)}) %collective-permute-start.2) | collective-permute-done | bytes 32800 | tf_op jit(solution)/shard_map/ppermute | solution.py:28
  8.1 1.6 %collective-permute-start.3 = (bf16[128,256]{1,0:T(8,128)(2,1)S(1)}, bf16[128,256]{1,0:T(8,128)(2,1)S(1)}, u32[]{:S(2)}, u32[]{:S(2)}) collective-permute-start(bf16[128,256]{1,0:T(8,128)(2,1)S(1)} %pad_maximum_fusion.1), channel_id=1, source_target_pairs={{0,9},{1,8},{2,11},{3,10},{4,13},{5,12},{6,15},{7,14},{8,1},{9,0},... | collective-permute-start | bytes 196616 | tf_op jit(solution)/shard_map/ppermute | solution.py:28
  9.6 0.0 collective-permute-done.1
  9.6 3.0 %collective-permute-start.5 = (bf16[32,128]{1,0:T(8,128)(2,1)S(1)}, bf16[32,128]{1,0:T(8,128)(2,1)S(1)}, u32[]{:S(2)}, u32[]{:S(2)}) collective-permute-start(bf16[32,128]{1,0:T(8,128)(2,1)S(1)} %slice.4), channel_id=1, source_target_pairs={{0,17},{1,16},{2,19},{3,18},{4,21},{5,20},{6,23},{7,22},{8,25},{9,... | collective-permute-start | bytes 24584 | tf_op jit(solution)/shard_map/ppermute | solution.py:28
  12.7 0.0 collective-permute-done.3
  12.7 1.2 %collective-permute-start.7 = (bf16[256,256]{1,0:T(8,128)(2,1)S(1)}, bf16[256,256]{1,0:T(8,128)(2,1)S(1)}, u32[]{:S(2)}, u32[]{:S(2)}) collective-permute-start(bf16[256,256]{1,0:T(8,128)(2,1)S(1)} %pad_maximum_fusion.kv_ref), channel_id=1, source_target_pairs={{0,5},{1,4},{2,7},{3,6},{4,1},{5,0},{6,3},{7,2},{8,13},{9,12},{10,... | collective-permute-start | bytes 393224 | tf_op jit(solution)/shard_map/ppermute | solution.py:28
  13.9 0.4 %collective-permute-start.4 = (bf16[256,256]{1,0:T(8,128)(2,1)S(1)}, bf16[256,256]{1,0:T(8,128)(2,1)S(1)}, u32[]{:S(2)}, u32[]{:S(2)}) collective-permute-start(bf16[256,256]{1,0:T(8,128)(2,1)S(1)} %pad_maximum_fusion.kv_ref), channel_id=1, source_target_pairs={{0,1},{1,0},{2,3},{3,2},{4,5},{5,4},{6,7},{7,6},{8,9},{9,8},{10,11... | collective-permute-start | bytes 393224 | tf_op jit(solution)/shard_map/ppermute | solution.py:28
  14.3 0.0 collective-permute-done.5
  14.4 0.9 %collective-permute-start.6 = (bf16[64,128]{1,0:T(8,128)(2,1)S(1)}, bf16[64,128]{1,0:T(8,128)(2,1)S(1)}, u32[]{:S(2)}, u32[]{:S(2)}) collective-permute-start(bf16[64,128]{1,0:T(8,128)(2,1)S(1)} %pad_maximum_fusion.3), channel_id=1, source_target_pairs={{0,9},{1,8},{2,11},{3,10},{4,13},{5,12},{6,15},{7,14},{8,1},{9,0},... | collective-permute-start | bytes 49160 | tf_op jit(solution)/shard_map/ppermute | solution.py:28
  15.2 2.3 %collective-permute-done.6 = bf16[64,128]{1,0:T(8,128)(2,1)S(1)} collective-permute-done((bf16[64,128]{1,0:T(8,128)(2,1)S(1)}, bf16[64,128]{1,0:T(8,128)(2,1)S(1)}, u32[]{:S(2)}, u32[]{:S(2)}) %collective-permute-start.6) | collective-permute-done | bytes 16416 | tf_op jit(solution)/shard_map/ppermute | solution.py:28
  17.5 1.1 %collective-permute-start.9 = (bf16[128,128]{1,0:T(8,128)(2,1)S(1)}, bf16[128,128]{1,0:T(8,128)(2,1)S(1)}, u32[]{:S(2)}, u32[]{:S(2)}) collective-permute-start(bf16[128,128]{1,0:T(8,128)(2,1)S(1)} %pad_maximum_fusion.2.low_value_ref), channel_id=1, source_target_pairs={{0,5},{1,4},{2,7},{3,6},{4,1},{5,0},{6,3},{7,2},{8,13},{9,12},{10,... | collective-permute-start | bytes 98312 | tf_op jit(solution)/shard_map/ppermute | solution.py:28
  18.6 0.0 collective-permute-done.7.kv_ref
  18.6 0.2 collective-permute-start.8
  18.8 0.0 collective-permute-done.4.other_kv_ref
  18.8 0.9 %shard_map.96 = (bf16[128,768]{1,0:T(8,128)(2,1)S(1)}, f32[128,768]{1,0:T(8,128)S(1)}, f32[768,256]{1,0:T(8,128)S(1)}) custom-call(bf16[128,768]{1,0:T(8,128)(2,1)S(1)} %get-tuple-element.18.frozen_query_ref, bf16[64,128]{1,0:T(8,128)(2,1)S(1)} %add_convert_fusion.low_ref, bf16[32,768]{1,0:T(8,128)(2,1)S(1)} %get-tuple-element.20.query_up_ref, ...), custom_call_target="tpu_custom_call" | custom-call | flops 9059696640 | bytes 23592960 | tf_op jit(solution)/shard_map/pallas_call | solution.py:311
  19.7 0.4 %shard_map.97 = (bf16[768,256]{1,0:T(8,128)(2,1)S(1)}, f32[128,768]{1,0:T(8,128)S(1)}, f32[128,768]{1,0:T(8,128)S(1)}) custom-call(bf16[128,768]{1,0:T(8,128)(2,1)S(1)} %get-tuple-element.25.queries_ref, f32[128,1024]{1,0:T(8,128)S(1)} %get-tuple-element.21.bias_ref, bf16[256,256]{1,0:T(8,128)(2,1)S(1)} %collective-permute-done.7.kv_ref, ...), custom_call_target="tpu_custom_call" | custom-call | flops 4529848320 | bytes 11796480 | tf_op jit(solution)/shard_map/pallas_call | solution.py:311
  20.2 0.0 collective-permute-done.8.kv_ref.other_kv_ref
  20.2 0.4 %shard_map.98 = (bf16[768,256]{1,0:T(8,128)(2,1)S(1)}, f32[128,768]{1,0:T(8,128)S(1)}, f32[128,768]{1,0:T(8,128)S(1)}) custom-call(bf16[128,768]{1,0:T(8,128)(2,1)S(1)} %get-tuple-element.25.queries_ref, f32[128,1024]{1,0:T(8,128)S(1)} %get-tuple-element.21.bias_ref, bf16[256,256]{1,0:T(8,128)(2,1)S(1)} %collective-permute-done.8.kv_ref.other_kv_ref, ...), custom_call_target="tpu_custom_call" | custom-call | flops 4529848320 | bytes 11796480 | tf_op jit(solution)/shard_map/pallas_call | solution.py:311
  20.6 0.3 %collective-permute-done.9.low_value_ref = bf16[128,128]{1,0:T(8,128)(2,1)S(1)} collective-permute-done((bf16[128,128]{1,0:T(8,128)(2,1)S(1)}, bf16[128,128]{1,0:T(8,128)(2,1)S(1)}, u32[]{:S(2)}, u32[]{:S(2)}) %collective-permute-start.9) | collective-permute-done | bytes 32800 | tf_op jit(solution)/shard_map/ppermute | solution.py:28
  20.9 1.4 %shard_map.99 = (bf16[128,768]{1,0:T(8,128)(2,1)}, f32[6,128]{1,0:T(8,128)}) custom-call(bf16[768,256]{1,0:T(8,128)(2,1)S(1)} %get-tuple-element.27.weights_ref, bf16[768,256]{1,0:T(8,128)(2,1)S(1)} %get-tuple-element.29.other_weights_ref, f32[128,768]{1,0:T(8,128)S(1)} %get-tuple-element.30.top_ref, f32[128,768]{1,0:T(8,128)S(1)} %get-tuple-element.31.scale_ref, ...), custom_call_target="tpu_custom_call" | custom-call | flops 301989888 | bytes 786432 | tf_op jit(solution)/shard_map/pallas_call | solution.py:311
  (7 shorter events, 0.0 us)
Async XLA Ops:
  2.1 4.2 %collective-permute-start = (bf16[64,128]{1,0:T(8,128)(2,1)S(1)}, bf16[64,128]{1,0:T(8,128)(2,1)S(1)}, u32[]{:S(2)}, u32[]{:S(2)}) collective-permute-start(bf16[64,128]{1,0:T(8,128)(2,1)S(1)} %get-tuple-element.19), channel_id=1, source_target_pairs={{0,1},{1,0},{2,3},{3,2},{4,5},{5,4},{6,7},{7,6},{8,9},{9,8},{10,11... | collective-permute-start | bytes 49160 | tf_op jit(solution)/shard_map/ppermute | solution.py:28
  2.7 5.4 %collective-permute-start.2 = (bf16[64,256]{1,0:T(8,128)(2,1)S(1)}, bf16[64,256]{1,0:T(8,128)(2,1)S(1)}, u32[]{:S(2)}, u32[]{:S(2)}) collective-permute-start(bf16[64,256]{1,0:T(8,128)(2,1)S(1)} %get-tuple-element.22), channel_id=1, source_target_pairs={{0,17},{1,16},{2,19},{3,18},{4,21},{5,20},{6,23},{7,22},{8,25},{9,... | collective-permute-start | bytes 98312 | tf_op jit(solution)/shard_map/ppermute | solution.py:28
  6.4 3.2 %collective-permute-start.1 = (bf16[64,128]{1,0:T(8,128)(2,1)S(1)}, bf16[64,128]{1,0:T(8,128)(2,1)S(1)}, u32[]{:S(2)}, u32[]{:S(2)}) collective-permute-start(bf16[64,128]{1,0:T(8,128)(2,1)S(1)} %add_convert_fusion.1), channel_id=1, source_target_pairs={{0,3},{1,2},{2,1},{3,0},{4,7},{5,6},{6,5},{7,4},{8,11},{9,10},{10,... | collective-permute-start | bytes 49160 | tf_op jit(solution)/shard_map/ppermute | solution.py:28
  8.1 4.6 %collective-permute-start.3 = (bf16[128,256]{1,0:T(8,128)(2,1)S(1)}, bf16[128,256]{1,0:T(8,128)(2,1)S(1)}, u32[]{:S(2)}, u32[]{:S(2)}) collective-permute-start(bf16[128,256]{1,0:T(8,128)(2,1)S(1)} %pad_maximum_fusion.1), channel_id=1, source_target_pairs={{0,9},{1,8},{2,11},{3,10},{4,13},{5,12},{6,15},{7,14},{8,1},{9,0},... | collective-permute-start | bytes 196616 | tf_op jit(solution)/shard_map/ppermute | solution.py:28
  9.6 4.7 %collective-permute-start.5 = (bf16[32,128]{1,0:T(8,128)(2,1)S(1)}, bf16[32,128]{1,0:T(8,128)(2,1)S(1)}, u32[]{:S(2)}, u32[]{:S(2)}) collective-permute-start(bf16[32,128]{1,0:T(8,128)(2,1)S(1)} %slice.4), channel_id=1, source_target_pairs={{0,17},{1,16},{2,19},{3,18},{4,21},{5,20},{6,23},{7,22},{8,25},{9,... | collective-permute-start | bytes 24584 | tf_op jit(solution)/shard_map/ppermute | solution.py:28
  12.7 6.0 %collective-permute-start.7 = (bf16[256,256]{1,0:T(8,128)(2,1)S(1)}, bf16[256,256]{1,0:T(8,128)(2,1)S(1)}, u32[]{:S(2)}, u32[]{:S(2)}) collective-permute-start(bf16[256,256]{1,0:T(8,128)(2,1)S(1)} %pad_maximum_fusion.kv_ref), channel_id=1, source_target_pairs={{0,5},{1,4},{2,7},{3,6},{4,1},{5,0},{6,3},{7,2},{8,13},{9,12},{10,... | collective-permute-start | bytes 393224 | tf_op jit(solution)/shard_map/ppermute | solution.py:28
  13.9 4.9 %collective-permute-start.4 = (bf16[256,256]{1,0:T(8,128)(2,1)S(1)}, bf16[256,256]{1,0:T(8,128)(2,1)S(1)}, u32[]{:S(2)}, u32[]{:S(2)}) collective-permute-start(bf16[256,256]{1,0:T(8,128)(2,1)S(1)} %pad_maximum_fusion.kv_ref), channel_id=1, source_target_pairs={{0,1},{1,0},{2,3},{3,2},{4,5},{5,4},{6,7},{7,6},{8,9},{9,8},{10,11... | collective-permute-start | bytes 393224 | tf_op jit(solution)/shard_map/ppermute | solution.py:28
  14.4 3.2 %collective-permute-start.6 = (bf16[64,128]{1,0:T(8,128)(2,1)S(1)}, bf16[64,128]{1,0:T(8,128)(2,1)S(1)}, u32[]{:S(2)}, u32[]{:S(2)}) collective-permute-start(bf16[64,128]{1,0:T(8,128)(2,1)S(1)} %pad_maximum_fusion.3), channel_id=1, source_target_pairs={{0,9},{1,8},{2,11},{3,10},{4,13},{5,12},{6,15},{7,14},{8,1},{9,0},... | collective-permute-start | bytes 49160 | tf_op jit(solution)/shard_map/ppermute | solution.py:28
  17.5 3.4 %collective-permute-start.9 = (bf16[128,128]{1,0:T(8,128)(2,1)S(1)}, bf16[128,128]{1,0:T(8,128)(2,1)S(1)}, u32[]{:S(2)}, u32[]{:S(2)}) collective-permute-start(bf16[128,128]{1,0:T(8,128)(2,1)S(1)} %pad_maximum_fusion.2.low_value_ref), channel_id=1, source_target_pairs={{0,5},{1,4},{2,7},{3,6},{4,1},{5,0},{6,3},{7,2},{8,13},{9,12},{10,... | collective-permute-start | bytes 98312 | tf_op jit(solution)/shard_map/ppermute | solution.py:28
  18.6 1.5 %collective-permute-start.8 = (bf16[256,256]{1,0:T(8,128)(2,1)S(1)}, bf16[256,256]{1,0:T(8,128)(2,1)S(1)}, u32[]{:S(2)}, u32[]{:S(2)}) collective-permute-start(bf16[256,256]{1,0:T(8,128)(2,1)S(1)} %collective-permute-done.7.kv_ref), channel_id=1, source_target_pairs={{0,1},{1,0},{2,3},{3,2},{4,5},{5,4},{6,7},{7,6},{8,9},{9,8},{10,11... | collective-permute-start | bytes 393224 | tf_op jit(solution)/shard_map/ppermute | solution.py:28

commit v11 on v9

--- a/solution.py
+++ b/solution.py
@@ -428,7 +428,8 @@
     low_value = low[ADAPTER_RANK:]
     short = hidden.shape[0] * ctx_count <= 1024
     for bit in bits[:-1]:
-        low_value = jnp.concatenate([low_value, exchange(low_value, bit, 1)], axis=0)
+        cores = 0 if bit == bits[0] else 1
+        low_value = jnp.concatenate([low_value, exchange(low_value, bit, cores)], axis=0)
         kv = jnp.concatenate([kv, exchange(kv, bit, 1)], axis=0)
     if short:
         kv, _ = lax.optimization_barrier((kv, low))

time: 22.3 us -> 22.3 us (level)
  waiting for transfers between devices: 3.29 us -> 2.93 us
  starting transfers between devices: 13.9 us -> 14.2 us
    ppermute x10, waiting for transfers between devices: 3.29 us -> 2.93 us  [exchange(): return lax.ppermute(value, AXES, pairs)]
    ppermute x10, starting transfers between devices: 13.9 us -> 14.2 us  [exchange(): return lax.ppermute(value, AXES, pairs)]
where the time goes in v11:
time: 22.3 us; the launch traced here: 22.1 us
  starting transfers between devices  14.2 us (64%)
  Pallas kernels  4.26 us (19%)
  waiting for transfers between devices  2.93 us (13%)
  between operations  0.69 us (3%)
    ppermute x10, starting transfers between devices, exchange(): return lax.ppermute(value, AXES, pairs)  14.2 us
    ppermute x10, waiting for transfers between devices, exchange(): return lax.ppermute(value, AXES, pairs)  2.93 us
    pallas_call x3, Pallas kernels, call(): pl.pallas_call(functools.partial(kernel, patterns), out_shape=out_shape,...  2.76 us
    pallas_call x1, Pallas kernels, prologue(): pl.pallas_call(functools.partial(prologue_kernel, patterns), out_shape=(j...  1.5 us
  transfers between devices with their start and end apart: 10, of which 4 were waited for; matrix products, arithmetic and copies ran while one was open for 0% of the time, Pallas kernels for 7%

profile of v11, /device:TPU:0, one launch (start us, length us, event | category | flops | bytes accessed | tf_op | source)
XLA Modules:
  0.0 22.1 jit_solution(6844623433275103043)
XLA Ops:
  0.6 1.5 %shard_map.95 = (bf16[64,128]{1,0:T(8,128)(2,1)S(1)}, bf16[64,256]{1,0:T(8,128)(2,1)S(1)}, f32[128,1024]{1,0:T(8,128)S(1)}, bf16[128,768]{1,0:T(8,128)(2,1)S(1)}...) custom-call(bf16[128,2048]{1,0:T(8,128)(2,1)} %hidden_hbm.1, bf16[64,2048]{1,0:T(8,128)(2,1)} %bitcast.1, ...), custom_call_target="tpu_custom_call" | custom-call | flops 33554432 | bytes 1048576 | tf_op jit(solution)/shard_map/pallas_call | solution.py:130
  2.1 0.5 %collective-permute-start = (bf16[64,128]{1,0:T(8,128)(2,1)S(1)}, bf16[64,128]{1,0:T(8,128)(2,1)S(1)}, u32[]{:S(2)}, u32[]{:S(2)}) collective-permute-start(bf16[64,128]{1,0:T(8,128)(2,1)S(1)} %get-tuple-element.16), channel_id=1, source_target_pairs={{0,1},{1,0},{2,3},{3,2},{4,5},{5,4},{6,7},{7,6},{8,9},{9,8},{10,11... | collective-permute-start | bytes 49160 | tf_op jit(solution)/shard_map/ppermute | solution.py:28
  2.7 3.7 %collective-permute-start.2 = (bf16[64,256]{1,0:T(8,128)(2,1)S(1)}, bf16[64,256]{1,0:T(8,128)(2,1)S(1)}, u32[]{:S(2)}, u32[]{:S(2)}) collective-permute-start(bf16[64,256]{1,0:T(8,128)(2,1)S(1)} %get-tuple-element.19), channel_id=1, source_target_pairs={{0,17},{1,16},{2,19},{3,18},{4,21},{5,20},{6,23},{7,22},{8,25},{9,... | collective-permute-start | bytes 98312 | tf_op jit(solution)/shard_map/ppermute | solution.py:28
  6.4 0.0 collective-permute-done
  6.4 1.3 %collective-permute-start.1 = (bf16[64,128]{1,0:T(8,128)(2,1)S(1)}, bf16[64,128]{1,0:T(8,128)(2,1)S(1)}, u32[]{:S(2)}, u32[]{:S(2)}) collective-permute-start(bf16[64,128]{1,0:T(8,128)(2,1)S(1)} %add_convert_fusion.1), channel_id=1, source_target_pairs={{0,3},{1,2},{2,1},{3,0},{4,7},{5,6},{6,5},{7,4},{8,11},{9,10},{10,... | collective-permute-start | bytes 49160 | tf_op jit(solution)/shard_map/ppermute | solution.py:28
  7.6 0.4 %collective-permute-done.2 = bf16[64,256]{1,0:T(8,128)(2,1)S(1)} collective-permute-done((bf16[64,256]{1,0:T(8,128)(2,1)S(1)}, bf16[64,256]{1,0:T(8,128)(2,1)S(1)}, u32[]{:S(2)}, u32[]{:S(2)}) %collective-permute-start.2) | collective-permute-done | bytes 32800 | tf_op jit(solution)/shard_map/ppermute | solution.py:28
  8.1 1.6 %collective-permute-start.3 = (bf16[128,256]{1,0:T(8,128)(2,1)S(1)}, bf16[128,256]{1,0:T(8,128)(2,1)S(1)}, u32[]{:S(2)}, u32[]{:S(2)}) collective-permute-start(bf16[128,256]{1,0:T(8,128)(2,1)S(1)} %pad_maximum_fusion.1), channel_id=1, source_target_pairs={{0,9},{1,8},{2,11},{3,10},{4,13},{5,12},{6,15},{7,14},{8,1},{9,0},... | collective-permute-start | bytes 196616 | tf_op jit(solution)/shard_map/ppermute | solution.py:28
  9.6 0.0 collective-permute-done.1
  9.6 3.0 %collective-permute-start.5 = (bf16[32,128]{1,0:T(8,128)(2,1)S(1)}, bf16[32,128]{1,0:T(8,128)(2,1)S(1)}, u32[]{:S(2)}, u32[]{:S(2)}) collective-permute-start(bf16[32,128]{1,0:T(8,128)(2,1)S(1)} %slice.4), channel_id=1, source_target_pairs={{0,16},{1,17},{2,18},{3,19},{4,20},{5,21},{6,22},{7,23},{8,24},{9,... | collective-permute-start | bytes 24584 | tf_op jit(solution)/shard_map/ppermute | solution.py:28
  12.6 0.0 collective-permute-done.3
  12.6 1.3 %collective-permute-start.7 = (bf16[256,256]{1,0:T(8,128)(2,1)S(1)}, bf16[256,256]{1,0:T(8,128)(2,1)S(1)}, u32[]{:S(2)}, u32[]{:S(2)}) collective-permute-start(bf16[256,256]{1,0:T(8,128)(2,1)S(1)} %pad_maximum_fusion.kv_ref), channel_id=1, source_target_pairs={{0,5},{1,4},{2,7},{3,6},{4,1},{5,0},{6,3},{7,2},{8,13},{9,12},{10,... | collective-permute-start | bytes 393224 | tf_op jit(solution)/shard_map/ppermute | solution.py:28
  14.0 0.4 %collective-permute-start.4 = (bf16[256,256]{1,0:T(8,128)(2,1)S(1)}, bf16[256,256]{1,0:T(8,128)(2,1)S(1)}, u32[]{:S(2)}, u32[]{:S(2)}) collective-permute-start(bf16[256,256]{1,0:T(8,128)(2,1)S(1)} %pad_maximum_fusion.kv_ref), channel_id=1, source_target_pairs={{0,1},{1,0},{2,3},{3,2},{4,5},{5,4},{6,7},{7,6},{8,9},{9,8},{10,11... | collective-permute-start | bytes 393224 | tf_op jit(solution)/shard_map/ppermute | solution.py:28
  14.3 0.0 collective-permute-done.5
  14.3 0.9 %collective-permute-start.6 = (bf16[64,128]{1,0:T(8,128)(2,1)S(1)}, bf16[64,128]{1,0:T(8,128)(2,1)S(1)}, u32[]{:S(2)}, u32[]{:S(2)}) collective-permute-start(bf16[64,128]{1,0:T(8,128)(2,1)S(1)} %pad_maximum_fusion.3), channel_id=1, source_target_pairs={{0,9},{1,8},{2,11},{3,10},{4,13},{5,12},{6,15},{7,14},{8,1},{9,0},... | collective-permute-start | bytes 49160 | tf_op jit(solution)/shard_map/ppermute | solution.py:28
  15.2 2.2 %collective-permute-done.6 = bf16[64,128]{1,0:T(8,128)(2,1)S(1)} collective-permute-done((bf16[64,128]{1,0:T(8,128)(2,1)S(1)}, bf16[64,128]{1,0:T(8,128)(2,1)S(1)}, u32[]{:S(2)}, u32[]{:S(2)}) %collective-permute-start.6) | collective-permute-done | bytes 16416 | tf_op jit(solution)/shard_map/ppermute | solution.py:28
  17.5 1.3 %collective-permute-start.9 = (bf16[128,128]{1,0:T(8,128)(2,1)S(1)}, bf16[128,128]{1,0:T(8,128)(2,1)S(1)}, u32[]{:S(2)}, u32[]{:S(2)}) collective-permute-start(bf16[128,128]{1,0:T(8,128)(2,1)S(1)} %pad_maximum_fusion.2.low_value_ref), channel_id=1, source_target_pairs={{0,5},{1,4},{2,7},{3,6},{4,1},{5,0},{6,3},{7,2},{8,13},{9,12},{10,... | collective-permute-start | bytes 98312 | tf_op jit(solution)/shard_map/ppermute | solution.py:28
  18.8 0.0 collective-permute-done.7.kv_ref
  18.8 0.3 %collective-permute-start.8 = (bf16[256,256]{1,0:T(8,128)(2,1)S(1)}, bf16[256,256]{1,0:T(8,128)(2,1)S(1)}, u32[]{:S(2)}, u32[]{:S(2)}) collective-permute-start(bf16[256,256]{1,0:T(8,128)(2,1)S(1)} %collective-permute-done.7.kv_ref), channel_id=1, source_target_pairs={{0,1},{1,0},{2,3},{3,2},{4,5},{5,4},{6,7},{7,6},{8,9},{9,8},{10,11... | collective-permute-start | bytes 393224 | tf_op jit(solution)/shard_map/ppermute | solution.py:28
  19.1 0.0 collective-permute-done.4.other_kv_ref
  19.1 0.9 %shard_map.96 = (bf16[128,768]{1,0:T(8,128)(2,1)S(1)}, f32[128,768]{1,0:T(8,128)S(1)}, f32[768,256]{1,0:T(8,128)S(1)}) custom-call(bf16[128,768]{1,0:T(8,128)(2,1)S(1)} %get-tuple-element.15.frozen_query_ref, bf16[64,128]{1,0:T(8,128)(2,1)S(1)} %add_convert_fusion.low_ref, bf16[32,768]{1,0:T(8,128)(2,1)S(1)} %get-tuple-element.17.query_up_ref, ...), custom_call_target="tpu_custom_call" | custom-call | flops 9059696640 | bytes 23592960 | tf_op jit(solution)/shard_map/pallas_call | solution.py:315
  20.0 0.2 collective-permute-done.8.other_kv_ref
  20.2 0.6 %shard_map.97 = (bf16[768,512]{1,0:T(8,128)(2,1)S(1)}, f32[128,768]{1,0:T(8,128)S(1)}, f32[128,768]{1,0:T(8,128)S(1)}) custom-call(bf16[128,768]{1,0:T(8,128)(2,1)S(1)} %get-tuple-element.22.queries_ref, f32[128,1024]{1,0:T(8,128)S(1)} %get-tuple-element.18.bias_ref, bf16[256,256]{1,0:T(8,128)(2,1)S(1)} %collective-permute-done.7.kv_ref, ...), custom_call_target="tpu_custom_call" | custom-call | flops 9059696640 | bytes 23592960 | tf_op jit(solution)/shard_map/pallas_call | solution.py:315
  20.8 0.1 collective-permute-done.9.low_value_ref
  20.8 1.3 %shard_map.98 = (bf16[128,768]{1,0:T(8,128)(2,1)}, f32[6,128]{1,0:T(8,128)}) custom-call(bf16[768,512]{1,0:T(8,128)(2,1)S(1)} %get-tuple-element.24.weights_ref, f32[128,768]{1,0:T(8,128)S(1)} %get-tuple-element.25.top_ref, f32[128,768]{1,0:T(8,128)S(1)} %get-tuple-element.26.scale_ref, f32[768,256]{1,0:T(8,128)S(1)} %get-tuple-element.27.first_sums_ref, ...), custom_call_target="tpu_custom_call" | custom-call | flops 301989888 | bytes 786432 | tf_op jit(solution)/shard_map/pallas_call | solution.py:315
  (7 shorter events, 0.0 us)
Async XLA Ops:
  2.1 4.2 %collective-permute-start = (bf16[64,128]{1,0:T(8,128)(2,1)S(1)}, bf16[64,128]{1,0:T(8,128)(2,1)S(1)}, u32[]{:S(2)}, u32[]{:S(2)}) collective-permute-start(bf16[64,128]{1,0:T(8,128)(2,1)S(1)} %get-tuple-element.16), channel_id=1, source_target_pairs={{0,1},{1,0},{2,3},{3,2},{4,5},{5,4},{6,7},{7,6},{8,9},{9,8},{10,11... | collective-permute-start | bytes 49160 | tf_op jit(solution)/shard_map/ppermute | solution.py:28
  2.7 5.4 %collective-permute-start.2 = (bf16[64,256]{1,0:T(8,128)(2,1)S(1)}, bf16[64,256]{1,0:T(8,128)(2,1)S(1)}, u32[]{:S(2)}, u32[]{:S(2)}) collective-permute-start(bf16[64,256]{1,0:T(8,128)(2,1)S(1)} %get-tuple-element.19), channel_id=1, source_target_pairs={{0,17},{1,16},{2,19},{3,18},{4,21},{5,20},{6,23},{7,22},{8,25},{9,... | collective-permute-start | bytes 98312 | tf_op jit(solution)/shard_map/ppermute | solution.py:28
  6.4 3.2 %collective-permute-start.1 = (bf16[64,128]{1,0:T(8,128)(2,1)S(1)}, bf16[64,128]{1,0:T(8,128)(2,1)S(1)}, u32[]{:S(2)}, u32[]{:S(2)}) collective-permute-start(bf16[64,128]{1,0:T(8,128)(2,1)S(1)} %add_convert_fusion.1), channel_id=1, source_target_pairs={{0,3},{1,2},{2,1},{3,0},{4,7},{5,6},{6,5},{7,4},{8,11},{9,10},{10,... | collective-permute-start | bytes 49160 | tf_op jit(solution)/shard_map/ppermute | solution.py:28
  8.1 4.6 %collective-permute-start.3 = (bf16[128,256]{1,0:T(8,128)(2,1)S(1)}, bf16[128,256]{1,0:T(8,128)(2,1)S(1)}, u32[]{:S(2)}, u32[]{:S(2)}) collective-permute-start(bf16[128,256]{1,0:T(8,128)(2,1)S(1)} %pad_maximum_fusion.1), channel_id=1, source_target_pairs={{0,9},{1,8},{2,11},{3,10},{4,13},{5,12},{6,15},{7,14},{8,1},{9,0},... | collective-permute-start | bytes 196616 | tf_op jit(solution)/shard_map/ppermute | solution.py:28
  9.6 4.7 %collective-permute-start.5 = (bf16[32,128]{1,0:T(8,128)(2,1)S(1)}, bf16[32,128]{1,0:T(8,128)(2,1)S(1)}, u32[]{:S(2)}, u32[]{:S(2)}) collective-permute-start(bf16[32,128]{1,0:T(8,128)(2,1)S(1)} %slice.4), channel_id=1, source_target_pairs={{0,16},{1,17},{2,18},{3,19},{4,20},{5,21},{6,22},{7,23},{8,24},{9,... | collective-permute-start | bytes 24584 | tf_op jit(solution)/shard_map/ppermute | solution.py:28
  12.6 6.2 %collective-permute-start.7 = (bf16[256,256]{1,0:T(8,128)(2,1)S(1)}, bf16[256,256]{1,0:T(8,128)(2,1)S(1)}, u32[]{:S(2)}, u32[]{:S(2)}) collective-permute-start(bf16[256,256]{1,0:T(8,128)(2,1)S(1)} %pad_maximum_fusion.kv_ref), channel_id=1, source_target_pairs={{0,5},{1,4},{2,7},{3,6},{4,1},{5,0},{6,3},{7,2},{8,13},{9,12},{10,... | collective-permute-start | bytes 393224 | tf_op jit(solution)/shard_map/ppermute | solution.py:28
  14.0 5.1 %collective-permute-start.4 = (bf16[256,256]{1,0:T(8,128)(2,1)S(1)}, bf16[256,256]{1,0:T(8,128)(2,1)S(1)}, u32[]{:S(2)}, u32[]{:S(2)}) collective-permute-start(bf16[256,256]{1,0:T(8,128)(2,1)S(1)} %pad_maximum_fusion.kv_ref), channel_id=1, source_target_pairs={{0,1},{1,0},{2,3},{3,2},{4,5},{5,4},{6,7},{7,6},{8,9},{9,8},{10,11... | collective-permute-start | bytes 393224 | tf_op jit(solution)/shard_map/ppermute | solution.py:28
  14.3 3.2 %collective-permute-start.6 = (bf16[64,128]{1,0:T(8,128)(2,1)S(1)}, bf16[64,128]{1,0:T(8,128)(2,1)S(1)}, u32[]{:S(2)}, u32[]{:S(2)}) collective-permute-start(bf16[64,128]{1,0:T(8,128)(2,1)S(1)} %pad_maximum_fusion.3), channel_id=1, source_target_pairs={{0,9},{1,8},{2,11},{3,10},{4,13},{5,12},{6,15},{7,14},{8,1},{9,0},... | collective-permute-start | bytes 49160 | tf_op jit(solution)/shard_map/ppermute | solution.py:28
  17.5 3.3 %collective-permute-start.9 = (bf16[128,128]{1,0:T(8,128)(2,1)S(1)}, bf16[128,128]{1,0:T(8,128)(2,1)S(1)}, u32[]{:S(2)}, u32[]{:S(2)}) collective-permute-start(bf16[128,128]{1,0:T(8,128)(2,1)S(1)} %pad_maximum_fusion.2.low_value_ref), channel_id=1, source_target_pairs={{0,5},{1,4},{2,7},{3,6},{4,1},{5,0},{6,3},{7,2},{8,13},{9,12},{10,... | collective-permute-start | bytes 98312 | tf_op jit(solution)/shard_map/ppermute | solution.py:28
  18.8 1.3 %collective-permute-start.8 = (bf16[256,256]{1,0:T(8,128)(2,1)S(1)}, bf16[256,256]{1,0:T(8,128)(2,1)S(1)}, u32[]{:S(2)}, u32[]{:S(2)}) collective-permute-start(bf16[256,256]{1,0:T(8,128)(2,1)S(1)} %collective-permute-done.7.kv_ref), channel_id=1, source_target_pairs={{0,1},{1,0},{2,3},{3,2},{4,5},{5,4},{6,7},{7,6},{8,9},{9,8},{10,11... | collective-permute-start | bytes 393224 | tf_op jit(solution)/shard_map/ppermute | solution.py:28
